TPU v7x, 32 devices: a whole 2x2x4 slice. The times are simulated.
32 devices in a mesh: gy: 8 (over y, x, core), gz: 4 (over z).
Axes of the slice: x: 2, y: 2, z: 4, core: 2. Of those that a mesh axis runs over, the one named last changes fastest.
Arguments:
- volume: float32 [160, 8, 4096], P('gz', 'gy'), may hold values from -6 to 6
- x_offsets: int32 [160], replicated, may hold values from -64 to 64, as said below
- x_fracs: float32 [160], replicated, may hold values from 0 to 1
- z_offsets: int32 [8], P('gy'), may hold values from -4 to 4, as said below
- z_fracs: float32 [8], P('gy'), may hold values from 0 to 1
- y_offsets: int32 [4096], P('gy'), may hold values from -2 to 2, as said below
- y_fracs: float32 [4096], P('gy'), may hold values from 0 to 1
- slopes: int32 [8], replicated, may hold values from -4 to 4, as said below
Outputs:
- rotated: float32 [160, 8, 4096], P('gz', 'gy')
- projections: float32 [8, 4096, 8], P('gz', 'gy')
Inputs may be any that keep to these rules, and one draw needn't show every extreme that they name: `x_offsets`: each value between -64 and 64, both ends taken by some plane. `z_offsets`: each value between -4 and 4, both ends taken by some row. `y_offsets`: each value between -2 and 2, both ends taken by some column. `slopes`: each value between -4 and 4, both ends taken by some tilt.
All inputs are finite; a program needn't handle non-finite values.
Results may differ from a plain program's by a relative error of at most 0.0003.
Values sent between devices are 32-bit elements; how exact they have to be, the bound alone decides.
No kernel may reach another device: no remote copies, remote signals or barrier semaphores. Data moves between devices by JAX's collectives and lax.ppermute only.
A program may use at most 64 MiB of HBM per device.

v0:
```python
import jax
import jax.numpy as jnp
from jax import lax
from jax.sharding import PartitionSpec as P

TAPS = 64
OFFX = 64
OFFZ = 4


def with_halo(value, sides, width):
    for axis, dim in sides:
        peers, length = (lax.axis_size(axis), value.shape[dim])
        up = [(i, (i + 1) % peers) for i in range(peers - 1)]
        down = [(j, i) for i, j in up]
        last = lax.slice_in_dim(value, length - width, length, axis=dim)
        first = lax.slice_in_dim(value, 0, width, axis=dim)
        before = lax.ppermute(last, axis, up)
        after = lax.ppermute(first, axis, down)
        value = jnp.concatenate([before, value, after], axis=dim)
    return value


def tap_weight(offset, fraction):
    moved = offset.astype(jnp.float32) - fraction
    inside = (offset >= 1 - TAPS // 2) & (offset <= TAPS // 2)
    value = jnp.sinc(moved) * (0.5 + 0.5 * jnp.cos(jnp.pi * moved / (TAPS // 2 + 1)))
    return jnp.where(inside, value, jnp.zeros_like(value))


def shear_lines(planes, shifts, fractions):
    plane_total, row_total, line_length = planes.shape
    tile_width = 128
    margin = OFFX + tile_width
    padded = jnp.pad(planes, ((0, 0), (0, 0), (margin, margin)))
    starts = margin + shifts - (TAPS // 2 - 1)
    spans = jax.vmap(
        lambda one_plane, first_index: lax.dynamic_slice_in_dim(
            one_plane, first_index, line_length + tile_width, 1
        )
    )(padded, starts)
    tile_count = line_length // tile_width
    pieces = spans.reshape(plane_total, row_total, tile_count + 1, tile_width)
    windows = jnp.concatenate([pieces[:, :, :-1], pieces[:, :, 1:]], axis=3)
    inner_index = jnp.arange(2 * tile_width, dtype=jnp.int32)[:, None]
    outer_index = jnp.arange(tile_width, dtype=jnp.int32)[None, :]
    band_matrix = tap_weight(
        (inner_index - outer_index - (TAPS // 2 - 1))[None], fractions[:, None, None]
    )
    sheared = jnp.einsum("prbj,pji->prbi", windows, band_matrix, precision=lax.Precision.HIGHEST)
    return sheared.reshape(plane_total, row_total, line_length)


def local(volume, x_offsets, x_fracs, z_offsets, z_fracs, y_offsets, y_fracs, slopes):
    depth = TAPS // 2 + OFFZ
    plane_count, row_local, width_all = volume.shape
    groups = lax.axis_size("gy")
    col_local = width_all // groups
    first_plane = lax.axis_index("gz") * plane_count
    plane_shifts = lax.dynamic_slice_in_dim(x_offsets, first_plane, plane_count)
    plane_fracs = lax.dynamic_slice_in_dim(x_fracs, first_plane, plane_count)
    sheared_x = shear_lines(volume, plane_shifts, plane_fracs)
    extended = with_halo(sheared_x, (("gz", 0),), depth)
    plane_index = jnp.arange(plane_count, dtype=jnp.int32)[:, None]
    source_index = jnp.arange(plane_count + 2 * depth, dtype=jnp.int32)[None, :]
    mixing = tap_weight(
        (source_index - depth - plane_index)[None] - z_offsets[:, None, None],
        z_fracs[:, None, None],
    )
    blocked = extended.reshape(plane_count + 2 * depth, row_local, groups, col_local)
    outgoing = jnp.einsum("rzj,jrgc->grcz", mixing, blocked, precision=lax.Precision.HIGHEST)
    outgoing = outgoing.reshape(groups, 1, row_local * col_local * plane_count)
    arrived = lax.all_to_all(outgoing, "gy", split_axis=0, concat_axis=1, tiled=True)
    row_total = groups * row_local
    columns = arrived.reshape(row_total, col_local, plane_count)
    target_row = jnp.arange(row_total, dtype=jnp.int32)[:, None]
    source_row = jnp.arange(row_total, dtype=jnp.int32)[None, :]
    operator = tap_weight(
        (source_row - target_row)[None] - y_offsets[:, None, None], y_fracs[:, None, None]
    )
    rotated_cols = jnp.einsum("cij,jcz->zci", operator, columns, precision=lax.Precision.HIGHEST)
    span_pad = row_total // 4
    total_planes = plane_count * lax.axis_size("gz")
    global_planes = first_plane + jnp.arange(plane_count, dtype=jnp.int32)
    padded_cols = jnp.pad(rotated_cols, ((0, 0), (0, 0), (span_pad, span_pad)))
    per_tilt = []
    for tilt_index in range(slopes.shape[0]):
        lifts = (
            slopes[tilt_index]
            * (2 * global_planes - total_planes)
            * row_total
            // (16 * total_planes)
        )
        moved = jax.vmap(
            lambda one_plane, lift_one: lax.dynamic_slice_in_dim(
                one_plane, span_pad + lift_one, row_total, 1
            )
        )(padded_cols, lifts)
        per_tilt.append(jnp.sum(moved, axis=0))
    partial_terms = jnp.stack(per_tilt) * total_planes ** (-0.5)
    projections = lax.psum_scatter(partial_terms, "gz", scatter_dimension=0, tiled=True)
    returning = rotated_cols.reshape(plane_count, col_local, groups, row_local)
    returning = jnp.transpose(returning, (2, 3, 1, 0)).reshape(
        groups, 1, row_local * col_local * plane_count
    )
    landed = lax.all_to_all(returning, "gy", split_axis=0, concat_axis=1, tiled=True)
    landed = landed.reshape(groups, row_local, col_local, plane_count)
    rotated = jnp.transpose(landed, (3, 1, 0, 2)).reshape(
        plane_count, row_local, groups * col_local
    )
    return (rotated, projections)


def solution(mesh):
    return jax.shard_map(
        local,
        mesh=mesh,
        in_specs=(P("gz", "gy", None), P(), P(), P("gy"), P("gy"), P("gy"), P("gy"), P()),
        out_specs=(P("gz", "gy", None), P("gz", "gy", None)),
        check_vma=False,
    )
```

profile of v0, /device:TPU:0, one launch (start us, length us, event | category | flops | bytes accessed | tf_op | source)
XLA Modules:
  0.0 244.9 jit_solution(8727704525355963002)
XLA Ops:
  8.0 2.5 %pad.17 = f32[40,1,4480]{2,1,0:T(1,128)S(1)} pad(f32[40,1,4096]{2,1,0:T(1,128)} %param.8, f32[]{:T(128)} %constant.165.clone.1), padding=0_0x0_0x192_192 | pad | bytes 1372164 | tf_op jit(solution)/shard_map/jit(_pad)/pad | solution.py:35
  10.6 85.5 %while.1 = (s32[]{:T(128)}, f32[40,1,4480]{2,1,0:T(1,128)S(1)}, s32[40,3]{0,1:T(4,128)S(1)}, f32[40,1,4224]{2,1,0:T(1,128)S(1)}, s32[]{:T(128)}) while((s32[]{:T(128)}, f32[40,1,4480]{2,1,0:T(1,128)S(1)}, s32[40,3]{0,1:T(4,128)S(1)}, f32[40,1,4224]{2,1,0:T(1,128)S(1)}, s32[]{:T(128)}) %tuple.39), condition=%wide.while_cond, body=%wide.while_body.sunk | while | flops 2 | bytes 33909 | solution.py:38
  11.2 1.4 dynamic-slice_dynamic-update-slice_fusion.2
  13.4 1.4 dynamic-slice_dynamic-update-slice_fusion.2
  15.5 1.4 dynamic-slice_dynamic-update-slice_fusion.2
  17.7 1.4 dynamic-slice_dynamic-update-slice_fusion.2
  19.8 1.4 dynamic-slice_dynamic-update-slice_fusion.2
  21.9 1.4 dynamic-slice_dynamic-update-slice_fusion.2
  24.1 1.4 dynamic-slice_dynamic-update-slice_fusion.2
  26.2 1.4 dynamic-slice_dynamic-update-slice_fusion.2
  28.4 1.4 dynamic-slice_dynamic-update-slice_fusion.2
  30.5 1.4 dynamic-slice_dynamic-update-slice_fusion.2
  32.6 1.4 dynamic-slice_dynamic-update-slice_fusion.2
  34.8 1.4 dynamic-slice_dynamic-update-slice_fusion.2
  36.9 1.4 dynamic-slice_dynamic-update-slice_fusion.2
  39.0 1.4 dynamic-slice_dynamic-update-slice_fusion.2
  41.2 1.4 dynamic-slice_dynamic-update-slice_fusion.2
  43.3 1.4 dynamic-slice_dynamic-update-slice_fusion.2
  45.5 1.4 dynamic-slice_dynamic-update-slice_fusion.2
  47.6 1.4 dynamic-slice_dynamic-update-slice_fusion.2
  49.7 1.4 dynamic-slice_dynamic-update-slice_fusion.2
  51.9 1.4 dynamic-slice_dynamic-update-slice_fusion.2
  54.0 1.4 dynamic-slice_dynamic-update-slice_fusion.2
  56.2 1.4 dynamic-slice_dynamic-update-slice_fusion.2
  58.3 1.4 dynamic-slice_dynamic-update-slice_fusion.2
  60.4 1.4 dynamic-slice_dynamic-update-slice_fusion.2
  77.5 1.4 dynamic-slice_dynamic-update-slice_fusion.2
  79.7 1.4 dynamic-slice_dynamic-update-slice_fusion.2
  81.8 1.4 dynamic-slice_dynamic-update-slice_fusion.2
  84.0 1.4 dynamic-slice_dynamic-update-slice_fusion.2
  86.1 1.4 dynamic-slice_dynamic-update-slice_fusion.2
  88.2 1.4 dynamic-slice_dynamic-update-slice_fusion.2
  90.4 1.4 dynamic-slice_dynamic-update-slice_fusion.2
  96.1 1.6 reduce
  98.5 27.7 %fusion.28 = f32[40,32,128]{2,1,0:T(8,128)S(1)} fusion(f32[40]{0:T(128)S(1)} %dynamic_slice.7, f32[256,128]{1,0:T(8,128)S(1)} %fusion.87, pred[256,128]{1,0:T(8,128)(4,1)S(1)} %fusion.90, f32[40,1,32,128]{3,2,0,1:T(8,128)S(1)} %get-tuple-element.27, f32[40,1,32,128]{3,2,0,1:T(8,128)S(1)} %get-tuple-element.26), kind=kOutput, calls=%fused_computation.46 | convolution fusion | flops 554762240 | bytes 2130080 | tf_op jit(solution)/shard_map/prbj,pji->prbi/dot_general | solution.py:50
  127.1 5.0 %collective-permute-start = (f32[36,1,4096]{2,1,0:T(1,128)S(1)}, f32[36,1,4096]{2,1,0:T(1,128)S(1)}, u32[]{:S(2)}, u32[]{:S(2)}) collective-permute-start(f32[36,1,4096]{2,1,0:T(1,128)S(1)} %bitcast.93), channel_id=1, source_target_pairs={{0,1},{1,2},{2,3},{4,5},{5,6},{6,7},{8,9},{9,10},{10,11},{12,13},{... | collective-permute-start | bytes 1769480 | tf_op jit(solution)/shard_map/ppermute | solution.py:18
  135.2 9.4 %collective-permute-done = f32[36,1,4096]{2,1,0:T(1,128)S(1)} collective-permute-done((f32[36,1,4096]{2,1,0:T(1,128)S(1)}, f32[36,1,4096]{2,1,0:T(1,128)S(1)}, u32[]{:S(2)}, u32[]{:S(2)}) %collective-permute-start) | collective-permute-done | bytes 589856 | tf_op jit(solution)/shard_map/ppermute | solution.py:18
  146.8 2.3 collective-permute-done.1
  149.1 2.5 %reduce.2 = f32[36,4096]{1,0:T(8,128)S(1)} reduce(f32[36,1,4096]{2,1,0:T(1,128)} %collective-permute-done.1, f32[]{:T(128)} %constant.402), dimensions={1}, to_apply=%ppermute.7.reduce_sub_computation | reduce | bytes 1179652 | tf_op jit(solution)/shard_map/ppermute | solution.py:19
  152.4 3.5 %fusion.50 = f32[8,512,40]{2,1,0:T(8,128)S(1)} fusion(f32[36,1,8,512]{3,0,2,1:T(8,128)S(1)} %copy.57, f32[40,1,8,512]{3,0,2,1:T(8,128)S(1)} %copy.56, f32[36,1,8,512]{3,0,2,1:T(8,128)S(1)} %copy.55, f32[]{:T(128)} %bitcast.85, s32[]{:T(128)} %bitcast.84, s32[112]{0:T(128)S(1)} %iota_add_fusion), kind=kOutput, calls=%fused_computation.65 | convolution fusion | flops 221320064 | bytes 2490824 | tf_op jit(solution)/shard_map/rzj,jrgc->grcz/dot_general | solution.py:71
  155.9 2.9 %transpose.120 = f32[8,1,20480]{2,1,0:T(1,128)} reshape(f32[8,512,40]{2,1,0:T(8,128)S(1)} %fusion.50) | data formatting | bytes 1310720 | tf_op jit(solution)/shard_map/reshape;rzj,jrgc->grcz/transpose | solution.py:72
  158.8 4.0 %all-to-all-start = ((f32[8,1,20480]{2,1,0:T(1,128)}), f32[8,1,20480]{2,1,0:T(1,128)S(1)}, u32[]{:S(2)}, u32[]{:S(2)}) async-start(f32[8,1,20480]{2,1,0:T(1,128)} %transpose.120), calls=%async_computation | async-start | bytes 1310720 | tf_op jit(solution)/shard_map/all_to_all | solution.py:73
  163.5 2.0 copy.61
  169.8 1.8 or_bitcast_fusion
  171.6 2.2 all-to-all-done
  173.8 1.6 reduce.3
  175.3 3.0 %reshape.525 = f32[8,512,40]{2,1,0:T(8,128)} reshape(f32[8,20480]{1,0:T(8,128)S(1)} %reduce.3) | data formatting | bytes 1310720 | tf_op jit(solution)/shard_map/reshape | solution.py:75
  178.3 6.7 %fusion.48 = f32[512,40,8]{1,2,0:T(8,128)S(1)} fusion(f32[512,8,8]{2,1,0:T(8,128)} %copy.61, f32[8,512,40]{2,1,0:T(8,128)} %reshape.525), kind=kOutput, calls=%fused_computation.62 | convolution fusion | flops 15728640 | bytes 1441792 | tf_op jit(solution)/shard_map/cij,jcz->zci/dot_general | solution.py:81
  187.2 2.0 gather_fusion
  190.0 2.3 gather_fusion.1
  192.9 2.0 gather_fusion.2
  195.0 2.0 gather_fusion.3
  197.2 2.0 gather_fusion.4
  199.3 2.0 gather_fusion.5
  201.5 2.0 gather_fusion.6
  203.6 2.0 gather_fusion.7
  205.7 2.0 copy.62
  207.8 3.1 %reshape.602 = f32[8,1,20480]{2,1,0:T(1,128)} reshape(f32[8,1,512,40]{3,2,0,1:T(8,128)S(1)} %copy.62) | data formatting | bytes 1310720 | tf_op jit(solution)/shard_map/reshape | solution.py:103
  210.9 3.5 %all-to-all-start.1 = ((f32[8,1,20480]{2,1,0:T(1,128)}), f32[8,1,20480]{2,1,0:T(1,128)S(1)}, u32[]{:S(2)}, u32[]{:S(2)}) async-start(f32[8,1,20480]{2,1,0:T(1,128)} %reshape.602), calls=%async_computation.1 | async-start | bytes 1310720 | tf_op jit(solution)/shard_map/all_to_all | solution.py:106
  215.3 10.3 %all-to-all-done.1 = f32[8,1,20480]{2,1,0:T(1,128)S(1)} async-done(((f32[8,1,20480]{2,1,0:T(1,128)}), f32[8,1,20480]{2,1,0:T(1,128)S(1)}, u32[]{:S(2)}, u32[]{:S(2)}) %all-to-all-start.1) | async-done | bytes 655392 | tf_op jit(solution)/shard_map/all_to_all | solution.py:106
  225.5 1.6 reduce.4
  227.1 1.7 reshape.528
  228.8 2.5 %copy.72 = f32[40,1,4096]{2,1,0:T(1,128)} copy(f32[40,1,4096]{0,2,1:T(8,128)S(1)} %bitcast.88) | data formatting | bytes 1310720
  231.3 6.5 %reduce-scatter.2.cloned.1.call-done = f32[2,512,8]{1,2,0:T(8,128)} async-done(((f32[8,512,8]{1,2,0:T(8,128)}), f32[2,512,8]{1,2,0:T(8,128)}) %reduce-scatter.2.cloned.1.call-update) | async-done | bytes 32784 | tf_op jit(solution)/shard_map/reduce_scatter | solution.py:101
  (155 shorter events, 56.8 us)
Async XLA Ops:
  97.7 0.7 copy-start.8
  127.1 17.5 %collective-permute-start = (f32[36,1,4096]{2,1,0:T(1,128)S(1)}, f32[36,1,4096]{2,1,0:T(1,128)S(1)}, u32[]{:S(2)}, u32[]{:S(2)}) collective-permute-start(f32[36,1,4096]{2,1,0:T(1,128)S(1)} %bitcast.93), channel_id=1, source_target_pairs={{0,1},{1,2},{2,3},{4,5},{5,6},{6,7},{8,9},{9,10},{10,11},{12,13},{... | collective-permute-start | bytes 1769480 | tf_op jit(solution)/shard_map/ppermute | solution.py:18
  132.1 17.0 %collective-permute-start.1 = (f32[36,1,4096]{2,1,0:T(1,128)}, f32[36,1,4096]{2,1,0:T(1,128)}, u32[]{:S(2)}, u32[]{:S(2)}) collective-permute-start(f32[36,1,4096]{2,1,0:T(1,128)} %bitcast.3), channel_id=1, source_target_pairs={{1,0},{2,1},{3,2},{5,4},{6,5},{7,6},{9,8},{10,9},{11,10},{13,12},{... | collective-permute-start | bytes 1769480 | tf_op jit(solution)/shard_map/ppermute | solution.py:19
  155.9 6.9 %copy-start.6 = (f32[512]{0:T(512)S(1)}, f32[512]{0:T(512)}, u32[]{:S(2)}) copy-start(f32[512]{0:T(512)} %param.14) | copy-start | bytes 6148
  155.9 6.9 %copy-start.7 = (s32[512]{0:T(512)S(1)}, s32[512]{0:T(512)}, u32[]{:S(2)}) copy-start(s32[512]{0:T(512)} %param.13) | copy-start | bytes 6148
  158.8 6.7 %copy-start.5 = (s32[8]{0:T(128)S(1)}, s32[8]{0:T(128)}, u32[]{:S(2)}) copy-start(s32[8]{0:T(128)} %param.15) | copy-start | bytes 100
  158.8 15.0 %all-to-all-start = ((f32[8,1,20480]{2,1,0:T(1,128)}), f32[8,1,20480]{2,1,0:T(1,128)S(1)}, u32[]{:S(2)}, u32[]{:S(2)}) async-start(f32[8,1,20480]{2,1,0:T(1,128)} %transpose.120), calls=%async_computation | async-start | bytes 1310720 | tf_op jit(solution)/shard_map/all_to_all | solution.py:73
  185.1 1.4 copy-start
  199.3 2.1 copy-start.2
  201.5 2.1 copy-start.1
  207.7 6.8 %copy-start.3 = (f32[8,512,8]{1,2,0:T(8,128)S(1)}, f32[8,512,8]{1,2,0:T(8,128)}, u32[]{:S(2)}) copy-start(f32[8,512,8]{1,2,0:T(8,128)} %constant_dynamic-update-slice_fusion.7) | copy-start | bytes 393220
  207.8 6.8 %copy-start.4 = (f32[512,8]{0,1:T(8,128)S(1)}, f32[512,8]{0,1:T(8,128)}, u32[]{:S(2)}) copy-start(f32[512,8]{0,1:T(8,128)} %reduce_sum.73) | copy-start | bytes 49156
  210.9 14.6 %all-to-all-start.1 = ((f32[8,1,20480]{2,1,0:T(1,128)}), f32[8,1,20480]{2,1,0:T(1,128)S(1)}, u32[]{:S(2)}, u32[]{:S(2)}) async-start(f32[8,1,20480]{2,1,0:T(1,128)} %reshape.602), calls=%async_computation.1 | async-start | bytes 1310720 | tf_op jit(solution)/shard_map/all_to_all | solution.py:106
  214.5 23.4 %reduce-scatter.2.cloned.1.call-start = ((), (), s32[]{:S(2)}) async-start(), calls=%async_computation.3 | async-start | bytes 163840 | tf_op jit(solution)/shard_map/reduce_scatter | solution.py:101
Sparse Core Ops, SparseCore 0:
  218.1 19.6 reduce-scatter.1
where the time goes:
time: 249 us; the launch traced here: 245 us
  local copies, waits for them, and re-layouts  128 us (51%)
  matrix products  37.9 us (15%)
  waiting for transfers between devices  30.7 us (12%)
  other arithmetic  17.5 us (7%)
  between operations  16.1 us (6%)
  starting transfers between devices  13.8 us (6%)
    gather x120, local copies, waits for them, and re-layouts  84.8 us
    dot_general x1, matrix products, shear_lines(): jnp.einsum('prbj,pji->prbi', windows, band_matrix, precision=lax.Precisio...  27.7 us
    gather x8, local copies, waits for them, and re-layouts, local(): lax.dynamic_slice_in_dim(one_plane, span_pad + lift_one, row_total, 1)  16.5 us
    all_to_all x1, waiting for transfers between devices, local(): lax.all_to_all(returning, 'gy', split_axis=0, concat_axis=1, tiled=True)  10.3 us
    ppermute x1, waiting for transfers between devices, with_halo(): before = lax.ppermute(last, axis, up)  9.42 us
    dot_general x1, matrix products, local(): jnp.einsum('cij,jcz->zci', operator, columns, precision=lax.Precision.HIG...  6.73 us
    reduce_scatter x1, waiting for transfers between devices, local(): lax.psum_scatter(partial_terms, 'gz', scatter_dimension=0, tiled=True)  6.54 us
    unnamed x30, local copies, waits for them, and re-layouts  6.36 us
  transfers between devices with their start and end apart: 5, of which 5 were waited for; matrix products, arithmetic and copies ran while one was open for 7% of the time, Pallas kernels for 0%

commit v1 on v0

v1 whole, which is shorter than its diff:
```python
import functools

import jax
import jax.numpy as jnp
from jax import lax
from jax.experimental import pallas as pl
from jax.experimental.pallas import tpu as pltpu
from jax.sharding import PartitionSpec as P

TAPS = 64
OFFX = 64
OFFZ = 4
LANES = 128
BELOW = TAPS // 2 - 1
VMEM_LIMIT = 48 * 1024 * 1024

SMEM_SPEC = pl.BlockSpec(memory_space=pltpu.SMEM)
VMEM_SPEC = pl.BlockSpec(memory_space=pltpu.VMEM)


def tap_weight(offset, fraction):
    moved = offset.astype(jnp.float32) - fraction
    inside = (offset >= 1 - TAPS // 2) & (offset <= TAPS // 2)
    value = jnp.sinc(moved) * (0.5 + 0.5 * jnp.cos(jnp.pi * moved / (TAPS // 2 + 1)))
    return jnp.where(inside, value, jnp.zeros_like(value))


def tap_weight_in_kernel(offset, fraction):
    moved = offset.astype(jnp.float32) - fraction
    inside = (offset >= 1 - TAPS // 2) & (offset <= TAPS // 2)
    angle = jnp.pi * moved
    at_zero = moved == 0.0
    sinc = jnp.where(at_zero, 1.0, jnp.sin(angle) / jnp.where(at_zero, 1.0, angle))
    window = 0.5 + 0.5 * jnp.cos(angle / (TAPS // 2 + 1))
    return jnp.where(inside, sinc * window, 0.0)


def split_high_low(value):
    high = value.astype(jnp.bfloat16)
    low = (value - high.astype(jnp.float32)).astype(jnp.bfloat16)
    return high, low


def shear_x_kernel(first_ref, shifts_ref, fracs_ref, planes_ref, out_ref, margin_ref):
    plane_count, rows, lanes = planes_ref.shape
    before, after = 8, 8
    line = lax.broadcasted_iota(jnp.int32, (lanes, lanes), 0)
    lane = lax.broadcasted_iota(jnp.int32, (lanes, lanes), 1)
    own_side = lane <= line
    tap = (lanes - lax.broadcasted_iota(jnp.int32, (8, lanes), 1)) % lanes
    lane_of_row = lax.broadcasted_iota(jnp.int32, (rows, lanes), 1)
    zeros = jnp.zeros((8, lanes), jnp.float32)
    first = first_ref[0]

    def one_plane(z, carry):
        shift = shifts_ref[first + z]
        frac = fracs_ref[first + z]
        margin_ref[z, 0:before, :] = zeros
        margin_ref[z, before:before + rows, :] = planes_ref[z]
        margin_ref[z, before + rows:before + rows + after, :] = zeros
        base = tap_weight_in_kernel(tap - BELOW, frac)
        spread = pltpu.roll(
            jnp.broadcast_to(base[0:1], (lanes, lanes)), 0, 1, stride=1, stride_axis=0
        )
        own = jnp.where(own_side, spread, 0.0)
        band = jnp.concatenate([own, spread - own], axis=0)
        band = jnp.concatenate(split_high_low(band), axis=1)
        start = shift - BELOW + before * lanes
        top = start // lanes
        turn = start - top * lanes
        back = lanes - turn
        parts = [
            pltpu.roll(margin_ref[z, pl.ds(top + i, rows), :], back, 1) for i in range(3)
        ]
        keep = lane_of_row < back
        window = jnp.concatenate(
            [jnp.where(keep, parts[0], parts[1]), jnp.where(keep, parts[1], parts[2])], axis=1
        )
        window = jnp.concatenate(split_high_low(window), axis=0)
        product = jnp.dot(window, band, preferred_element_type=jnp.float32)
        product = product[:rows] + product[rows:]
        out_ref[z] = product[:, :lanes] + product[:, lanes:]
        return carry

    lax.fori_loop(0, plane_count, one_plane, 0, unroll=2)


def shear_x(volume, x_offsets, x_fracs, first_plane):
    plane_count, rows, lanes = volume.shape
    return pl.pallas_call(
        shear_x_kernel,
        out_shape=jax.ShapeDtypeStruct(volume.shape, jnp.float32),
        in_specs=[SMEM_SPEC, SMEM_SPEC, SMEM_SPEC, VMEM_SPEC],
        out_specs=VMEM_SPEC,
        scratch_shapes=[pltpu.VMEM((plane_count, rows + 16, lanes), jnp.float32)],
        compiler_params=pltpu.CompilerParams(vmem_limit_bytes=VMEM_LIMIT),
        name="shear_x",
    )(first_plane.reshape(1), x_offsets, x_fracs, volume)


def shear_z_kernel(plane_count, depth, shift_ref, frac_ref, left_ref, own_ref, right_ref, out_ref):
    lanes = own_ref.shape[1]
    rows = own_ref.shape[0] // plane_count
    reach = plane_count + 2 * depth
    target = lax.broadcasted_iota(jnp.int32, (plane_count, reach), 0)
    source = lax.broadcasted_iota(jnp.int32, (plane_count, reach), 1)
    mixing = tap_weight_in_kernel(source - depth - target - shift_ref[0], frac_ref[0])
    mixing_high, mixing_low = split_high_low(mixing)
    mixing = jnp.concatenate(
        [
            jnp.concatenate([mixing_high, mixing_high], axis=1),
            jnp.concatenate([mixing_low, mixing_low], axis=1),
        ],
        axis=0,
    )

    def stack_of(row):
        return jnp.concatenate(
            [
                left_ref[pl.ds(row, depth, stride=rows), :],
                own_ref[pl.ds(row, plane_count, stride=rows), :],
                right_ref[pl.ds(row, depth, stride=rows), :],
            ],
            axis=0,
        )

    chunks, _, width = out_ref.shape
    per_chunk = width // lanes
    pair = 2 if per_chunk % 2 == 0 else 1

    for chunk in range(chunks):
        for piece in range(per_chunk // pair):
            row = chunk * per_chunk + piece * pair
            stack = jnp.concatenate([stack_of(row + i) for i in range(pair)], axis=1)
            stack = jnp.concatenate(split_high_low(stack), axis=0)
            product = jnp.dot(mixing, stack, preferred_element_type=jnp.float32)
            out_ref[chunk, :, piece * pair * lanes:(piece + 1) * pair * lanes] = (
                product[:plane_count] + product[plane_count:]
            )


def shear_z(own, left, right, z_offsets, z_fracs, chunks):
    plane_count, rows, lanes = own.shape
    depth = left.shape[0]
    return pl.pallas_call(
        functools.partial(shear_z_kernel, plane_count, depth),
        out_shape=jax.ShapeDtypeStruct((chunks, plane_count, rows * lanes // chunks), jnp.float32),
        in_specs=[SMEM_SPEC, SMEM_SPEC, VMEM_SPEC, VMEM_SPEC, VMEM_SPEC],
        out_specs=VMEM_SPEC,
        compiler_params=pltpu.CompilerParams(vmem_limit_bytes=VMEM_LIMIT),
        name="shear_z",
    )(
        z_offsets,
        z_fracs,
        left.reshape(depth * rows, lanes),
        own.reshape(plane_count * rows, lanes),
        right.reshape(depth * rows, lanes),
    )


def shear_y_kernel(
    total_planes, first_ref, slopes_ref, shifts_ref, fracs_ref, in_ref, out_ref, tilted_ref,
    taps_ref, totals_ref,
):
    ny, plane_count, width = in_ref.shape
    tilts = slopes_ref.shape[0]
    span = ny // 4
    shares = tilted_ref.shape[0]
    tap_rows = taps_ref.shape[0]
    distance = lax.broadcasted_iota(jnp.int32, (tap_rows, width), 0) - (ny - 1)
    taps_ref[...] = tap_weight_in_kernel(distance - shifts_ref[...], fracs_ref[...])

    for tile in range(width // LANES):
        lanes = slice(tile * LANES, (tile + 1) * LANES)
        weights = [
            jnp.broadcast_to(taps_ref[d:d + 1, lanes], (8, LANES)) for d in range(2 * ny - 1)
        ]
        for block in range(plane_count // 8):
            planes = slice(block * 8, (block + 1) * 8)
            source = [in_ref[j, planes, lanes] for j in range(ny)]
            for i in range(ny):
                value = weights[ny - 1 - i] * source[0]
                for j in range(1, ny):
                    value = value + weights[j - i + ny - 1] * source[j]
                out_ref[i, planes, lanes] = value

    lifts = 2 * span + 1
    entry = lax.broadcasted_iota(jnp.int32, (lifts * tilts, plane_count), 0)
    plane = lax.broadcasted_iota(jnp.int32, (lifts * tilts, plane_count), 1) + first_ref[0]
    lift = entry // tilts - span
    tilt = entry - (lift + span) * tilts
    slope = jnp.zeros_like(tilt)
    for t in range(tilts):
        slope = jnp.where(tilt == t, slopes_ref[t], slope)
    numerator = slope * (2 * plane - total_planes) * ny
    floor_at = lift * (16 * total_planes)
    chosen = (numerator >= floor_at) & (numerator < floor_at + 16 * total_planes)
    chosen = jnp.where(chosen, 1.0, 0.0).astype(jnp.bfloat16)
    chosen = jnp.concatenate([chosen, chosen], axis=1)

    totals_ref[...] = jnp.zeros(totals_ref.shape, jnp.float32)
    for j in range(ny):
        sums = jnp.dot(
            chosen,
            jnp.concatenate(split_high_low(out_ref[j]), axis=0),
            preferred_element_type=jnp.float32,
        )
        for l in range(lifts):
            i = j - (l - span)
            if 0 <= i < ny:
                for tile in range(width // LANES):
                    place = (tile * ny + i) * tilts
                    totals_ref[place:place + tilts, :] += sums[
                        l * tilts:(l + 1) * tilts, tile * LANES:(tile + 1) * LANES
                    ]
    per_share = tilts // shares
    for t in range(tilts):
        for tile in range(width // LANES):
            lanes = slice(tile * LANES, (tile + 1) * LANES)
            tilted_ref[t // per_share, t % per_share, :, lanes] = (
                totals_ref[pl.ds(tile * ny * tilts + t, ny, stride=tilts), :] * total_planes ** (-0.5)
            )


def shear_y(columns, y_offsets, y_fracs, slopes, first_plane, total_planes, shares):
    ny, plane_count, width = columns.shape
    tilts = slopes.shape[0]
    return pl.pallas_call(
        functools.partial(shear_y_kernel, total_planes),
        out_shape=(
            jax.ShapeDtypeStruct(columns.shape, jnp.float32),
            jax.ShapeDtypeStruct((shares, tilts // shares, ny, width), jnp.float32),
        ),
        in_specs=[SMEM_SPEC, SMEM_SPEC, VMEM_SPEC, VMEM_SPEC, VMEM_SPEC],
        out_specs=(VMEM_SPEC, VMEM_SPEC),
        scratch_shapes=[
            pltpu.VMEM((2 * ny, width), jnp.float32),
            pltpu.VMEM((width // LANES * ny * tilts, LANES), jnp.float32),
        ],
        compiler_params=pltpu.CompilerParams(vmem_limit_bytes=VMEM_LIMIT),
        name="shear_y",
    )(first_plane.reshape(1), slopes, y_offsets.reshape(1, width), y_fracs.reshape(1, width), columns)


def finish_kernel(landed_ref, shares_ref, rotated_ref, projections_ref):
    groups, plane_count, width = landed_ref.shape
    per_group = width // LANES
    rows = groups * per_group
    for group in range(groups):
        for tile in range(per_group):
            rotated_ref[pl.ds(group * per_group + tile, plane_count, stride=rows), :] = landed_ref[
                group, :, tile * LANES:(tile + 1) * LANES
            ]
    total = shares_ref[0]
    for share in range(1, shares_ref.shape[0]):
        total = total + shares_ref[share]
    projections_ref[...] = total


def finish(landed, shares):
    groups, plane_count, width = landed.shape
    return pl.pallas_call(
        finish_kernel,
        out_shape=(
            jax.ShapeDtypeStruct((plane_count * groups * width // LANES, LANES), jnp.float32),
            jax.ShapeDtypeStruct(shares.shape[1:], jnp.float32),
        ),
        in_specs=[VMEM_SPEC, VMEM_SPEC],
        out_specs=(VMEM_SPEC, VMEM_SPEC),
        compiler_params=pltpu.CompilerParams(vmem_limit_bytes=VMEM_LIMIT),
        name="finish",
    )(landed, shares)


def narrow_columns(columns, y_offsets, y_fracs, slopes, first_plane, total_planes):
    row_total, plane_count, col_local = columns.shape
    target_row = jnp.arange(row_total, dtype=jnp.int32)[:, None]
    source_row = jnp.arange(row_total, dtype=jnp.int32)[None, :]
    operator = tap_weight(
        (source_row - target_row)[None] - y_offsets[:, None, None], y_fracs[:, None, None]
    )
    rotated = jnp.einsum("cij,jzc->izc", operator, columns, precision=lax.Precision.HIGHEST)
    span = row_total // 4
    planes = first_plane + jnp.arange(plane_count, dtype=jnp.int32)
    padded = jnp.pad(rotated, ((span, span), (0, 0), (0, 0)))
    per_tilt = []
    for tilt in range(slopes.shape[0]):
        lifts = slopes[tilt] * (2 * planes - total_planes) * row_total // (16 * total_planes)
        moved = jax.vmap(
            lambda one_plane, lift: lax.dynamic_slice_in_dim(one_plane, span + lift, row_total, 0),
            in_axes=(1, 0),
        )(padded, lifts)
        per_tilt.append(jnp.sum(moved, axis=0))
    return rotated, jnp.stack(per_tilt) * total_planes ** (-0.5)


def local(volume, x_offsets, x_fracs, z_offsets, z_fracs, y_offsets, y_fracs, slopes):
    depth = TAPS // 2 + OFFZ
    plane_count, row_local, width_all = volume.shape
    groups, shares = lax.axis_size("gy"), lax.axis_size("gz")
    assert row_local == 1 and width_all % LANES == 0
    rows = width_all // LANES
    col_local = width_all // groups
    total_planes = plane_count * shares
    first_plane = (lax.axis_index("gz") * plane_count).astype(jnp.int32)
    sheared = shear_x(volume.reshape(plane_count, rows, LANES), x_offsets, x_fracs, first_plane)
    up = [(i, i + 1) for i in range(shares - 1)]
    down = [(j, i) for i, j in up]
    left = lax.ppermute(sheared[plane_count - depth:], "gz", up)
    right = lax.ppermute(sheared[:depth], "gz", down)
    if col_local % LANES:
        mixed = shear_z(sheared, left, right, z_offsets, z_fracs, rows)
        mixed = jnp.moveaxis(mixed, 0, 1).reshape(plane_count, groups, col_local)
        outgoing = jnp.moveaxis(mixed, 1, 0)
        columns = lax.all_to_all(outgoing, "gy", split_axis=0, concat_axis=0, tiled=True)
        rotated, tilted = narrow_columns(
            columns, y_offsets, y_fracs, slopes, first_plane, total_planes
        )
        projections = lax.psum_scatter(tilted, "gz", scatter_dimension=0, tiled=True)
        landed = lax.all_to_all(rotated, "gy", split_axis=0, concat_axis=0, tiled=True)
        rotated = jnp.moveaxis(landed, 0, 1).reshape(plane_count, row_local, width_all)
        return rotated, jnp.swapaxes(projections, 1, 2)
    outgoing = shear_z(sheared, left, right, z_offsets, z_fracs, groups)
    columns = lax.all_to_all(outgoing, "gy", split_axis=0, concat_axis=0, tiled=True)
    rotated, tilted = shear_y(
        columns, y_offsets, y_fracs, slopes, first_plane, total_planes, shares
    )
    tilted = lax.all_to_all(tilted, "gz", split_axis=0, concat_axis=0, tiled=True)
    landed = lax.all_to_all(rotated, "gy", split_axis=0, concat_axis=0, tiled=True)
    rotated, projections = finish(landed, tilted)
    return (
        rotated.reshape(plane_count, row_local, width_all),
        jnp.swapaxes(projections, 1, 2),
    )


def solution(mesh):
    return jax.shard_map(
        local,
        mesh=mesh,
        in_specs=(P("gz", "gy", None), P(), P(), P("gy"), P("gy"), P("gy"), P("gy"), P()),
        out_specs=(P("gz", "gy", None), P("gz", "gy", None)),
        check_vma=False,
    )
```

time: 249 us -> 74.7 us (0.30); the launches traced: 245 us -> 74.3 us
  local copies, waits for them, and re-layouts: 128 us -> 2.6 us
  blocking collectives: 0 us -> 40 us
  matrix products: 37.9 us -> 0 us
  waiting for transfers between devices: 30.7 us -> 11.2 us
  other arithmetic: 17.5 us -> 0 us
  between operations: 16.1 us -> 2 us
  Pallas kernels: 0 us -> 11.5 us
  starting transfers between devices: 13.8 us -> 6.89 us
    gather x128 -> x0, local copies, waits for them, and re-layouts: 101 us -> none
    all_to_all x0 -> x3, blocking collectives: none -> 40 us  [the longest x1 14.8 us: local(): lax.all_to_all(outgoing, 'gy', split_axis=0, concat_axis=0, tiled=True)]
    dot_general x3 -> x0, matrix products: 37.9 us -> none  [the longest x1 27.7 us: shear_lines(): jnp.einsum('prbj,pji->prbi', windows, band_matrix, precision=lax.Precisio...]
    all_to_all x2 -> x0, waiting for transfers between devices: 12.4 us -> none  [the longest x1 10.3 us: local(): lax.all_to_all(returning, 'gy', split_axis=0, concat_axis=1, tiled=True)]
    pallas_call x0 -> x4, Pallas kernels: none -> 11.5 us  [the longest x1 7.06 us: shear_x(): pl.pallas_call(shear_x_kernel, out_shape=jax.ShapeDtypeStruct(volume.shap...]
    reshape x4 -> x0, local copies, waits for them, and re-layouts: 7.93 us -> none  [the longest x1 3.14 us: local(): jnp.transpose(returning, (2, 3, 1, 0))]
    all_to_all x2 -> x0, starting transfers between devices: 7.55 us -> none  [the longest x1 4 us: local(): lax.all_to_all(outgoing, 'gy', split_axis=0, concat_axis=1, tiled=True)]
    gather x6 -> x0, other arithmetic: 7.08 us -> none  [the longest x4 5.47 us: local(): lax.dynamic_slice_in_dim(one_plane, span_pad + lift_one, row_total, 1)]
  transfers between devices with their start and end apart: 5 -> 2, of which waited for: 5 -> 2; matrix products, arithmetic and copies ran while one was open for 7% -> 0% of each run, Pallas kernels for 0% -> 0%
where the time goes in v1:
time: 74.7 us; the launch traced here: 74.3 us
  blocking collectives  40 us (54%)
  Pallas kernels  11.5 us (15%)
  waiting for transfers between devices  11.2 us (15%)
  starting transfers between devices  6.89 us (9%)
  local copies, waits for them, and re-layouts  2.6 us (3%)
  between operations  2 us (3%)
    all_to_all x1, blocking collectives, local(): lax.all_to_all(outgoing, 'gy', split_axis=0, concat_axis=0, tiled=True)  14.8 us
    all_to_all x1, blocking collectives, local(): lax.all_to_all(rotated, 'gy', split_axis=0, concat_axis=0, tiled=True)  13.5 us
    all_to_all x1, blocking collectives, local(): lax.all_to_all(tilted, 'gz', split_axis=0, concat_axis=0, tiled=True)  11.7 us
    ppermute x1, waiting for transfers between devices, local(): right = lax.ppermute(sheared[:depth], 'gz', down)  10.1 us
    pallas_call x1, Pallas kernels, shear_x(): pl.pallas_call(shear_x_kernel, out_shape=jax.ShapeDtypeStruct(volume.shap...  7.06 us
    ppermute x1, starting transfers between devices, local(): left = lax.ppermute(sheared[plane_count - depth:], 'gz', up)  5.59 us
    unnamed x12, local copies, waits for them, and re-layouts  2.45 us
    pallas_call x1, Pallas kernels, shear_z(): pl.pallas_call(functools.partial(shear_z_kernel, plane_count, depth), out...  1.52 us
  transfers between devices with their start and end apart: 2, of which 2 were waited for; matrix products, arithmetic and copies ran while one was open for 0% of the time, Pallas kernels for 0%

profile of v1, /device:TPU:0, one launch (start us, length us, event | category | flops | bytes accessed | tf_op | source)
XLA Modules:
  0.0 74.3 jit_solution(8279290605028445138)
XLA Ops:
  0.6 0.0 copy-start.4
  0.6 0.0 copy-start.3
  0.7 0.7 copy-done.4
  1.3 0.0 copy-done.3
  1.3 0.0 copy-start
  1.3 1.1 %copy-done = f32[40,1,4096]{2,1,0:T(1,128)S(1)} copy-done((f32[40,1,4096]{2,1,0:T(1,128)S(1)}, f32[40,1,4096]{2,1,0:T(1,128)}, u32[]{:S(2)}) %copy-start) | copy-done | bytes 655384
  2.4 7.1 %shear_x.1 = f32[40,32,128]{2,1,0:T(8,128)S(1)} custom-call(s32[1]{0:T(128)} %bitcast.first_ref, s32[160]{0:T(256)S(1)} %copy-done.3, f32[160]{0:T(256)S(1)} %copy-done.4, f32[40,32,128]{2,1,0:T(8,128)S(1)} %bitcast.10), custom_call_target="tpu_custom_call" | custom-call | tf_op jit(solution)/shard_map/shear_x/pallas_call | solution.py:90
  9.5 0.1 fusion
  9.6 1.3 %collective-permute-start.1 = (f32[36,32,128]{2,1,0:T(8,128)S(1)}, f32[36,32,128]{2,1,0:T(8,128)S(1)}, u32[]{:S(2)}, u32[]{:S(2)}) collective-permute-start(f32[36,32,128]{2,1,0:T(8,128)S(1)} %get-tuple-element.12), channel_id=1, source_target_pairs={{1,0},{2,1},{3,2},{5,4},{6,5},{7,6},{9,8},{10,9},{11,10},{13,12},{... | collective-permute-start | bytes 1769480 | tf_op jit(solution)/shard_map/ppermute | solution.py:310
  10.9 5.6 %collective-permute-start = (f32[36,32,128]{2,1,0:T(8,128)S(1)}, f32[36,32,128]{2,1,0:T(8,128)S(1)}, u32[]{:S(2)}, u32[]{:S(2)}) collective-permute-start(f32[36,32,128]{2,1,0:T(8,128)S(1)} %get-tuple-element.13), channel_id=1, source_target_pairs={{0,1},{1,2},{2,3},{4,5},{5,6},{6,7},{8,9},{9,10},{10,11},{12,13},{... | collective-permute-start | bytes 1769480 | tf_op jit(solution)/shard_map/ppermute | solution.py:309
  17.8 10.1 %collective-permute-done.1 = f32[36,32,128]{2,1,0:T(8,128)S(1)} collective-permute-done((f32[36,32,128]{2,1,0:T(8,128)S(1)}, f32[36,32,128]{2,1,0:T(8,128)S(1)}, u32[]{:S(2)}, u32[]{:S(2)}) %collective-permute-start.1) | collective-permute-done | bytes 589856 | tf_op jit(solution)/shard_map/ppermute | solution.py:310
  27.9 1.2 %collective-permute-done = f32[36,32,128]{2,1,0:T(8,128)S(1)} collective-permute-done((f32[36,32,128]{2,1,0:T(8,128)S(1)}, f32[36,32,128]{2,1,0:T(8,128)S(1)}, u32[]{:S(2)}, u32[]{:S(2)}) %collective-permute-start) | collective-permute-done | bytes 589856 | tf_op jit(solution)/shard_map/ppermute | solution.py:309
  29.1 1.5 %shear_z.1 = f32[8,40,512]{2,1,0:T(8,128)S(1)} custom-call(s32[1]{0:T(128)S(6)} %copy.11.shift_ref, f32[1]{0:T(128)S(6)} %copy.12.frac_ref, f32[1152,128]{1,0:T(8,128)S(1)} %bitcast.12, f32[1280,128]{1,0:T(8,128)S(1)} %bitcast.9, f32[1152,128]{1,0:T(8,128)S(1)} %bitcast.11), custom_call_target="tpu_custom_call" | custom-call | tf_op jit(solution)/shard_map/shear_z/pallas_call | solution.py:145
  30.6 0.0 copy-start.2
  30.6 14.8 %all_to_all.15.in_ref = f32[8,40,512]{2,1,0:T(8,128)S(1)} all-to-all(f32[8,40,512]{2,1,0:T(8,128)S(1)} %shear_z.1), channel_id=1, replica_groups=mesh['gy'=8,'gz'=4] {'gy'}, dimensions={0} | all-to-all | bytes 1310720 | tf_op jit(solution)/shard_map/all_to_all | solution.py:324
  45.4 0.0 copy-start.1
  45.4 0.0 copy-start.5
  45.4 0.0 copy-done.2
  45.4 0.7 copy-done.1
  46.1 0.0 copy-done.5
  46.1 1.5 %shear_y.1 = (f32[8,40,512]{2,1,0:T(8,128)S(1)}, f32[4,2,8,512]{3,2,1,0:T(8,128)S(1)}) custom-call(s32[1]{0:T(128)} %bitcast.first_ref, s32[8]{0:T(128)S(1)} %copy-done.5, s32[1,512]{1,0:T(1,128)S(1)} %bitcast.13, f32[1,512]{1,0:T(1,128)S(1)} %bitcast.14, f32[8,40,512]{2,1,0:T(8,128)S(1)} %all_to_all.15.in_ref), custom_call_target="tpu_custom_call" | custom-call | tf_op jit(solution)/shard_map/shear_y/pallas_call | solution.py:228
  47.6 11.7 %all_to_all.16.shares_ref = f32[4,2,8,512]{3,2,1,0:T(8,128)S(1)} all-to-all(f32[4,2,8,512]{3,2,1,0:T(8,128)S(1)} %get-tuple-element.7), channel_id=1, replica_groups=mesh['gy'=8,'gz'=4] {'gz'}, dimensions={0} | all-to-all | bytes 262144 | tf_op jit(solution)/shard_map/all_to_all | solution.py:328
  59.3 13.5 %all_to_all.17.landed_ref = f32[8,40,512]{2,1,0:T(8,128)S(1)} all-to-all(f32[8,40,512]{2,1,0:T(8,128)S(1)} %get-tuple-element.6), channel_id=1, replica_groups=mesh['gy'=8,'gz'=4] {'gy'}, dimensions={0} | all-to-all | bytes 1310720 | tf_op jit(solution)/shard_map/all_to_all | solution.py:329
  72.8 1.5 %finish.1 = (f32[1280,128]{1,0:T(8,128)}, f32[2,8,512]{2,1,0:T(8,128)}) custom-call(f32[8,40,512]{2,1,0:T(8,128)S(1)} %all_to_all.17.landed_ref, f32[4,2,8,512]{3,2,1,0:T(8,128)S(1)} %all_to_all.16.shares_ref), custom_call_target="tpu_custom_call" | custom-call | tf_op jit(solution)/shard_map/finish/pallas_call | solution.py:262
Async XLA Ops:
  0.6 0.7 copy-start.4
  0.6 0.7 copy-start.3
  1.3 1.1 %copy-start = (f32[40,1,4096]{2,1,0:T(1,128)S(1)}, f32[40,1,4096]{2,1,0:T(1,128)}, u32[]{:S(2)}) copy-start(f32[40,1,4096]{2,1,0:T(1,128)} %param.8) | copy-start | bytes 1966084
  9.6 18.3 %collective-permute-start.1 = (f32[36,32,128]{2,1,0:T(8,128)S(1)}, f32[36,32,128]{2,1,0:T(8,128)S(1)}, u32[]{:S(2)}, u32[]{:S(2)}) collective-permute-start(f32[36,32,128]{2,1,0:T(8,128)S(1)} %get-tuple-element.12), channel_id=1, source_target_pairs={{1,0},{2,1},{3,2},{5,4},{6,5},{7,6},{9,8},{10,9},{11,10},{13,12},{... | collective-permute-start | bytes 1769480 | tf_op jit(solution)/shard_map/ppermute | solution.py:310
  10.9 18.1 %collective-permute-start = (f32[36,32,128]{2,1,0:T(8,128)S(1)}, f32[36,32,128]{2,1,0:T(8,128)S(1)}, u32[]{:S(2)}, u32[]{:S(2)}) collective-permute-start(f32[36,32,128]{2,1,0:T(8,128)S(1)} %get-tuple-element.13), channel_id=1, source_target_pairs={{0,1},{1,2},{2,3},{4,5},{5,6},{6,7},{8,9},{9,10},{10,11},{12,13},{... | collective-permute-start | bytes 1769480 | tf_op jit(solution)/shard_map/ppermute | solution.py:309
  30.6 14.8 %copy-start.2 = (f32[512]{0:T(512)S(1)}, f32[512]{0:T(512)}, u32[]{:S(2)}) copy-start(f32[512]{0:T(512)} %param.14) | copy-start | bytes 6148
  45.4 0.7 copy-start.1
  45.4 0.7 copy-start.5

commit v2 on v1

v2 whole, which is shorter than its diff:
```python
import functools

import jax
import jax.numpy as jnp
from jax import lax
from jax.experimental import pallas as pl
from jax.experimental.pallas import tpu as pltpu
from jax.sharding import PartitionSpec as P

TAPS = 64
OFFX = 64
OFFZ = 4
LANES = 128
PARTS = 1
BELOW = TAPS // 2 - 1
VMEM_LIMIT = 48 * 1024 * 1024

SMEM_SPEC = pl.BlockSpec(memory_space=pltpu.SMEM)
VMEM_SPEC = pl.BlockSpec(memory_space=pltpu.VMEM)


def tap_weight(offset, fraction):
    moved = offset.astype(jnp.float32) - fraction
    inside = (offset >= 1 - TAPS // 2) & (offset <= TAPS // 2)
    value = jnp.sinc(moved) * (0.5 + 0.5 * jnp.cos(jnp.pi * moved / (TAPS // 2 + 1)))
    return jnp.where(inside, value, jnp.zeros_like(value))


def tap_weight_in_kernel(offset, fraction):
    moved = offset.astype(jnp.float32) - fraction
    inside = (offset >= 1 - TAPS // 2) & (offset <= TAPS // 2)
    angle = jnp.pi * moved
    at_zero = moved == 0.0
    sinc = jnp.where(at_zero, 1.0, jnp.sin(angle) / jnp.where(at_zero, 1.0, angle))
    window = 0.5 + 0.5 * jnp.cos(angle / (TAPS // 2 + 1))
    return jnp.where(inside, sinc * window, 0.0)


def split_high_low(value):
    high = value.astype(jnp.bfloat16)
    low = (value - high.astype(jnp.float32)).astype(jnp.bfloat16)
    return high, low


def shear_x_kernel(
    classes, first_ref, shifts_hbm, fracs_hbm, planes_hbm, *rest
):
    parts = len(rest) - 7
    out_refs = rest[:parts]
    planes_ref, margin_ref, base_ref, shifts_ref, fracs_ref, small_sem, plane_sem = rest[parts:]
    plane_count, rows, lanes = planes_ref.shape
    per_class = rows // classes
    before, after = 8, margin_ref.shape[1] - rows - 8
    blocks = plane_sem.shape[0]
    per_block = plane_count // blocks
    small = [
        pltpu.make_async_copy(shifts_hbm, shifts_ref, small_sem.at[0]),
        pltpu.make_async_copy(fracs_hbm, fracs_ref, small_sem.at[1]),
    ]
    large = [
        pltpu.make_async_copy(
            planes_hbm.at[b * per_block:(b + 1) * per_block],
            planes_ref.at[b * per_block:(b + 1) * per_block],
            plane_sem.at[b],
        )
        for b in range(blocks)
    ]
    for copy in small + large:
        copy.start()
    line = lax.broadcasted_iota(jnp.int32, (lanes, lanes), 0)
    lane = lax.broadcasted_iota(jnp.int32, (lanes, lanes), 1)
    own_side = lane <= line
    tap = (lanes - lax.broadcasted_iota(jnp.int32, (plane_count, lanes), 1)) % lanes
    lane_of_row = lax.broadcasted_iota(jnp.int32, (per_class, lanes), 1)
    zeros = jnp.zeros((8, lanes), jnp.float32)
    first = first_ref[0]
    for copy in small:
        copy.wait()
    for z in range(plane_count):
        base_ref[z:z + 1, :] = jnp.full((1, lanes), fracs_ref[first + z], jnp.float32)
    base_ref[...] = tap_weight_in_kernel(tap - BELOW, base_ref[...])

    def one_plane(z, carry):
        margin_ref[z, 0:before, :] = zeros
        margin_ref[z, before:before + rows, :] = planes_ref[z]
        margin_ref[z, before + rows:before + rows + after, :] = zeros
        spread = pltpu.roll(
            jnp.broadcast_to(base_ref[pl.ds(z, 1), :], (lanes, lanes)),
            0, 1, stride=1, stride_axis=0,
        )
        own = jnp.where(own_side, spread, 0.0)
        band = jnp.concatenate([own, spread - own], axis=0)
        band = jnp.concatenate(split_high_low(band), axis=1)
        start = shifts_ref[first + z] - BELOW + before * lanes
        top = start // lanes
        back = lanes - (start - top * lanes)
        keep = lane_of_row < back
        turned = [
            pltpu.roll(margin_ref[z, pl.ds(top + i, per_class, stride=classes), :], back, 1)
            for i in range(classes + 2)
        ]
        lines = [jnp.where(keep, turned[i], turned[i + 1]) for i in range(classes + 1)]
        window = jnp.concatenate(
            [jnp.concatenate(lines[:-1], axis=0), jnp.concatenate(lines[1:], axis=0)], axis=1
        )
        window = jnp.concatenate(split_high_low(window), axis=0)
        product = jnp.dot(window, band, preferred_element_type=jnp.float32)
        product = product[:rows] + product[rows:]
        product = product[:, :lanes] + product[:, lanes:]
        for part in range(parts):
            out_refs[part][z] = product[part * rows // parts:(part + 1) * rows // parts]
        return carry

    for b in range(blocks):
        large[b].wait()
        lax.fori_loop(b * per_block, (b + 1) * per_block, one_plane, 0, unroll=True)


def shear_x(volume, x_offsets, x_fracs, first_plane, classes, parts):
    plane_count, rows, lanes = volume.shape
    blocks = 2 if plane_count % 2 == 0 else 1
    return pl.pallas_call(
        functools.partial(shear_x_kernel, classes),
        out_shape=[
            jax.ShapeDtypeStruct((plane_count, rows // parts, lanes), jnp.float32)
        ] * parts,
        in_specs=[SMEM_SPEC] + [pl.BlockSpec(memory_space=pl.ANY)] * 3,
        out_specs=[VMEM_SPEC] * parts,
        scratch_shapes=[
            pltpu.VMEM(volume.shape, jnp.float32),
            pltpu.VMEM((plane_count, rows + 16, lanes), jnp.float32),
            pltpu.VMEM((plane_count, lanes), jnp.float32),
            pltpu.SMEM(x_offsets.shape, jnp.int32),
            pltpu.SMEM(x_fracs.shape, jnp.float32),
            pltpu.SemaphoreType.DMA((2,)),
            pltpu.SemaphoreType.DMA((blocks,)),
        ],
        compiler_params=pltpu.CompilerParams(vmem_limit_bytes=VMEM_LIMIT),
        name="shear_x",
    )(first_plane.reshape(1), x_offsets, x_fracs, volume)


def shear_z_kernel(
    plane_count, depth, place_ref, shift_ref, frac_ref, pair_ref, own_ref, other_ref, out_ref
):
    lanes = own_ref.shape[1]
    rows = own_ref.shape[0] // plane_count
    reach = plane_count + 2 * depth
    even = place_ref[0] % 2 == 0
    target = lax.broadcasted_iota(jnp.int32, (plane_count, reach), 0)
    column = lax.broadcasted_iota(jnp.int32, (plane_count, reach), 1)
    pair_start = jnp.where(even, plane_count, -depth)
    other_start = jnp.where(even, -depth, plane_count)
    source = jnp.where(
        column < depth,
        column + pair_start,
        jnp.where(
            column < depth + plane_count,
            column - depth,
            column - (depth + plane_count) + other_start,
        ),
    )
    mixing = tap_weight_in_kernel(source - target - shift_ref[0], frac_ref[0])
    mixing_high, mixing_low = split_high_low(mixing)
    mixing = jnp.concatenate(
        [
            jnp.concatenate([mixing_high, mixing_high], axis=1),
            jnp.concatenate([mixing_low, mixing_low], axis=1),
        ],
        axis=0,
    )

    def stack_of(row):
        return jnp.concatenate(
            [
                pair_ref[pl.ds(row, depth, stride=rows), :],
                own_ref[pl.ds(row, plane_count, stride=rows), :],
                other_ref[pl.ds(row, depth, stride=rows), :],
            ],
            axis=0,
        )

    chunks, _, width = out_ref.shape
    per_chunk = width // lanes
    pair = 2 if per_chunk % 2 == 0 else 1
    for chunk in range(chunks):
        for piece in range(per_chunk // pair):
            stack = jnp.concatenate(
                [stack_of((piece * pair + i) * chunks + chunk) for i in range(pair)], axis=1
            )
            stack = jnp.concatenate(split_high_low(stack), axis=0)
            product = jnp.dot(mixing, stack, preferred_element_type=jnp.float32)
            out_ref[chunk, :, piece * pair * lanes:(piece + 1) * pair * lanes] = (
                product[:plane_count] + product[plane_count:]
            )


def shear_z(own, pair, other, z_offsets, z_fracs, place, chunks):
    plane_count, rows, lanes = own.shape
    depth = pair.shape[0]
    return pl.pallas_call(
        functools.partial(shear_z_kernel, plane_count, depth),
        out_shape=jax.ShapeDtypeStruct((chunks, plane_count, rows * lanes // chunks), jnp.float32),
        in_specs=[SMEM_SPEC, SMEM_SPEC, SMEM_SPEC, VMEM_SPEC, VMEM_SPEC, VMEM_SPEC],
        out_specs=VMEM_SPEC,
        compiler_params=pltpu.CompilerParams(vmem_limit_bytes=VMEM_LIMIT),
        name="shear_z",
    )(
        place.reshape(1),
        z_offsets,
        z_fracs,
        pair.reshape(depth * rows, lanes),
        own.reshape(plane_count * rows, lanes),
        other.reshape(depth * rows, lanes),
    )


def shear_y_kernel(part, parts, shares, place_ref, slopes_ref, shifts_ref, fracs_ref, in_ref, *rest):
    last = part == parts - 1
    earlier = rest[:part] if last else ()
    rest = rest[len(earlier):]
    out_ref = rest[0]
    share_refs = rest[1:1 + shares] if last else ()
    totals_ref, taps_ref = rest[-2:]
    ny, plane_count, width = in_ref.shape
    total_planes = plane_count * shares
    tilts = slopes_ref.shape[0]
    span = ny // 4
    tiles = width // LANES
    tap_rows = taps_ref.shape[0]
    own = slice(part * width, (part + 1) * width)
    distance = lax.broadcasted_iota(jnp.int32, (tap_rows, width), 0) - (ny - 1)
    taps_ref[...] = tap_weight_in_kernel(distance - shifts_ref[:, own], fracs_ref[:, own])

    for tile in range(tiles):
        lanes = slice(tile * LANES, (tile + 1) * LANES)
        weights = [
            jnp.broadcast_to(taps_ref[d:d + 1, lanes], (8, LANES)) for d in range(2 * ny - 1)
        ]
        for block in range(plane_count // 8):
            planes = slice(block * 8, (block + 1) * 8)
            source = [in_ref[j, planes, lanes] for j in range(ny)]
            for i in range(ny):
                value = weights[ny - 1 - i] * source[0]
                for j in range(1, ny):
                    value = value + weights[j - i + ny - 1] * source[j]
                out_ref[i, planes, lanes] = value

    lifts = 2 * span + 1
    entry = lax.broadcasted_iota(jnp.int32, (lifts * tilts, plane_count), 0)
    plane = lax.broadcasted_iota(jnp.int32, (lifts * tilts, plane_count), 1)
    plane = plane + place_ref[0] * plane_count
    lift = entry // tilts - span
    tilt = entry - (lift + span) * tilts
    slope = jnp.zeros_like(tilt)
    for t in range(tilts):
        slope = jnp.where(tilt == t, slopes_ref[t], slope)
    numerator = slope * (2 * plane - total_planes) * ny
    floor_at = lift * (16 * total_planes)
    chosen = (numerator >= floor_at) & (numerator < floor_at + 16 * total_planes)
    chosen = jnp.where(chosen, 1.0, 0.0).astype(jnp.bfloat16)
    chosen = jnp.concatenate([chosen, chosen], axis=1)

    totals_ref[...] = jnp.zeros(totals_ref.shape, jnp.float32)
    for j in range(ny):
        sums = jnp.dot(
            chosen,
            jnp.concatenate(split_high_low(out_ref[j]), axis=0),
            preferred_element_type=jnp.float32,
        )
        for l in range(lifts):
            i = j - (l - span)
            if 0 <= i < ny:
                for tile in range(tiles):
                    row = (tile * ny + i) * tilts
                    totals_ref[row:row + tilts, :] += sums[
                        l * tilts:(l + 1) * tilts, tile * LANES:(tile + 1) * LANES
                    ]
    if not last:
        return
    per_share = tilts // shares
    for step, share_ref in enumerate(share_refs):
        tilt = (place_ref[0] ^ step) * per_share
        for u in range(per_share):
            for source, ref in enumerate((*earlier, totals_ref)):
                for tile in range(tiles):
                    column = source * width + tile * LANES
                    share_ref[u, :, column:column + LANES] = (
                        ref[pl.ds(tile * ny * tilts + tilt + u, ny, stride=tilts), :]
                        * total_planes ** (-0.5)
                    )


def shear_y(columns, y_offsets, y_fracs, slopes, place, part, parts, shares, earlier):
    ny, plane_count, width = columns.shape
    tilts = slopes.shape[0]
    last = part == parts - 1
    totals = (width // LANES * ny * tilts, LANES)
    out_shape = [jax.ShapeDtypeStruct(columns.shape, jnp.float32)]
    scratch = [pltpu.VMEM((2 * ny, width), jnp.float32)]
    if last:
        share = (tilts // shares, ny, width * parts)
        out_shape += [jax.ShapeDtypeStruct(share, jnp.float32)] * shares
        scratch = [pltpu.VMEM(totals, jnp.float32)] + scratch
    else:
        out_shape += [jax.ShapeDtypeStruct(totals, jnp.float32)]
    return pl.pallas_call(
        functools.partial(shear_y_kernel, part, parts, shares),
        out_shape=out_shape,
        in_specs=[SMEM_SPEC, SMEM_SPEC] + [VMEM_SPEC] * (3 + len(earlier)),
        out_specs=[VMEM_SPEC] * len(out_shape),
        scratch_shapes=scratch,
        compiler_params=pltpu.CompilerParams(vmem_limit_bytes=VMEM_LIMIT),
        name="shear_y",
    )(
        place.reshape(1),
        slopes,
        y_offsets.reshape(1, width * parts),
        y_fracs.reshape(1, width * parts),
        columns,
        *earlier,
    )


def finish_kernel(parts, *refs):
    landed_refs, share_refs = refs[:parts], refs[parts:-2]
    rotated_ref, projections_ref = refs[-2:]
    groups, plane_count, width = landed_refs[0].shape
    per_part = width // LANES
    per_group = per_part * parts
    rows = groups * per_group
    for part, landed_ref in enumerate(landed_refs):
        for group in range(groups):
            for tile in range(per_part):
                row = group * per_group + part * per_part + tile
                rotated_ref[pl.ds(row, plane_count, stride=rows), :] = landed_ref[
                    group, :, tile * LANES:(tile + 1) * LANES
                ]
    total = share_refs[0][...]
    for share_ref in share_refs[1:]:
        total = total + share_ref[...]
    projections_ref[...] = total


def finish(landed, shares):
    groups, plane_count, width = landed[0].shape
    rows = plane_count * groups * len(landed) * width // LANES
    return pl.pallas_call(
        functools.partial(finish_kernel, len(landed)),
        out_shape=(
            jax.ShapeDtypeStruct((rows, LANES), jnp.float32),
            jax.ShapeDtypeStruct(shares[0].shape, jnp.float32),
        ),
        in_specs=[VMEM_SPEC] * (len(landed) + len(shares)),
        out_specs=(VMEM_SPEC, VMEM_SPEC),
        compiler_params=pltpu.CompilerParams(vmem_limit_bytes=VMEM_LIMIT),
        name="finish",
    )(*landed, *shares)


def narrow_columns(columns, y_offsets, y_fracs, slopes, first_plane, total_planes):
    row_total, plane_count, col_local = columns.shape
    target_row = jnp.arange(row_total, dtype=jnp.int32)[:, None]
    source_row = jnp.arange(row_total, dtype=jnp.int32)[None, :]
    operator = tap_weight(
        (source_row - target_row)[None] - y_offsets[:, None, None], y_fracs[:, None, None]
    )
    rotated = jnp.einsum("cij,jzc->izc", operator, columns, precision=lax.Precision.HIGHEST)
    span = row_total // 4
    planes = first_plane + jnp.arange(plane_count, dtype=jnp.int32)
    padded = jnp.pad(rotated, ((span, span), (0, 0), (0, 0)))
    per_tilt = []
    for tilt in range(slopes.shape[0]):
        lifts = slopes[tilt] * (2 * planes - total_planes) * row_total // (16 * total_planes)
        moved = jax.vmap(
            lambda one_plane, lift: lax.dynamic_slice_in_dim(one_plane, span + lift, row_total, 0),
            in_axes=(1, 0),
        )(padded, lifts)
        per_tilt.append(jnp.sum(moved, axis=0))
    return rotated, jnp.stack(per_tilt) * total_planes ** (-0.5)


def exchange(value, axis):
    return lax.all_to_all(value, axis, split_axis=0, concat_axis=0, tiled=True)


def local(volume, x_offsets, x_fracs, z_offsets, z_fracs, y_offsets, y_fracs, slopes):
    depth = TAPS // 2 + OFFZ
    plane_count, row_local, width_all = volume.shape
    groups, shares = lax.axis_size("gy"), lax.axis_size("gz")
    assert row_local == 1 and width_all % LANES == 0
    rows = width_all // LANES
    col_local = width_all // groups
    total_planes = plane_count * shares
    place = lax.axis_index("gz").astype(jnp.int32)
    first_plane = place * plane_count
    wide = col_local % LANES == 0
    classes = col_local // LANES if wide else 1
    parts = PARTS if classes % PARTS == 0 else 1
    sheared = shear_x(
        volume.reshape(plane_count, rows, LANES), x_offsets, x_fracs, first_plane, classes, parts
    )
    spare = plane_count - depth
    pair_first = jnp.where(place % 2 == 0, spare, 0)
    swaps = [[], []]
    for i in range(shares - 1):
        swaps[i % 2] += [(i, i + 1), (i + 1, i)]
    mixed = []
    for value in sheared:
        pair = lax.ppermute(
            lax.dynamic_slice_in_dim(value, pair_first, depth, 0), "gz", swaps[0]
        )
        other = lax.ppermute(
            lax.dynamic_slice_in_dim(value, spare - pair_first, depth, 0), "gz", swaps[1]
        )
        mixed.append(
            shear_z(value, pair, other, z_offsets, z_fracs, place, groups if wide else rows)
        )
    if not wide:
        outgoing = jnp.moveaxis(mixed[0], 0, 1).reshape(plane_count, groups, col_local)
        columns = exchange(jnp.moveaxis(outgoing, 1, 0), "gy")
        rotated, tilted = narrow_columns(
            columns, y_offsets, y_fracs, slopes, first_plane, total_planes
        )
        projections = lax.psum_scatter(tilted, "gz", scatter_dimension=0, tiled=True)
        landed = exchange(rotated, "gy")
        rotated = jnp.moveaxis(landed, 0, 1).reshape(plane_count, row_local, width_all)
        return rotated, jnp.swapaxes(projections, 1, 2)
    columns = [exchange(value, "gy") for value in mixed]
    landed, totals = [], []
    for part in range(parts):
        rotated, *tilted = shear_y(
            columns[part], y_offsets, y_fracs, slopes, place, part, parts, shares,
            totals if part == parts - 1 else [],
        )
        landed.append(exchange(rotated, "gy"))
        totals += tilted
    shares_own = [tilted[0]] + [
        lax.ppermute(tilted[step], "gz", [(i, i ^ step) for i in range(shares)])
        for step in range(1, shares)
    ]
    rotated, projections = finish(landed, shares_own)
    return (
        rotated.reshape(plane_count, row_local, width_all),
        jnp.swapaxes(projections, 1, 2),
    )


def solution(mesh):
    return jax.shard_map(
        local,
        mesh=mesh,
        in_specs=(P("gz", "gy", None), P(), P(), P("gy"), P("gy"), P("gy"), P("gy"), P()),
        out_specs=(P("gz", "gy", None), P("gz", "gy", None)),
        check_vma=False,
    )
```

time: 74.7 us -> 60.2 us (0.81)
  blocking collectives: 40 us -> 14.7 us
  starting transfers between devices: 6.89 us -> 14.6 us
  waiting for transfers between devices: 11.2 us -> 18.4 us
  Pallas kernels: 11.5 us -> 7.63 us
    all_to_all x3 -> x1, blocking collectives: 40 us -> 14.7 us  [exchange(): return lax.all_to_all(value, axis, split_axis=0, concat_axis=0, tiled=True)]
    ppermute x2 -> x5, starting transfers between devices: 6.89 us -> 11 us  [the longest x1 5.88 us: local(): lax.ppermute(lax.dynamic_slice_in_dim(value, pair_first, depth, 0), 'gz',...]
    pallas_call x3, Pallas kernels: 10 us -> 6.08 us  [the longest x1 2.37 us: shear_x(): pl.pallas_call(functools.partial(shear_x_kernel, classes), out_shape=[jax...]
    ppermute x2 -> x5, waiting for transfers between devices: 11.2 us -> 15.1 us  [the longest x1 11.7 us: local(): lax.ppermute(lax.dynamic_slice_in_dim(value, pair_first, depth, 0), 'gz',...]
    all_to_all x0 -> x1, starting transfers between devices: none -> 3.54 us  [exchange(): return lax.all_to_all(value, axis, split_axis=0, concat_axis=0, tiled=True)]
    all_to_all x0 -> x1, waiting for transfers between devices: none -> 3.28 us  [exchange(): return lax.all_to_all(value, axis, split_axis=0, concat_axis=0, tiled=True)]
  transfers between devices with their start and end apart: 2 -> 6, of which waited for: 2 -> 4; matrix products, arithmetic and copies ran while one was open for 0% -> 0% of each run, Pallas kernels for 0% -> 0%
where the time goes in v2:
time: 60.2 us; the launch traced here: 59.8 us
  waiting for transfers between devices  18.4 us (31%)
  blocking collectives  14.7 us (24%)
  starting transfers between devices  14.6 us (24%)
  Pallas kernels  7.63 us (13%)
  local copies, waits for them, and re-layouts  2.54 us (4%)
  between operations  2.02 us (3%)
    all_to_all x1, blocking collectives, exchange(): return lax.all_to_all(value, axis, split_axis=0, concat_axis=0, tiled=True)  14.7 us
    ppermute x1, waiting for transfers between devices, local(): lax.ppermute(lax.dynamic_slice_in_dim(value, pair_first, depth, 0), 'gz',...  11.7 us
    ppermute x1, starting transfers between devices, local(): lax.ppermute(lax.dynamic_slice_in_dim(value, pair_first, depth, 0), 'gz',...  5.88 us
    ppermute x3, starting transfers between devices, local(): lax.ppermute(tilted[step], 'gz', [(i, i ^ step) for i in range(shares)])  4.45 us
    all_to_all x1, starting transfers between devices, exchange(): return lax.all_to_all(value, axis, split_axis=0, concat_axis=0, tiled=True)  3.54 us
    ppermute x3, waiting for transfers between devices, local(): lax.ppermute(tilted[step], 'gz', [(i, i ^ step) for i in range(shares)])  3.34 us
    all_to_all x1, waiting for transfers between devices, exchange(): return lax.all_to_all(value, axis, split_axis=0, concat_axis=0, tiled=True)  3.28 us
    unnamed x12, local copies, waits for them, and re-layouts  2.45 us
  transfers between devices with their start and end apart: 6, of which 4 were waited for; matrix products, arithmetic and copies ran while one was open for 0% of the time, Pallas kernels for 0%

profile of v2, /device:TPU:0, one launch (start us, length us, event | category | flops | bytes accessed | tf_op | source)
XLA Modules:
  0.0 59.8 jit_solution(8931796486483819995)
XLA Ops:
  0.6 0.0 copy-start.4
  0.7 0.0 copy-start.3
  0.7 0.7 %copy-done.4 = f32[160]{0:T(256)S(1)} copy-done((f32[160]{0:T(256)S(1)}, f32[160]{0:T(256)}, u32[]{:S(2)}) %copy-start.4) | copy-done | bytes 664
  1.3 0.0 copy-done.3
  1.3 0.0 copy-start
  1.3 1.1 %copy-done = f32[40,1,4096]{2,1,0:T(1,128)S(1)} copy-done((f32[40,1,4096]{2,1,0:T(1,128)S(1)}, f32[40,1,4096]{2,1,0:T(1,128)}, u32[]{:S(2)}) %copy-start) | copy-done | bytes 655384
  2.4 2.4 %shear_x.1 = f32[40,32,128]{2,1,0:T(8,128)S(1)} custom-call(s32[1]{0:T(128)} %bitcast.3.first_ref, s32[160]{0:T(256)S(1)} %copy-done.3, f32[160]{0:T(256)S(1)} %copy-done.4, f32[40,32,128]{2,1,0:T(8,128)S(1)} %bitcast.11), custom_call_target="tpu_custom_call" | custom-call | tf_op jit(solution)/shard_map/shear_x/pallas_call | solution.py:122
  4.8 0.1 constant_dynamic-slice_fusion
  4.9 0.7 %collective-permute-start.1 = (f32[36,32,128]{2,1,0:T(8,128)S(1)}, f32[36,32,128]{2,1,0:T(8,128)S(1)}, u32[]{:S(2)}, u32[]{:S(2)}) collective-permute-start(f32[36,32,128]{2,1,0:T(8,128)S(1)} %get-tuple-element.18), channel_id=1, source_target_pairs={{1,2},{2,1},{5,6},{6,5},{9,10},{10,9},{13,14},{14,13},{17,18},{18,... | collective-permute-start | bytes 1769480 | tf_op jit(solution)/shard_map/ppermute | solution.py:413
  5.6 5.9 %collective-permute-start = (f32[36,32,128]{2,1,0:T(8,128)S(1)}, f32[36,32,128]{2,1,0:T(8,128)S(1)}, u32[]{:S(2)}, u32[]{:S(2)}) collective-permute-start(f32[36,32,128]{2,1,0:T(8,128)S(1)} %get-tuple-element.19), channel_id=1, source_target_pairs={{0,1},{1,0},{2,3},{3,2},{4,5},{5,4},{6,7},{7,6},{8,9},{9,8},{10,11... | collective-permute-start | bytes 1769480 | tf_op jit(solution)/shard_map/ppermute | solution.py:410
  12.8 0.0 collective-permute-done.1
  12.8 11.7 %collective-permute-done = f32[36,32,128]{2,1,0:T(8,128)S(1)} collective-permute-done((f32[36,32,128]{2,1,0:T(8,128)S(1)}, f32[36,32,128]{2,1,0:T(8,128)S(1)}, u32[]{:S(2)}, u32[]{:S(2)}) %collective-permute-start) | collective-permute-done | bytes 589856 | tf_op jit(solution)/shard_map/ppermute | solution.py:410
  24.5 1.6 %shear_z.1 = f32[8,40,512]{2,1,0:T(8,128)S(1)} custom-call(s32[1]{0:T(128)} %bitcast.place_ref, s32[1]{0:T(128)S(6)} %copy.11.shift_ref, f32[1]{0:T(128)S(6)} %copy.12.frac_ref, f32[1152,128]{1,0:T(8,128)S(1)} %bitcast.13, f32[1280,128]{1,0:T(8,128)S(1)} %bitcast.10, f32[1152,128]{1,0:T(8,128)S(1)} %bitcast.12), custom_call_target="tpu_custom_call" | custom-call | tf_op jit(solution)/shard_map/shear_z/pallas_call | solution.py:201
  26.1 0.0 copy-start.2
  26.1 14.7 %all_to_all.10.in_ref = f32[8,40,512]{2,1,0:T(8,128)S(1)} all-to-all(f32[8,40,512]{2,1,0:T(8,128)S(1)} %shear_z.1), channel_id=1, replica_groups=mesh['gy'=8,'gz'=4] {'gy'}, dimensions={0} | all-to-all | bytes 1310720 | tf_op jit(solution)/shard_map/all_to_all | solution.py:384
  40.8 0.0 copy-start.1
  40.8 0.0 copy-start.5
  40.8 0.0 copy-done.2
  40.8 0.7 %copy-done.1 = s32[512]{0:T(512)S(1)} copy-done((s32[512]{0:T(512)S(1)}, s32[512]{0:T(512)}, u32[]{:S(2)}) %copy-start.1) | copy-done | bytes 2072
  41.4 0.0 copy-done.5
  41.4 2.3 %shear_y.1 = (f32[8,40,512]{2,1,0:T(8,128)}, f32[2,8,512]{2,1,0:T(8,128)S(1)}, f32[2,8,512]{2,1,0:T(8,128)S(1)}, f32[2,8,512]{2,1,0:T(8,128)S(1)}, f32[2,8,512]{2,1,0:T(8,128)S(1)}) custom-call(s32[1]{0:T(128)} %bitcast.place_ref, s32[8]{0:T(128)S(1)} %copy-done.5, s32[1,512]{1,0:T(1,128)S(1)} %bitcast.14, f32[1,512]{1,0:T(1,128)S(1)} %bitcast.15, ...), custom_call_target="tpu_custom_call" | custom-call | tf_op jit(solution)/shard_map/shear_y/pallas_call | solution.py:307
  43.7 3.5 %all-to-all-start.1 = ((f32[8,40,512]{2,1,0:T(8,128)}), f32[8,40,512]{2,1,0:T(8,128)S(1)}, u32[]{:S(2)}, u32[]{:S(2)}) async-start(f32[8,40,512]{2,1,0:T(8,128)} %get-tuple-element.9), calls=%async_computation.1 | async-start | bytes 1310720 | tf_op jit(solution)/shard_map/all_to_all | solution.py:384
  47.3 1.8 %collective-permute-start.2 = (f32[2,8,512]{2,1,0:T(8,128)S(1)}, f32[2,8,512]{2,1,0:T(8,128)S(1)}, u32[]{:S(2)}, u32[]{:S(2)}) collective-permute-start(f32[2,8,512]{2,1,0:T(8,128)S(1)} %get-tuple-element.11), channel_id=1, source_target_pairs={{0,1},{1,0},{2,3},{3,2},{4,5},{5,4},{6,7},{7,6},{8,9},{9,8},{10,11... | collective-permute-start | bytes 98312 | tf_op jit(solution)/shard_map/ppermute | solution.py:439
  49.1 0.2 collective-permute-start.3
  49.2 2.5 %collective-permute-start.4 = (f32[2,8,512]{2,1,0:T(8,128)S(1)}, f32[2,8,512]{2,1,0:T(8,128)S(1)}, u32[]{:S(2)}, u32[]{:S(2)}) collective-permute-start(f32[2,8,512]{2,1,0:T(8,128)S(1)} %get-tuple-element.13), channel_id=1, source_target_pairs={{0,3},{1,2},{2,1},{3,0},{4,7},{5,6},{6,5},{7,4},{8,11},{9,10},{10,... | collective-permute-start | bytes 98312 | tf_op jit(solution)/shard_map/ppermute | solution.py:439
  51.7 0.0 collective-permute-done.2.refs_2_
  51.7 2.7 %collective-permute-done.3.refs_3_ = f32[2,8,512]{2,1,0:T(8,128)S(1)} collective-permute-done((f32[2,8,512]{2,1,0:T(8,128)S(1)}, f32[2,8,512]{2,1,0:T(8,128)S(1)}, u32[]{:S(2)}, u32[]{:S(2)}) %collective-permute-start.3) | collective-permute-done | bytes 32800 | tf_op jit(solution)/shard_map/ppermute | solution.py:439
  54.4 0.6 %collective-permute-done.4.refs_4_ = f32[2,8,512]{2,1,0:T(8,128)S(1)} collective-permute-done((f32[2,8,512]{2,1,0:T(8,128)S(1)}, f32[2,8,512]{2,1,0:T(8,128)S(1)}, u32[]{:S(2)}, u32[]{:S(2)}) %collective-permute-start.4) | collective-permute-done | bytes 32800 | tf_op jit(solution)/shard_map/ppermute | solution.py:439
  55.0 3.3 %all-to-all-done.1.refs_0_ = f32[8,40,512]{2,1,0:T(8,128)S(1)} async-done(((f32[8,40,512]{2,1,0:T(8,128)}), f32[8,40,512]{2,1,0:T(8,128)S(1)}, u32[]{:S(2)}, u32[]{:S(2)}) %all-to-all-start.1) | async-done | bytes 655392 | tf_op jit(solution)/shard_map/all_to_all | solution.py:384
  58.3 1.5 %finish.1 = (f32[1280,128]{1,0:T(8,128)}, f32[2,8,512]{2,1,0:T(8,128)}) custom-call(f32[8,40,512]{2,1,0:T(8,128)S(1)} %all-to-all-done.1.refs_0_, f32[2,8,512]{2,1,0:T(8,128)S(1)} %get-tuple-element.10.refs_1_, f32[2,8,512]{2,1,0:T(8,128)S(1)} %collective-permute-done.2.refs_2_, f32[2,8,512]{2,1,0:T(8,128)S(1)} %collective-permute-done.3.refs_3_, ...), custom_call_target="tpu_custom_call" | custom-call | tf_op jit(solution)/shard_map/finish/pallas_call | solution.py:348
Async XLA Ops:
  0.6 0.7 %copy-start.4 = (f32[160]{0:T(256)S(1)}, f32[160]{0:T(256)}, u32[]{:S(2)}) copy-start(f32[160]{0:T(256)} %fracs_hbm.1) | copy-start | bytes 1924
  0.7 0.7 %copy-start.3 = (s32[160]{0:T(256)S(1)}, s32[160]{0:T(256)}, u32[]{:S(2)}) copy-start(s32[160]{0:T(256)} %shifts_hbm.1) | copy-start | bytes 1924
  1.3 1.1 %copy-start = (f32[40,1,4096]{2,1,0:T(1,128)S(1)}, f32[40,1,4096]{2,1,0:T(1,128)}, u32[]{:S(2)}) copy-start(f32[40,1,4096]{2,1,0:T(1,128)} %param.8) | copy-start | bytes 1966084
  4.9 7.9 %collective-permute-start.1 = (f32[36,32,128]{2,1,0:T(8,128)S(1)}, f32[36,32,128]{2,1,0:T(8,128)S(1)}, u32[]{:S(2)}, u32[]{:S(2)}) collective-permute-start(f32[36,32,128]{2,1,0:T(8,128)S(1)} %get-tuple-element.18), channel_id=1, source_target_pairs={{1,2},{2,1},{5,6},{6,5},{9,10},{10,9},{13,14},{14,13},{17,18},{18,... | collective-permute-start | bytes 1769480 | tf_op jit(solution)/shard_map/ppermute | solution.py:413
  5.6 18.9 %collective-permute-start = (f32[36,32,128]{2,1,0:T(8,128)S(1)}, f32[36,32,128]{2,1,0:T(8,128)S(1)}, u32[]{:S(2)}, u32[]{:S(2)}) collective-permute-start(f32[36,32,128]{2,1,0:T(8,128)S(1)} %get-tuple-element.19), channel_id=1, source_target_pairs={{0,1},{1,0},{2,3},{3,2},{4,5},{5,4},{6,7},{7,6},{8,9},{9,8},{10,11... | collective-permute-start | bytes 1769480 | tf_op jit(solution)/shard_map/ppermute | solution.py:410
  26.1 14.7 %copy-start.2 = (f32[512]{0:T(512)S(1)}, f32[512]{0:T(512)}, u32[]{:S(2)}) copy-start(f32[512]{0:T(512)} %param.14) | copy-start | bytes 6148
  40.8 0.7 %copy-start.1 = (s32[512]{0:T(512)S(1)}, s32[512]{0:T(512)}, u32[]{:S(2)}) copy-start(s32[512]{0:T(512)} %param.13) | copy-start | bytes 6148
  40.8 0.7 %copy-start.5 = (s32[8]{0:T(128)S(1)}, s32[8]{0:T(128)}, u32[]{:S(2)}) copy-start(s32[8]{0:T(128)} %slopes_ref.1) | copy-start | bytes 100
  43.7 14.6 %all-to-all-start.1 = ((f32[8,40,512]{2,1,0:T(8,128)}), f32[8,40,512]{2,1,0:T(8,128)S(1)}, u32[]{:S(2)}, u32[]{:S(2)}) async-start(f32[8,40,512]{2,1,0:T(8,128)} %get-tuple-element.9), calls=%async_computation.1 | async-start | bytes 1310720 | tf_op jit(solution)/shard_map/all_to_all | solution.py:384
  47.3 4.5 %collective-permute-start.2 = (f32[2,8,512]{2,1,0:T(8,128)S(1)}, f32[2,8,512]{2,1,0:T(8,128)S(1)}, u32[]{:S(2)}, u32[]{:S(2)}) collective-permute-start(f32[2,8,512]{2,1,0:T(8,128)S(1)} %get-tuple-element.11), channel_id=1, source_target_pairs={{0,1},{1,0},{2,3},{3,2},{4,5},{5,4},{6,7},{7,6},{8,9},{9,8},{10,11... | collective-permute-start | bytes 98312 | tf_op jit(solution)/shard_map/ppermute | solution.py:439
  49.1 5.4 %collective-permute-start.3 = (f32[2,8,512]{2,1,0:T(8,128)S(1)}, f32[2,8,512]{2,1,0:T(8,128)S(1)}, u32[]{:S(2)}, u32[]{:S(2)}) collective-permute-start(f32[2,8,512]{2,1,0:T(8,128)S(1)} %get-tuple-element.12), channel_id=1, source_target_pairs={{0,2},{1,3},{2,0},{3,1},{4,6},{5,7},{6,4},{7,5},{8,10},{9,11},{10,... | collective-permute-start | bytes 98312 | tf_op jit(solution)/shard_map/ppermute | solution.py:439
  49.2 5.8 %collective-permute-start.4 = (f32[2,8,512]{2,1,0:T(8,128)S(1)}, f32[2,8,512]{2,1,0:T(8,128)S(1)}, u32[]{:S(2)}, u32[]{:S(2)}) collective-permute-start(f32[2,8,512]{2,1,0:T(8,128)S(1)} %get-tuple-element.13), channel_id=1, source_target_pairs={{0,3},{1,2},{2,1},{3,0},{4,7},{5,6},{6,5},{7,4},{8,11},{9,10},{10,... | collective-permute-start | bytes 98312 | tf_op jit(solution)/shard_map/ppermute | solution.py:439

commit v3 on v0

--- a/solution.py
+++ b/solution.py
@@ -1,11 +1,441 @@
+import functools
+
 import jax
 import jax.numpy as jnp
 from jax import lax
+from jax.experimental import pallas as pl
+from jax.experimental.pallas import tpu as pltpu
 from jax.sharding import PartitionSpec as P
 
 TAPS = 64
 OFFX = 64
 OFFZ = 4
+LANES = 128
+BELOW = TAPS // 2 - 1
+VMEM_LIMIT = 32 * 1024 * 1024
+
+SMEM_SPEC = pl.BlockSpec(memory_space=pltpu.SMEM)
+VMEM_SPEC = pl.BlockSpec(memory_space=pltpu.VMEM)
+
+
+def tap_weight(offset, fraction):
+    moved = offset.astype(jnp.float32) - fraction
+    inside = (offset >= 1 - TAPS // 2) & (offset <= TAPS // 2)
+    value = jnp.sinc(moved) * (0.5 + 0.5 * jnp.cos(jnp.pi * moved / (TAPS // 2 + 1)))
+    return jnp.where(inside, value, jnp.zeros_like(value))
+
+
+def tap_weight_in_kernel(offset, fraction):
+    moved = offset.astype(jnp.float32) - fraction
+    inside = (offset >= 1 - TAPS // 2) & (offset <= TAPS // 2)
+    angle = jnp.pi * moved
+    at_zero = moved == 0.0
+    sinc = jnp.where(at_zero, 1.0, jnp.sin(angle) / jnp.where(at_zero, 1.0, angle))
+    window = 0.5 + 0.5 * jnp.cos(angle / (TAPS // 2 + 1))
+    return jnp.where(inside, sinc * window, 0.0)
+
+
+def split_high_low(value):
+    high = value.astype(jnp.bfloat16)
+    low = (value - high.astype(jnp.float32)).astype(jnp.bfloat16)
+    return high, low
+
+
+def shear_x_kernel(
+    classes, first_ref, side_ref, shifts_hbm, fracs_hbm, planes_hbm, *rest
+):
+    out_refs = rest[:-8]
+    planes_ref, margin_ref, base_ref, lines_ref, shifts_ref, fracs_ref, small_sem, plane_sem = (
+        rest[-8:]
+    )
+    plane_count, rows, lanes = planes_ref.shape
+    per_class = rows // classes
+    before, after = 8, margin_ref.shape[1] - rows - 8
+    blocks = plane_sem.shape[0]
+    per_block = plane_count // blocks
+    small = [
+        pltpu.make_async_copy(shifts_hbm, shifts_ref, small_sem.at[0]),
+        pltpu.make_async_copy(fracs_hbm, fracs_ref, small_sem.at[1]),
+    ]
+    large = [
+        pltpu.make_async_copy(
+            planes_hbm.at[b * per_block:(b + 1) * per_block],
+            planes_ref.at[b * per_block:(b + 1) * per_block],
+            plane_sem.at[b],
+        )
+        for b in range(blocks)
+    ]
+    for copy in small + large:
+        copy.start()
+    line = lax.broadcasted_iota(jnp.int32, (lanes, lanes), 0)
+    lane = lax.broadcasted_iota(jnp.int32, (lanes, lanes), 1)
+    own_side = lane <= line
+    tap = (lanes - lax.broadcasted_iota(jnp.int32, (plane_count, lanes), 1)) % lanes
+    lane_of_row = lax.broadcasted_iota(jnp.int32, (per_class, lanes), 1)
+    zeros = jnp.zeros((8, lanes), jnp.float32)
+    first = first_ref[0]
+    first_lines = (2 - 2 * side_ref[0], 2 * side_ref[0])
+    for copy in small:
+        copy.wait()
+    for z in range(plane_count):
+        base_ref[z:z + 1, :] = jnp.full((1, lanes), fracs_ref[first + z], jnp.float32)
+    base_ref[...] = tap_weight_in_kernel(tap - BELOW, base_ref[...])
+
+    def one_plane(z, carry):
+        margin_ref[z, 0:before, :] = zeros
+        margin_ref[z, before:before + rows, :] = planes_ref[z]
+        margin_ref[z, before + rows:before + rows + after, :] = zeros
+        spread = pltpu.roll(
+            jnp.broadcast_to(base_ref[pl.ds(z, 1), :], (lanes, lanes)),
+            0, 1, stride=1, stride_axis=0,
+        )
+        own = jnp.where(own_side, spread, 0.0)
+        band = jnp.concatenate([own, spread - own], axis=0)
+        band = jnp.concatenate(split_high_low(band), axis=1)
+        start = shifts_ref[first + z] - BELOW + before * lanes
+        top = start // lanes
+        back = lanes - (start - top * lanes)
+        keep = lane_of_row < back
+        turned = [
+            pltpu.roll(margin_ref[z, pl.ds(top + i, per_class, stride=classes), :], back, 1)
+            for i in range(classes + 2)
+        ]
+        lines = [jnp.where(keep, turned[i], turned[i + 1]) for i in range(classes + 1)]
+        window = jnp.concatenate(
+            [jnp.concatenate(lines[:-1], axis=0), jnp.concatenate(lines[1:], axis=0)], axis=1
+        )
+        window = jnp.concatenate(split_high_low(window), axis=0)
+        product = jnp.dot(window, band, preferred_element_type=jnp.float32)
+        product = product[:rows] + product[rows:]
+        product = product[:, :lanes] + product[:, lanes:]
+        if len(out_refs) == 1:
+            out_refs[0][z] = product
+            return carry
+        lines_ref[z] = product
+        quarter = rows // 4
+        for out_ref, first_line in zip(out_refs, first_lines):
+            for core in range(2):
+                out_ref[z, core * quarter:(core + 1) * quarter, :] = lines_ref[
+                    z, pl.ds(first_line + core, quarter, stride=4), :
+                ]
+        return carry
+
+    for b in range(blocks):
+        large[b].wait()
+        lax.fori_loop(b * per_block, (b + 1) * per_block, one_plane, 0, unroll=True)
+
+
+def shear_x(volume, x_offsets, x_fracs, first_plane, side, classes, parts):
+    plane_count, rows, lanes = volume.shape
+    blocks = 2 if plane_count % 2 == 0 else 1
+    return pl.pallas_call(
+        functools.partial(shear_x_kernel, classes),
+        out_shape=[
+            jax.ShapeDtypeStruct((plane_count, rows // parts, lanes), jnp.float32)
+        ] * parts,
+        in_specs=[SMEM_SPEC] * 2 + [pl.BlockSpec(memory_space=pltpu.HBM)] * 3,
+        out_specs=[VMEM_SPEC] * parts,
+        scratch_shapes=[
+            pltpu.VMEM(volume.shape, jnp.float32),
+            pltpu.VMEM((plane_count, rows + 16, lanes), jnp.float32),
+            pltpu.VMEM((plane_count, lanes), jnp.float32),
+            pltpu.VMEM(volume.shape, jnp.float32),
+            pltpu.SMEM(x_offsets.shape, jnp.int32),
+            pltpu.SMEM(x_fracs.shape, jnp.float32),
+            pltpu.SemaphoreType.DMA((2,)),
+            pltpu.SemaphoreType.DMA((blocks,)),
+        ],
+        compiler_params=pltpu.CompilerParams(vmem_limit_bytes=VMEM_LIMIT),
+        name="shear_x",
+    )(
+        first_plane.reshape(1),
+        side.reshape(1),
+        *(pltpu.with_memory_space_constraint(v, pltpu.HBM) for v in (x_offsets, x_fracs, volume)),
+    )
+
+
+def weights_kernel(
+    plane_count, depth, ny, shares, place_ref, shift_ref, frac_ref, slopes_ref, shifts_ref,
+    fracs_ref, mixing_ref, taps_ref, chosen_ref,
+):
+    reach = plane_count + 2 * depth
+    even = place_ref[0] % 2 == 0
+    target = lax.broadcasted_iota(jnp.int32, (plane_count, reach), 0)
+    column = lax.broadcasted_iota(jnp.int32, (plane_count, reach), 1)
+    pair_start = jnp.where(even, plane_count, -depth)
+    other_start = jnp.where(even, -depth, plane_count)
+    source = jnp.where(
+        column < depth,
+        column + pair_start,
+        jnp.where(
+            column < depth + plane_count,
+            column - depth,
+            column - (depth + plane_count) + other_start,
+        ),
+    )
+    mixing_ref[...] = tap_weight_in_kernel(source - target - shift_ref[0], frac_ref[0])
+    lanes = taps_ref.shape[1]
+    distance = lax.broadcasted_iota(jnp.int32, (2 * ny, lanes), 0) - (ny - 1)
+    for tile in range(shifts_ref.shape[1] // lanes):
+        part = slice(tile * lanes, (tile + 1) * lanes)
+        taps_ref[tile * 2 * ny:(tile + 1) * 2 * ny, :] = tap_weight_in_kernel(
+            distance - shifts_ref[:, part], fracs_ref[:, part]
+        )
+    total_planes = plane_count * shares
+    tilts = slopes_ref.shape[0]
+    span = ny // 4
+    entry = lax.broadcasted_iota(jnp.int32, chosen_ref.shape, 0)
+    plane = lax.broadcasted_iota(jnp.int32, chosen_ref.shape, 1) + place_ref[0] * plane_count
+    lift = entry // tilts - span
+    tilt = entry - (lift + span) * tilts
+    slope = jnp.zeros_like(tilt)
+    for t in range(tilts):
+        slope = jnp.where(tilt == t, slopes_ref[t], slope)
+    numerator = slope * (2 * plane - total_planes) * ny
+    floor_at = lift * (16 * total_planes)
+    chosen = (numerator >= floor_at) & (numerator < floor_at + 16 * total_planes)
+    chosen_ref[...] = jnp.where(chosen, 1.0, 0.0)
+
+
+def weights(
+    place, z_offsets, z_fracs, slopes, y_offsets, y_fracs, plane_count, depth, ny, shares
+):
+    width = y_offsets.shape[0]
+    lifts = 2 * (ny // 4) + 1
+    return pl.pallas_call(
+        functools.partial(weights_kernel, plane_count, depth, ny, shares),
+        out_shape=(
+            jax.ShapeDtypeStruct((plane_count, plane_count + 2 * depth), jnp.float32),
+            jax.ShapeDtypeStruct((width // LANES * 2 * ny, LANES), jnp.float32),
+            jax.ShapeDtypeStruct((lifts * slopes.shape[0], plane_count), jnp.float32),
+        ),
+        in_specs=[SMEM_SPEC] * 4 + [VMEM_SPEC] * 2,
+        out_specs=(VMEM_SPEC, VMEM_SPEC, VMEM_SPEC),
+        compiler_params=pltpu.CompilerParams(vmem_limit_bytes=VMEM_LIMIT),
+        name="weights",
+    )(
+        place.reshape(1), z_offsets, z_fracs, slopes,
+        y_offsets.reshape(1, width), y_fracs.reshape(1, width),
+    )
+
+
+def shear_z_kernel(
+    plane_count, depth, chips, row_ref, mixing_ref, pair_ref, own_ref, other_ref, *outs
+):
+    lanes = own_ref.shape[1]
+    rows = own_ref.shape[0] // plane_count
+    half = chips // 2
+    tiles = rows // chips
+    pair = 2 if tiles % 2 == 0 else 1
+    high, low = split_high_low(mixing_ref[...])
+    mixing = jnp.concatenate(
+        [jnp.concatenate([high, high], axis=1), jnp.concatenate([low, low], axis=1)], axis=0
+    )
+    core, chip_pair = row_ref[0] % 2, row_ref[0] // 4
+    for index, out_ref in enumerate(outs):
+        first = (core ^ (index % 2)) * (rows // 2) + (chip_pair ^ (index // 2))
+        for tile in range(0, tiles, pair):
+            columns = []
+            for i in range(tile, tile + pair):
+                row = first + i * half
+                columns.append(
+                    jnp.concatenate(
+                        [
+                            pair_ref[pl.ds(row, depth, stride=rows), :],
+                            own_ref[pl.ds(row, plane_count, stride=rows), :],
+                            other_ref[pl.ds(row, depth, stride=rows), :],
+                        ],
+                        axis=0,
+                    )
+                )
+            stack = jnp.concatenate(columns, axis=1)
+            stack = jnp.concatenate(split_high_low(stack), axis=0)
+            product = jnp.dot(mixing, stack, preferred_element_type=jnp.float32)
+            out_ref[:, tile * lanes:(tile + pair) * lanes] = (
+                product[:plane_count] + product[plane_count:]
+            )
+
+
+def shear_z(row, mixing, pair, own, other, chips):
+    plane_count, rows, lanes = own.shape
+    depth = pair.shape[0]
+    width = rows * lanes // chips
+    return pl.pallas_call(
+        functools.partial(shear_z_kernel, plane_count, depth, chips),
+        out_shape=[jax.ShapeDtypeStruct((plane_count, width), jnp.float32)] * chips,
+        in_specs=[SMEM_SPEC] + [VMEM_SPEC] * 4,
+        out_specs=[VMEM_SPEC] * chips,
+        compiler_params=pltpu.CompilerParams(vmem_limit_bytes=VMEM_LIMIT),
+        name="shear_z",
+    )(row.reshape(1), mixing, *(value.reshape(-1, lanes) for value in (pair, own, other)))
+
+
+def shear_y_kernel(ny, row_ref, taps_ref, *refs):
+    in_refs, own_refs, out_refs = refs[:ny][::-1], refs[ny:ny + 2], refs[ny + 2:]
+    plane_count, width = in_refs[0].shape
+    row = row_ref[0]
+    for tile in range(width // LANES):
+        lanes = slice(tile * LANES, (tile + 1) * LANES)
+        first = tile * 2 * ny + ny - 1
+        for target in range(ny):
+            weight = [
+                jnp.broadcast_to(
+                    taps_ref[pl.ds(first + (row ^ source) - (row ^ target), 1), :], (8, LANES)
+                )
+                for source in range(ny)
+            ]
+            for block in range(plane_count // 8):
+                planes = slice(block * 8, (block + 1) * 8)
+                value = weight[0] * in_refs[0][planes, lanes]
+                for source in range(1, ny):
+                    value = value + weight[source] * in_refs[source][planes, lanes]
+                if target < 2:
+                    own_refs[target][planes, lanes] = value
+                else:
+                    out_refs[target // 2 - 1][target % 2, planes, lanes] = value
+
+
+def shear_y(row, taps, columns):
+    ny = len(columns)
+    shape = columns[0].shape
+    out_shape = [jax.ShapeDtypeStruct(shape, jnp.float32)] * 2
+    out_shape += [jax.ShapeDtypeStruct((2, *shape), jnp.float32)] * (ny // 2 - 1)
+    return pl.pallas_call(
+        functools.partial(shear_y_kernel, ny),
+        out_shape=out_shape,
+        in_specs=[SMEM_SPEC] + [VMEM_SPEC] * (1 + ny),
+        out_specs=[VMEM_SPEC] * len(out_shape),
+        compiler_params=pltpu.CompilerParams(vmem_limit_bytes=VMEM_LIMIT),
+        name="shear_y",
+    )(row.reshape(1), taps, *columns[::-1])
+
+
+def collect_kernel(*refs):
+    out_ref = refs[-1]
+    for index, ref in enumerate(refs[:-1]):
+        out_ref[index] = ref[1]
+
+
+def collect(landed):
+    return pl.pallas_call(
+        collect_kernel,
+        out_shape=jax.ShapeDtypeStruct((len(landed), *landed[0].shape[1:]), jnp.float32),
+        in_specs=[VMEM_SPEC] * len(landed),
+        out_specs=VMEM_SPEC,
+        compiler_params=pltpu.CompilerParams(vmem_limit_bytes=VMEM_LIMIT),
+        name="collect",
+    )(*landed)
+
+
+def project_kernel(chips, tilts, place_ref, row_ref, chosen_ref, *refs):
+    in_refs, share_refs, totals_ref = refs[:chips + 1], refs[chips + 1:-1], refs[-1]
+    ny, shares = 2 * chips, len(share_refs)
+    plane_count, width = in_refs[0].shape
+    total_planes = plane_count * shares
+    span = ny // 4
+    tiles = width // LANES
+    lifts = 2 * span + 1
+    chosen = chosen_ref[...].astype(jnp.bfloat16)
+    chosen = jnp.concatenate([chosen, chosen], axis=1)
+
+    per_tile = (ny + 2 * span) * tilts
+    totals_ref[...] = jnp.zeros(totals_ref.shape, jnp.float32)
+    for source in range(ny):
+        if source < 2:
+            value = in_refs[source][...]
+        else:
+            value = in_refs[source // 2 + 1][source % 2]
+        sums = jnp.dot(
+            chosen,
+            jnp.concatenate(split_high_low(value), axis=0),
+            preferred_element_type=jnp.float32,
+        )
+        row = row_ref[0] ^ source
+        for l in range(lifts):
+            for tile in range(tiles):
+                start = pl.multiple_of(tile * per_tile + (row + 2 * span - l) * tilts, tilts)
+                totals_ref[pl.ds(start, tilts), :] += sums[
+                    l * tilts:(l + 1) * tilts, tile * LANES:(tile + 1) * LANES
+                ]
+    per_share = tilts // shares
+    for step, share_ref in enumerate(share_refs):
+        tilt = (place_ref[0] ^ step) * per_share
+        for u in range(per_share):
+            for tile in range(tiles):
+                share_ref[u, :, tile * LANES:(tile + 1) * LANES] = (
+                    totals_ref[
+                        pl.ds(tile * per_tile + span * tilts + tilt + u, ny, stride=tilts), :
+                    ]
+                    * total_planes ** (-0.5)
+                )
+
+
+def project(place, row, chosen, rotated, shares):
+    chips = len(rotated) - 1
+    ny = 2 * chips
+    tilts = chosen.shape[0] // (2 * (ny // 4) + 1)
+    width = rotated[0].shape[1]
+    share = jax.ShapeDtypeStruct((tilts // shares, ny, width), jnp.float32)
+    totals = (width // LANES * (ny + 2 * (ny // 4)) * tilts, LANES)
+    return pl.pallas_call(
+        functools.partial(project_kernel, chips, tilts),
+        out_shape=[share] * shares,
+        in_specs=[SMEM_SPEC] * 2 + [VMEM_SPEC] * (1 + len(rotated)),
+        out_specs=[VMEM_SPEC] * shares,
+        scratch_shapes=[pltpu.VMEM(totals, jnp.float32)],
+        compiler_params=pltpu.CompilerParams(vmem_limit_bytes=VMEM_LIMIT),
+        name="project",
+    )(place.reshape(1), row.reshape(1), chosen, *rotated)
+
+
+def finish_kernel(slots, row_ref, *refs):
+    rotated_ref, sources = refs[-1], refs[:len(slots)]
+    rows = rotated_ref.shape[0] // sources[0].shape[-2]
+    for ref, (slot, index) in zip(sources, slots):
+        plane_count, width = ref.shape[-2:]
+        per_group = width // LANES
+        start = (row_ref[0] ^ slot) * per_group
+        source = ref if index is None else ref.at[index]
+        for tile in range(per_group):
+            rotated_ref[pl.ds(start + tile, plane_count, stride=rows), :] = source[
+                :, tile * LANES:(tile + 1) * LANES
+            ]
+
+
+def finish(row, own, early, late, landed):
+    chips = len(landed) + 1
+    plane_count, width = own.shape
+    slots = [(0, None), (1, None)]
+    slots += [(2 * step, 0) for step in range(1, chips)]
+    slots += [(2 * step + 1, step - 1) for step in range(1, chips)]
+    return pl.pallas_call(
+        functools.partial(finish_kernel, slots),
+        out_shape=jax.ShapeDtypeStruct(
+            (plane_count * 2 * chips * width // LANES, LANES), jnp.float32
+        ),
+        in_specs=[SMEM_SPEC] + [VMEM_SPEC] * len(slots),
+        out_specs=VMEM_SPEC,
+        compiler_params=pltpu.CompilerParams(vmem_limit_bytes=VMEM_LIMIT),
+        name="finish",
+    )(row.reshape(1), own, early, *landed, *([late] * (chips - 1)))
+
+
+def add_kernel(*refs):
+    total = refs[0][...]
+    for ref in refs[1:-1]:
+        total = total + ref[...]
+    refs[-1][...] = total
+
+
+def add(shares):
+    return pl.pallas_call(
+        add_kernel,
+        out_shape=jax.ShapeDtypeStruct(shares[0].shape, jnp.float32),
+        in_specs=[VMEM_SPEC] * len(shares),
+        out_specs=VMEM_SPEC,
+        compiler_params=pltpu.CompilerParams(vmem_limit_bytes=VMEM_LIMIT),
+        name="add_shares",
+    )(*shares)
 
 
 def with_halo(value, sides, width):
@@ -21,45 +451,11 @@
     return value
 
 
-def tap_weight(offset, fraction):
-    moved = offset.astype(jnp.float32) - fraction
-    inside = (offset >= 1 - TAPS // 2) & (offset <= TAPS // 2)
-    value = jnp.sinc(moved) * (0.5 + 0.5 * jnp.cos(jnp.pi * moved / (TAPS // 2 + 1)))
-    return jnp.where(inside, value, jnp.zeros_like(value))
-
-
-def shear_lines(planes, shifts, fractions):
-    plane_total, row_total, line_length = planes.shape
-    tile_width = 128
-    margin = OFFX + tile_width
-    padded = jnp.pad(planes, ((0, 0), (0, 0), (margin, margin)))
-    starts = margin + shifts - (TAPS // 2 - 1)
-    spans = jax.vmap(
-        lambda one_plane, first_index: lax.dynamic_slice_in_dim(
-            one_plane, first_index, line_length + tile_width, 1
-        )
-    )(padded, starts)
-    tile_count = line_length // tile_width
-    pieces = spans.reshape(plane_total, row_total, tile_count + 1, tile_width)
-    windows = jnp.concatenate([pieces[:, :, :-1], pieces[:, :, 1:]], axis=3)
-    inner_index = jnp.arange(2 * tile_width, dtype=jnp.int32)[:, None]
-    outer_index = jnp.arange(tile_width, dtype=jnp.int32)[None, :]
-    band_matrix = tap_weight(
-        (inner_index - outer_index - (TAPS // 2 - 1))[None], fractions[:, None, None]
-    )
-    sheared = jnp.einsum("prbj,pji->prbi", windows, band_matrix, precision=lax.Precision.HIGHEST)
-    return sheared.reshape(plane_total, row_total, line_length)
-
-
-def local(volume, x_offsets, x_fracs, z_offsets, z_fracs, y_offsets, y_fracs, slopes):
+def narrow_local(sheared_x, first_plane, z_offsets, z_fracs, y_offsets, y_fracs, slopes):
     depth = TAPS // 2 + OFFZ
-    plane_count, row_local, width_all = volume.shape
+    plane_count, row_local, width_all = sheared_x.shape
     groups = lax.axis_size("gy")
     col_local = width_all // groups
-    first_plane = lax.axis_index("gz") * plane_count
-    plane_shifts = lax.dynamic_slice_in_dim(x_offsets, first_plane, plane_count)
-    plane_fracs = lax.dynamic_slice_in_dim(x_fracs, first_plane, plane_count)
-    sheared_x = shear_lines(volume, plane_shifts, plane_fracs)
     extended = with_halo(sheared_x, (("gz", 0),), depth)
     plane_index = jnp.arange(plane_count, dtype=jnp.int32)[:, None]
     source_index = jnp.arange(plane_count + 2 * depth, dtype=jnp.int32)[None, :]
@@ -111,6 +507,65 @@
     return (rotated, projections)
 
 
+def swap(value, axis, step):
+    return lax.ppermute(value, axis, [(i, i ^ step) for i in range(lax.axis_size(axis))])
+
+
+def local(volume, x_offsets, x_fracs, z_offsets, z_fracs, y_offsets, y_fracs, slopes):
+    depth = TAPS // 2 + OFFZ
+    plane_count, row_local, width_all = volume.shape
+    groups, shares = lax.axis_size("gy"), lax.axis_size("gz")
+    assert row_local == 1 and width_all % LANES == 0
+    rows = width_all // LANES
+    col_local = width_all // groups
+    place = lax.axis_index("gz").astype(jnp.int32)
+    row = lax.axis_index("gy").astype(jnp.int32)
+    first_plane = place * plane_count
+    chips = groups // 2
+    wide = col_local % LANES == 0 and col_local > LANES and chips % 2 == 0
+    sheared = shear_x(
+        volume.reshape(plane_count, rows, LANES), x_offsets, x_fracs, first_plane, row // 2 % 2,
+        col_local // LANES if wide else 1, 2 if wide else 1,
+    )
+    if not wide:
+        return narrow_local(
+            sheared[0].reshape(volume.shape), first_plane, z_offsets, z_fracs, y_offsets, y_fracs,
+            slopes,
+        )
+    mixing, taps, chosen = weights(
+        place, z_offsets, z_fracs, slopes, y_offsets, y_fracs, plane_count, depth, groups, shares
+    )
+    spare = plane_count - depth
+    pair_first = jnp.where(place % 2 == 0, spare, 0)
+    ends = [[], []]
+    for i in range(shares - 1):
+        ends[i % 2] += [(i, i + 1), (i + 1, i)]
+    columns = [None] * groups
+    for half, value in zip((1, 0), sheared):
+        pair, other = (
+            lax.ppermute(lax.dynamic_slice_in_dim(value, first, depth, 0), "gz", ends[parity])
+            for parity, first in ((0, pair_first), (1, spare - pair_first))
+        )
+        mixed = shear_z(row, mixing, pair, value, other, chips)
+        mixing, *mixed = lax.optimization_barrier((mixing, *mixed))
+        for index in reversed(range(chips)):
+            step = 2 * (2 * (index // 2) + half) + index % 2
+            columns[step] = swap(mixed[index], "gy", step) if step else mixed[index]
+    own, cross, *rotated = shear_y(row, taps, columns)
+    landed = [swap(value, "gy", 2 * step + 2) for step, value in enumerate(rotated)]
+    early = swap(cross, "gy", 1)
+    tilted = project(place, row, chosen, (own, cross, *rotated), shares)
+    tilted = [tilted[0]] + [swap(tilted[step], "gz", step) for step in range(1, shares)]
+    tilted, landed = lax.optimization_barrier((tilted, landed[::-1]))
+    landed = landed[::-1]
+    late = swap(collect(landed), "gy", 1)
+    rotated = finish(row, own, early, late, landed)
+    return (
+        rotated.reshape(plane_count, row_local, width_all),
+        jnp.swapaxes(add(tilted), 1, 2),
+    )
+
+
 def solution(mesh):
     return jax.shard_map(
         local,

time: 249 us -> 47.5 us (0.19); the launches traced: 245 us -> 47.3 us
  local copies, waits for them, and re-layouts: 128 us -> 0.77 us
  matrix products: 37.9 us -> 0 us
  waiting for transfers between devices: 30.7 us -> 11.6 us
  other arithmetic: 17.5 us -> 0 us
  between operations: 16.1 us -> 2.1 us
  starting transfers between devices: 13.8 us -> 25.3 us
  Pallas kernels: 0 us -> 7.51 us
    gather x128 -> x0, local copies, waits for them, and re-layouts: 101 us -> none
    dot_general x3 -> x0, matrix products: 37.9 us -> none  [the longest x1 27.7 us: shear_lines(): jnp.einsum('prbj,pji->prbi', windows, band_matrix, precision=lax.Precisio...]
    ppermute x2 -> x19, starting transfers between devices: 6.24 us -> 25.3 us  [the longest x15 16.3 us: swap(): lax.ppermute(value, axis, [(i, i ^ step) for i in range(lax.axis_size(axi...]
    all_to_all x2 -> x0, waiting for transfers between devices: 12.4 us -> none  [the longest x1 10.3 us: local(): lax.all_to_all(returning, 'gy', split_axis=0, concat_axis=1, tiled=True)]
    reshape x4 -> x0, local copies, waits for them, and re-layouts: 7.93 us -> none  [the longest x1 3.14 us: local(): jnp.transpose(returning, (2, 3, 1, 0))]
    all_to_all x2 -> x0, starting transfers between devices: 7.55 us -> none  [the longest x1 4 us: local(): lax.all_to_all(outgoing, 'gy', split_axis=0, concat_axis=1, tiled=True)]
    pallas_call x0 -> x9, Pallas kernels: none -> 7.51 us  [the longest x1 2.7 us: shear_x(): pl.pallas_call(functools.partial(shear_x_kernel, classes), out_shape=[jax...]
    gather x6 -> x0, other arithmetic: 7.08 us -> none  [the longest x4 5.47 us: local(): lax.dynamic_slice_in_dim(one_plane, span_pad + lift_one, row_total, 1)]
  transfers between devices with their start and end apart: 5 -> 19, of which waited for: 5 -> 10; matrix products, arithmetic and copies ran while one was open for 7% -> 0% of each run, Pallas kernels for 0% -> 6%
where the time goes in v3:
time: 47.5 us; the launch traced here: 47.3 us
  starting transfers between devices  25.3 us (53%)
  waiting for transfers between devices  11.6 us (24%)
  Pallas kernels  7.51 us (16%)
  between operations  2.1 us (4%)
  local copies, waits for them, and re-layouts  0.77 us (2%)
    ppermute x15, starting transfers between devices, swap(): lax.ppermute(value, axis, [(i, i ^ step) for i in range(lax.axis_size(axi...  16.3 us
    ppermute x4, starting transfers between devices, local(): lax.ppermute(lax.dynamic_slice_in_dim(value, first, depth, 0), 'gz', ends...  9.02 us
    ppermute x15, waiting for transfers between devices, swap(): lax.ppermute(value, axis, [(i, i ^ step) for i in range(lax.axis_size(axi...  9 us
    pallas_call x1, Pallas kernels, shear_x(): pl.pallas_call(functools.partial(shear_x_kernel, classes), out_shape=[jax...  2.7 us
    ppermute x4, waiting for transfers between devices, local(): lax.ppermute(lax.dynamic_slice_in_dim(value, first, depth, 0), 'gz', ends...  2.62 us
    pallas_call x1, Pallas kernels, finish(): pl.pallas_call(functools.partial(finish_kernel, slots), out_shape=jax.Sha...  1.46 us
    pallas_call x2, Pallas kernels, shear_z(): pl.pallas_call(functools.partial(shear_z_kernel, plane_count, depth, chip...  1.03 us
  transfers between devices with their start and end apart: 19, of which 10 were waited for; matrix products, arithmetic and copies ran while one was open for 0% of the time, Pallas kernels for 6%

profile of v3, /device:TPU:0, one launch (start us, length us, event | category | flops | bytes accessed | tf_op | source)
XLA Modules:
  0.0 47.3 jit_solution(9403228310234260164)
XLA Ops:
  0.7 2.7 %shear_x.1 = (f32[40,16,128]{2,1,0:T(8,128)S(1)}, f32[40,16,128]{2,1,0:T(8,128)S(1)}) custom-call(s32[1]{0:T(128)} %bitcast.4.first_ref, s32[1]{0:T(128)} %bitcast.5.side_ref, s32[160]{0:T(256)} %shifts_hbm.1, f32[160]{0:T(256)} %fracs_hbm.1, f32[40,32,128]{2,1,0:T(8,128)} %bitcast.23), custom_call_target="tpu_custom_call" | custom-call | tf_op jit(solution)/shard_map/shear_x/pallas_call | solution.py:131
  3.4 0.7 %collective-permute-start.1 = (f32[36,16,128]{2,1,0:T(8,128)S(1)}, f32[36,16,128]{2,1,0:T(8,128)S(1)}, u32[]{:S(2)}, u32[]{:S(2)}) collective-permute-start(f32[36,16,128]{2,1,0:T(8,128)S(1)} %get-tuple-element.82), channel_id=1, source_target_pairs={{1,2},{2,1},{5,6},{6,5},{9,10},{10,9},{13,14},{14,13},{17,18},{18,... | collective-permute-start | bytes 884744 | tf_op jit(solution)/shard_map/ppermute | solution.py:546
  4.1 5.9 %collective-permute-start = (f32[36,16,128]{2,1,0:T(8,128)S(1)}, f32[36,16,128]{2,1,0:T(8,128)S(1)}, u32[]{:S(2)}, u32[]{:S(2)}) collective-permute-start(f32[36,16,128]{2,1,0:T(8,128)S(1)} %get-tuple-element.83), channel_id=1, source_target_pairs={{0,1},{1,0},{2,3},{3,2},{4,5},{5,4},{6,7},{7,6},{8,9},{9,8},{10,11... | collective-permute-start | bytes 884744 | tf_op jit(solution)/shard_map/ppermute | solution.py:546
  10.1 0.7 %collective-permute-start.5 = (f32[36,16,128]{2,1,0:T(8,128)S(1)}, f32[36,16,128]{2,1,0:T(8,128)S(1)}, u32[]{:S(2)}, u32[]{:S(2)}) collective-permute-start(f32[36,16,128]{2,1,0:T(8,128)S(1)} %get-tuple-element.80), channel_id=1, source_target_pairs={{1,2},{2,1},{5,6},{6,5},{9,10},{10,9},{13,14},{14,13},{17,18},{18,... | collective-permute-start | bytes 884744 | tf_op jit(solution)/shard_map/ppermute | solution.py:546
  10.7 1.8 %collective-permute-start.4 = (f32[36,16,128]{2,1,0:T(8,128)S(1)}, f32[36,16,128]{2,1,0:T(8,128)S(1)}, u32[]{:S(2)}, u32[]{:S(2)}) collective-permute-start(f32[36,16,128]{2,1,0:T(8,128)S(1)} %get-tuple-element.81), channel_id=1, source_target_pairs={{0,1},{1,0},{2,3},{3,2},{4,5},{5,4},{6,7},{7,6},{8,9},{9,8},{10,11... | collective-permute-start | bytes 884744 | tf_op jit(solution)/shard_map/ppermute | solution.py:546
  13.8 0.0 copy-start.1
  13.8 0.0 copy-start
  13.8 0.0 copy-start.2
  13.8 0.6 %copy-done.1 = f32[512]{0:T(512)S(1)} copy-done((f32[512]{0:T(512)S(1)}, f32[512]{0:T(512)}, u32[]{:S(2)}) %copy-start.1) | copy-done | bytes 2072
  14.5 0.0 copy-done
  14.5 0.0 copy-done.2
  14.5 0.9 %weights.1 = (f32[40,112]{1,0:T(8,128)S(1)}, f32[64,128]{1,0:T(8,128)S(1)}, f32[40,40]{1,0:T(8,128)S(1)}) custom-call(s32[1]{0:T(128)} %bitcast.1.place_ref, s32[1]{0:T(128)S(6)} %copy.11.shift_ref, f32[1]{0:T(128)S(6)} %copy.12.frac_ref, s32[8]{0:T(128)S(1)} %copy-done.2, s32[1,512]{1,0:T(1,128)S(1)} %bitcast.21, f32[1,512]{1,0:T(1,128)S(1)} %bitcast.22), custom_call_target="tpu_custom_call" | custom-call | tf_op jit(solution)/shard_map/weights/pallas_call | solution.py:205
  15.5 0.0 collective-permute-done.1
  15.5 2.4 %collective-permute-done = f32[36,16,128]{2,1,0:T(8,128)S(1)} collective-permute-done((f32[36,16,128]{2,1,0:T(8,128)S(1)}, f32[36,16,128]{2,1,0:T(8,128)S(1)}, u32[]{:S(2)}, u32[]{:S(2)}) %collective-permute-start) | collective-permute-done | bytes 294944 | tf_op jit(solution)/shard_map/ppermute | solution.py:546
  17.9 0.5 %shear_z.2 = (f32[40,512]{1,0:T(8,128)S(1)}, f32[40,512]{1,0:T(8,128)S(1)}, f32[40,512]{1,0:T(8,128)S(1)}, f32[40,512]{1,0:T(8,128)S(1)}) custom-call(s32[1]{0:T(128)} %bitcast.row_ref, f32[40,112]{1,0:T(8,128)S(1)} %get-tuple-element.49.mixing_ref, f32[576,128]{1,0:T(8,128)S(1)} %bitcast.20, f32[640,128]{1,0:T(8,128)S(1)} %bitcast.16, f32[576,128]{1,0:T(8,128)S(1)} %bitcast.19), custom_call_target="tpu_custom_call" | custom-call | tf_op jit(solution)/shard_map/shear_z/pallas_call | solution.py:263
  18.4 0.1 collective-permute-start.2
  18.5 2.5 %collective-permute-start.3 = (f32[40,512]{1,0:T(8,128)S(1)}, f32[40,512]{1,0:T(8,128)S(1)}, u32[]{:S(2)}, u32[]{:S(2)}) collective-permute-start(f32[40,512]{1,0:T(8,128)S(1)} %get-tuple-element.48), channel_id=1, source_target_pairs={{0,24},{4,28},{8,16},{12,20},{16,8},{20,12},{24,0},{28,4},{1,25},{... | collective-permute-start | bytes 245768 | tf_op jit(solution)/shard_map/ppermute | solution.py:511
  21.0 1.3 %collective-permute-start.8 = (f32[40,512]{1,0:T(8,128)S(1)}, f32[40,512]{1,0:T(8,128)S(1)}, u32[]{:S(2)}, u32[]{:S(2)}) collective-permute-start(f32[40,512]{1,0:T(8,128)S(1)} %get-tuple-element.57), channel_id=1, source_target_pairs={{0,12},{4,8},{8,4},{12,0},{16,28},{20,24},{24,20},{28,16},{1,13},{... | collective-permute-start | bytes 245768 | tf_op jit(solution)/shard_map/ppermute | solution.py:511
  22.3 0.0 collective-permute-done.5
  22.3 0.5 %collective-permute-start.9 = (f32[40,512]{1,0:T(8,128)S(1)}, f32[40,512]{1,0:T(8,128)S(1)}, u32[]{:S(2)}, u32[]{:S(2)}) collective-permute-start(f32[40,512]{1,0:T(8,128)S(1)} %get-tuple-element.58), channel_id=1, source_target_pairs={{0,8},{4,12},{8,0},{12,4},{16,24},{20,28},{24,16},{28,20},{1,9},{5... | collective-permute-start | bytes 245768 | tf_op jit(solution)/shard_map/ppermute | solution.py:511
  22.9 0.2 collective-permute-done.4
  23.1 0.5 %shear_z.3 = (f32[40,512]{1,0:T(8,128)S(1)}, f32[40,512]{1,0:T(8,128)S(1)}, f32[40,512]{1,0:T(8,128)S(1)}, f32[40,512]{1,0:T(8,128)S(1)}) custom-call(s32[1]{0:T(128)} %bitcast.row_ref, f32[40,112]{1,0:T(8,128)S(1)} %get-tuple-element.49.mixing_ref, f32[576,128]{1,0:T(8,128)S(1)} %bitcast.18, f32[640,128]{1,0:T(8,128)S(1)} %bitcast.15, f32[576,128]{1,0:T(8,128)S(1)} %bitcast.17), custom_call_target="tpu_custom_call" | custom-call | tf_op jit(solution)/shard_map/shear_z/pallas_call | solution.py:263
  23.6 0.6 %collective-permute-start.6 = (f32[40,512]{1,0:T(8,128)S(1)}, f32[40,512]{1,0:T(8,128)S(1)}, u32[]{:S(2)}, u32[]{:S(2)}) collective-permute-start(f32[40,512]{1,0:T(8,128)S(1)} %get-tuple-element.55), channel_id=1, source_target_pairs={{0,20},{4,16},{8,28},{12,24},{16,4},{20,0},{24,12},{28,8},{1,21},{... | collective-permute-start | bytes 245768 | tf_op jit(solution)/shard_map/ppermute | solution.py:511
  24.2 0.0 collective-permute-done.2.refs_0_
  24.2 1.1 %collective-permute-start.7 = (f32[40,512]{1,0:T(8,128)S(1)}, f32[40,512]{1,0:T(8,128)S(1)}, u32[]{:S(2)}, u32[]{:S(2)}) collective-permute-start(f32[40,512]{1,0:T(8,128)S(1)} %get-tuple-element.56), channel_id=1, source_target_pairs={{0,16},{4,20},{8,24},{12,28},{16,0},{20,4},{24,8},{28,12},{1,17},{... | collective-permute-start | bytes 245768 | tf_op jit(solution)/shard_map/ppermute | solution.py:511
  25.2 0.1 collective-permute-done.3.refs_1_
  25.4 0.8 %collective-permute-start.10 = (f32[40,512]{1,0:T(8,128)S(1)}, f32[40,512]{1,0:T(8,128)S(1)}, u32[]{:S(2)}, u32[]{:S(2)}) collective-permute-start(f32[40,512]{1,0:T(8,128)S(1)} %get-tuple-element.59), channel_id=1, source_target_pairs={{0,4},{4,0},{8,12},{12,8},{16,20},{20,16},{24,28},{28,24},{1,5},{5... | collective-permute-start | bytes 245768 | tf_op jit(solution)/shard_map/ppermute | solution.py:511
  26.2 0.9 %collective-permute-done.8.refs_4_ = f32[40,512]{1,0:T(8,128)S(1)} collective-permute-done((f32[40,512]{1,0:T(8,128)S(1)}, f32[40,512]{1,0:T(8,128)S(1)}, u32[]{:S(2)}, u32[]{:S(2)}) %collective-permute-start.8) | collective-permute-done | bytes 81952 | tf_op jit(solution)/shard_map/ppermute | solution.py:511
  27.1 1.2 %collective-permute-done.9.refs_5_ = f32[40,512]{1,0:T(8,128)S(1)} collective-permute-done((f32[40,512]{1,0:T(8,128)S(1)}, f32[40,512]{1,0:T(8,128)S(1)}, u32[]{:S(2)}, u32[]{:S(2)}) %collective-permute-start.9) | collective-permute-done | bytes 81952 | tf_op jit(solution)/shard_map/ppermute | solution.py:511
  28.3 0.0 collective-permute-done.6.refs_2_
  28.3 1.8 %collective-permute-done.7.refs_3_ = f32[40,512]{1,0:T(8,128)S(1)} collective-permute-done((f32[40,512]{1,0:T(8,128)S(1)}, f32[40,512]{1,0:T(8,128)S(1)}, u32[]{:S(2)}, u32[]{:S(2)}) %collective-permute-start.7) | collective-permute-done | bytes 81952 | tf_op jit(solution)/shard_map/ppermute | solution.py:511
  30.1 0.0 collective-permute-done.10.refs_6_
  30.1 0.4 shear_y.1
  30.5 1.6 %collective-permute-start.17 = (f32[2,40,512]{2,1,0:T(8,128)S(1)}, f32[2,40,512]{2,1,0:T(8,128)S(1)}, u32[]{:S(2)}, u32[]{:S(2)}) collective-permute-start(f32[2,40,512]{2,1,0:T(8,128)S(1)} %get-tuple-element.64.refs_2_), channel_id=1, source_target_pairs={{0,8},{4,12},{8,0},{12,4},{16,24},{20,28},{24,16},{28,20},{1,9},{5... | collective-permute-start | bytes 491528 | tf_op jit(solution)/shard_map/ppermute | solution.py:511
  32.1 0.4 collective-permute-start.16
  32.5 1.6 %collective-permute-start.15 = (f32[2,40,512]{2,1,0:T(8,128)S(1)}, f32[2,40,512]{2,1,0:T(8,128)S(1)}, u32[]{:S(2)}, u32[]{:S(2)}) collective-permute-start(f32[2,40,512]{2,1,0:T(8,128)S(1)} %get-tuple-element.66.refs_4_), channel_id=1, source_target_pairs={{0,24},{4,28},{8,16},{12,20},{16,8},{20,12},{24,0},{28,4},{1,25},{... | collective-permute-start | bytes 491528 | tf_op jit(solution)/shard_map/ppermute | solution.py:511
  34.1 0.3 project.1
  34.4 1.9 %collective-permute-start.12 = (f32[2,8,512]{2,1,0:T(8,128)S(1)}, f32[2,8,512]{2,1,0:T(8,128)S(1)}, u32[]{:S(2)}, u32[]{:S(2)}) collective-permute-start(f32[2,8,512]{2,1,0:T(8,128)S(1)} %get-tuple-element.68), channel_id=1, source_target_pairs={{0,1},{1,0},{2,3},{3,2},{4,5},{5,4},{6,7},{7,6},{8,9},{9,8},{10,11... | collective-permute-start | bytes 98312 | tf_op jit(solution)/shard_map/ppermute | solution.py:511
  36.4 1.1 %collective-permute-start.13 = (f32[2,8,512]{2,1,0:T(8,128)S(1)}, f32[2,8,512]{2,1,0:T(8,128)S(1)}, u32[]{:S(2)}, u32[]{:S(2)}) collective-permute-start(f32[2,8,512]{2,1,0:T(8,128)S(1)} %get-tuple-element.69), channel_id=1, source_target_pairs={{0,2},{1,3},{2,0},{3,1},{4,6},{5,7},{6,4},{7,5},{8,10},{9,11},{10,... | collective-permute-start | bytes 98312 | tf_op jit(solution)/shard_map/ppermute | solution.py:511
  37.5 1.0 %collective-permute-done.12.refs_1_ = f32[2,8,512]{2,1,0:T(8,128)S(1)} collective-permute-done((f32[2,8,512]{2,1,0:T(8,128)S(1)}, f32[2,8,512]{2,1,0:T(8,128)S(1)}, u32[]{:S(2)}, u32[]{:S(2)}) %collective-permute-start.12) | collective-permute-done | bytes 32800 | tf_op jit(solution)/shard_map/ppermute | solution.py:511
  38.4 2.3 %collective-permute-start.14 = (f32[2,8,512]{2,1,0:T(8,128)S(1)}, f32[2,8,512]{2,1,0:T(8,128)S(1)}, u32[]{:S(2)}, u32[]{:S(2)}) collective-permute-start(f32[2,8,512]{2,1,0:T(8,128)S(1)} %get-tuple-element.70), channel_id=1, source_target_pairs={{0,3},{1,2},{2,1},{3,0},{4,7},{5,6},{6,5},{7,4},{8,11},{9,10},{10,... | collective-permute-start | bytes 98312 | tf_op jit(solution)/shard_map/ppermute | solution.py:511
  40.7 1.2 %collective-permute-done.13.refs_2_ = f32[2,8,512]{2,1,0:T(8,128)S(1)} collective-permute-done((f32[2,8,512]{2,1,0:T(8,128)S(1)}, f32[2,8,512]{2,1,0:T(8,128)S(1)}, u32[]{:S(2)}, u32[]{:S(2)}) %collective-permute-start.13) | collective-permute-done | bytes 32800 | tf_op jit(solution)/shard_map/ppermute | solution.py:511
  42.0 2.2 %collective-permute-done.14.refs_3_ = f32[2,8,512]{2,1,0:T(8,128)S(1)} collective-permute-done((f32[2,8,512]{2,1,0:T(8,128)S(1)}, f32[2,8,512]{2,1,0:T(8,128)S(1)}, u32[]{:S(2)}, u32[]{:S(2)}) %collective-permute-start.14) | collective-permute-done | bytes 32800 | tf_op jit(solution)/shard_map/ppermute | solution.py:511
  44.1 0.0 collective-permute-done.17.refs_0_.refs_2_
  44.1 0.0 collective-permute-done.16.refs_1_.refs_3_
  44.1 0.0 collective-permute-done.15.refs_2_.refs_4_
  44.2 0.1 collective-permute-start.18
  44.3 0.5 %collective-permute-start.11 = (f32[40,512]{1,0:T(8,128)S(1)}, f32[40,512]{1,0:T(8,128)S(1)}, u32[]{:S(2)}, u32[]{:S(2)}) collective-permute-start(f32[40,512]{1,0:T(8,128)S(1)} %get-tuple-element.62.refs_1_), channel_id=1, source_target_pairs={{0,4},{4,0},{8,12},{12,8},{16,20},{20,16},{24,28},{28,24},{1,5},{5... | collective-permute-start | bytes 245768 | tf_op jit(solution)/shard_map/ppermute | solution.py:511
  44.8 0.6 %add_shares.1 = f32[2,8,512]{2,1,0:T(8,128)} custom-call(f32[2,8,512]{2,1,0:T(8,128)S(1)} %get-tuple-element.74.refs_0_, f32[2,8,512]{2,1,0:T(8,128)S(1)} %collective-permute-done.12.refs_1_, f32[2,8,512]{2,1,0:T(8,128)S(1)} %collective-permute-done.13.refs_2_, f32[2,8,512]{2,1,0:T(8,128)S(1)} %collective-permute-done.14.refs_3_), custom_call_target="tpu_custom_call" | custom-call | tf_op jit(solution)/shard_map/add_shares/pallas_call | solution.py:431
  45.4 0.5 %collective-permute-done.11.refs_1_ = f32[40,512]{1,0:T(8,128)S(1)} collective-permute-done((f32[40,512]{1,0:T(8,128)S(1)}, f32[40,512]{1,0:T(8,128)S(1)}, u32[]{:S(2)}, u32[]{:S(2)}) %collective-permute-start.11) | collective-permute-done | bytes 81952 | tf_op jit(solution)/shard_map/ppermute | solution.py:511
  45.9 0.0 collective-permute-done.18.refs_5_.refs_6_.refs_7_
  45.9 1.5 %finish.1 = f32[1280,128]{1,0:T(8,128)} custom-call(s32[1]{0:T(128)} %bitcast.row_ref, f32[40,512]{1,0:T(8,128)S(1)} %get-tuple-element.61.refs_0_, f32[40,512]{1,0:T(8,128)S(1)} %collective-permute-done.11.refs_1_, f32[2,40,512]{2,1,0:T(8,128)S(1)} %collective-permute-done.17.refs_0_.refs_2_, f32[2,40,512]{2,1,0:T(8,128)S(1)} %collective-permute-done.16.refs_1_.refs_3_, ...), custom_call_target="tpu_custom_call" | custom-call | tf_op jit(solution)/shard_map/finish/pallas_call | solution.py:411
  (3 shorter events, 0.1 us)
Async XLA Ops:
  3.4 12.0 %collective-permute-start.1 = (f32[36,16,128]{2,1,0:T(8,128)S(1)}, f32[36,16,128]{2,1,0:T(8,128)S(1)}, u32[]{:S(2)}, u32[]{:S(2)}) collective-permute-start(f32[36,16,128]{2,1,0:T(8,128)S(1)} %get-tuple-element.82), channel_id=1, source_target_pairs={{1,2},{2,1},{5,6},{6,5},{9,10},{10,9},{13,14},{14,13},{17,18},{18,... | collective-permute-start | bytes 884744 | tf_op jit(solution)/shard_map/ppermute | solution.py:546
  4.1 13.8 %collective-permute-start = (f32[36,16,128]{2,1,0:T(8,128)S(1)}, f32[36,16,128]{2,1,0:T(8,128)S(1)}, u32[]{:S(2)}, u32[]{:S(2)}) collective-permute-start(f32[36,16,128]{2,1,0:T(8,128)S(1)} %get-tuple-element.83), channel_id=1, source_target_pairs={{0,1},{1,0},{2,3},{3,2},{4,5},{5,4},{6,7},{7,6},{8,9},{9,8},{10,11... | collective-permute-start | bytes 884744 | tf_op jit(solution)/shard_map/ppermute | solution.py:546
  10.1 12.3 %collective-permute-start.5 = (f32[36,16,128]{2,1,0:T(8,128)S(1)}, f32[36,16,128]{2,1,0:T(8,128)S(1)}, u32[]{:S(2)}, u32[]{:S(2)}) collective-permute-start(f32[36,16,128]{2,1,0:T(8,128)S(1)} %get-tuple-element.80), channel_id=1, source_target_pairs={{1,2},{2,1},{5,6},{6,5},{9,10},{10,9},{13,14},{14,13},{17,18},{18,... | collective-permute-start | bytes 884744 | tf_op jit(solution)/shard_map/ppermute | solution.py:546
  10.7 12.3 %collective-permute-start.4 = (f32[36,16,128]{2,1,0:T(8,128)S(1)}, f32[36,16,128]{2,1,0:T(8,128)S(1)}, u32[]{:S(2)}, u32[]{:S(2)}) collective-permute-start(f32[36,16,128]{2,1,0:T(8,128)S(1)} %get-tuple-element.81), channel_id=1, source_target_pairs={{0,1},{1,0},{2,3},{3,2},{4,5},{5,4},{6,7},{7,6},{8,9},{9,8},{10,11... | collective-permute-start | bytes 884744 | tf_op jit(solution)/shard_map/ppermute | solution.py:546
  13.8 0.7 %copy-start.1 = (f32[512]{0:T(512)S(1)}, f32[512]{0:T(512)}, u32[]{:S(2)}) copy-start(f32[512]{0:T(512)} %param.14) | copy-start | bytes 6148
  13.8 0.7 %copy-start = (s32[512]{0:T(512)S(1)}, s32[512]{0:T(512)}, u32[]{:S(2)}) copy-start(s32[512]{0:T(512)} %param.13) | copy-start | bytes 6148
  13.8 0.7 %copy-start.2 = (s32[8]{0:T(128)S(1)}, s32[8]{0:T(128)}, u32[]{:S(2)}) copy-start(s32[8]{0:T(128)} %slopes_ref.1) | copy-start | bytes 100
  18.4 5.8 %collective-permute-start.2 = (f32[40,512]{1,0:T(8,128)S(1)}, f32[40,512]{1,0:T(8,128)S(1)}, u32[]{:S(2)}, u32[]{:S(2)}) collective-permute-start(f32[40,512]{1,0:T(8,128)S(1)} %get-tuple-element.47), channel_id=1, source_target_pairs={{0,28},{4,24},{8,20},{12,16},{16,12},{20,8},{24,4},{28,0},{1,29},{... | collective-permute-start | bytes 245768 | tf_op jit(solution)/shard_map/ppermute | solution.py:511
  18.5 6.9 %collective-permute-start.3 = (f32[40,512]{1,0:T(8,128)S(1)}, f32[40,512]{1,0:T(8,128)S(1)}, u32[]{:S(2)}, u32[]{:S(2)}) collective-permute-start(f32[40,512]{1,0:T(8,128)S(1)} %get-tuple-element.48), channel_id=1, source_target_pairs={{0,24},{4,28},{8,16},{12,20},{16,8},{20,12},{24,0},{28,4},{1,25},{... | collective-permute-start | bytes 245768 | tf_op jit(solution)/shard_map/ppermute | solution.py:511
  21.0 6.1 %collective-permute-start.8 = (f32[40,512]{1,0:T(8,128)S(1)}, f32[40,512]{1,0:T(8,128)S(1)}, u32[]{:S(2)}, u32[]{:S(2)}) collective-permute-start(f32[40,512]{1,0:T(8,128)S(1)} %get-tuple-element.57), channel_id=1, source_target_pairs={{0,12},{4,8},{8,4},{12,0},{16,28},{20,24},{24,20},{28,16},{1,13},{... | collective-permute-start | bytes 245768 | tf_op jit(solution)/shard_map/ppermute | solution.py:511
  22.3 6.0 %collective-permute-start.9 = (f32[40,512]{1,0:T(8,128)S(1)}, f32[40,512]{1,0:T(8,128)S(1)}, u32[]{:S(2)}, u32[]{:S(2)}) collective-permute-start(f32[40,512]{1,0:T(8,128)S(1)} %get-tuple-element.58), channel_id=1, source_target_pairs={{0,8},{4,12},{8,0},{12,4},{16,24},{20,28},{24,16},{28,20},{1,9},{5... | collective-permute-start | bytes 245768 | tf_op jit(solution)/shard_map/ppermute | solution.py:511
  23.6 4.7 %collective-permute-start.6 = (f32[40,512]{1,0:T(8,128)S(1)}, f32[40,512]{1,0:T(8,128)S(1)}, u32[]{:S(2)}, u32[]{:S(2)}) collective-permute-start(f32[40,512]{1,0:T(8,128)S(1)} %get-tuple-element.55), channel_id=1, source_target_pairs={{0,20},{4,16},{8,28},{12,24},{16,4},{20,0},{24,12},{28,8},{1,21},{... | collective-permute-start | bytes 245768 | tf_op jit(solution)/shard_map/ppermute | solution.py:511
  24.2 6.0 %collective-permute-start.7 = (f32[40,512]{1,0:T(8,128)S(1)}, f32[40,512]{1,0:T(8,128)S(1)}, u32[]{:S(2)}, u32[]{:S(2)}) collective-permute-start(f32[40,512]{1,0:T(8,128)S(1)} %get-tuple-element.56), channel_id=1, source_target_pairs={{0,16},{4,20},{8,24},{12,28},{16,0},{20,4},{24,8},{28,12},{1,17},{... | collective-permute-start | bytes 245768 | tf_op jit(solution)/shard_map/ppermute | solution.py:511
  25.4 4.8 %collective-permute-start.10 = (f32[40,512]{1,0:T(8,128)S(1)}, f32[40,512]{1,0:T(8,128)S(1)}, u32[]{:S(2)}, u32[]{:S(2)}) collective-permute-start(f32[40,512]{1,0:T(8,128)S(1)} %get-tuple-element.59), channel_id=1, source_target_pairs={{0,4},{4,0},{8,12},{12,8},{16,20},{20,16},{24,28},{28,24},{1,5},{5... | collective-permute-start | bytes 245768 | tf_op jit(solution)/shard_map/ppermute | solution.py:511
  30.5 13.6 %collective-permute-start.17 = (f32[2,40,512]{2,1,0:T(8,128)S(1)}, f32[2,40,512]{2,1,0:T(8,128)S(1)}, u32[]{:S(2)}, u32[]{:S(2)}) collective-permute-start(f32[2,40,512]{2,1,0:T(8,128)S(1)} %get-tuple-element.64.refs_2_), channel_id=1, source_target_pairs={{0,8},{4,12},{8,0},{12,4},{16,24},{20,28},{24,16},{28,20},{1,9},{5... | collective-permute-start | bytes 491528 | tf_op jit(solution)/shard_map/ppermute | solution.py:511
  32.1 12.1 %collective-permute-start.16 = (f32[2,40,512]{2,1,0:T(8,128)S(1)}, f32[2,40,512]{2,1,0:T(8,128)S(1)}, u32[]{:S(2)}, u32[]{:S(2)}) collective-permute-start(f32[2,40,512]{2,1,0:T(8,128)S(1)} %get-tuple-element.65.refs_3_), channel_id=1, source_target_pairs={{0,16},{4,20},{8,24},{12,28},{16,0},{20,4},{24,8},{28,12},{1,17},{... | collective-permute-start | bytes 491528 | tf_op jit(solution)/shard_map/ppermute | solution.py:511
  32.5 11.7 %collective-permute-start.15 = (f32[2,40,512]{2,1,0:T(8,128)S(1)}, f32[2,40,512]{2,1,0:T(8,128)S(1)}, u32[]{:S(2)}, u32[]{:S(2)}) collective-permute-start(f32[2,40,512]{2,1,0:T(8,128)S(1)} %get-tuple-element.66.refs_4_), channel_id=1, source_target_pairs={{0,24},{4,28},{8,16},{12,20},{16,8},{20,12},{24,0},{28,4},{1,25},{... | collective-permute-start | bytes 491528 | tf_op jit(solution)/shard_map/ppermute | solution.py:511
  34.4 4.0 %collective-permute-start.12 = (f32[2,8,512]{2,1,0:T(8,128)S(1)}, f32[2,8,512]{2,1,0:T(8,128)S(1)}, u32[]{:S(2)}, u32[]{:S(2)}) collective-permute-start(f32[2,8,512]{2,1,0:T(8,128)S(1)} %get-tuple-element.68), channel_id=1, source_target_pairs={{0,1},{1,0},{2,3},{3,2},{4,5},{5,4},{6,7},{7,6},{8,9},{9,8},{10,11... | collective-permute-start | bytes 98312 | tf_op jit(solution)/shard_map/ppermute | solution.py:511
  36.4 5.6 %collective-permute-start.13 = (f32[2,8,512]{2,1,0:T(8,128)S(1)}, f32[2,8,512]{2,1,0:T(8,128)S(1)}, u32[]{:S(2)}, u32[]{:S(2)}) collective-permute-start(f32[2,8,512]{2,1,0:T(8,128)S(1)} %get-tuple-element.69), channel_id=1, source_target_pairs={{0,2},{1,3},{2,0},{3,1},{4,6},{5,7},{6,4},{7,5},{8,10},{9,11},{10,... | collective-permute-start | bytes 98312 | tf_op jit(solution)/shard_map/ppermute | solution.py:511
  38.4 5.7 %collective-permute-start.14 = (f32[2,8,512]{2,1,0:T(8,128)S(1)}, f32[2,8,512]{2,1,0:T(8,128)S(1)}, u32[]{:S(2)}, u32[]{:S(2)}) collective-permute-start(f32[2,8,512]{2,1,0:T(8,128)S(1)} %get-tuple-element.70), channel_id=1, source_target_pairs={{0,3},{1,2},{2,1},{3,0},{4,7},{5,6},{6,5},{7,4},{8,11},{9,10},{10,... | collective-permute-start | bytes 98312 | tf_op jit(solution)/shard_map/ppermute | solution.py:511
  44.2 1.7 %collective-permute-start.18 = (f32[3,40,512]{2,1,0:T(8,128)S(1)}, f32[3,40,512]{2,1,0:T(8,128)S(1)}, u32[]{:S(2)}, u32[]{:S(2)}) collective-permute-start(f32[3,40,512]{2,1,0:T(8,128)S(1)} %collect.1), channel_id=1, source_target_pairs={{0,4},{4,0},{8,12},{12,8},{16,20},{20,16},{24,28},{28,24},{1,5},{5... | collective-permute-start | bytes 737288 | tf_op jit(solution)/shard_map/ppermute | solution.py:511
  44.3 1.6 %collective-permute-start.11 = (f32[40,512]{1,0:T(8,128)S(1)}, f32[40,512]{1,0:T(8,128)S(1)}, u32[]{:S(2)}, u32[]{:S(2)}) collective-permute-start(f32[40,512]{1,0:T(8,128)S(1)} %get-tuple-element.62.refs_1_), channel_id=1, source_target_pairs={{0,4},{4,0},{8,12},{12,8},{16,20},{20,16},{24,28},{28,24},{1,5},{5... | collective-permute-start | bytes 245768 | tf_op jit(solution)/shard_map/ppermute | solution.py:511

commit v4 on v3

--- a/solution.py
+++ b/solution.py
@@ -42,7 +42,7 @@
 
 
 def shear_x_kernel(
-    classes, first_ref, side_ref, shifts_hbm, fracs_hbm, planes_hbm, *rest
+    classes, shifts_hbm, fracs_hbm, planes_hbm, *rest
 ):
     out_refs = rest[:-8]
     planes_ref, margin_ref, base_ref, lines_ref, shifts_ref, fracs_ref, small_sem, plane_sem = (
@@ -73,8 +73,9 @@
     tap = (lanes - lax.broadcasted_iota(jnp.int32, (plane_count, lanes), 1)) % lanes
     lane_of_row = lax.broadcasted_iota(jnp.int32, (per_class, lanes), 1)
     zeros = jnp.zeros((8, lanes), jnp.float32)
-    first = first_ref[0]
-    first_lines = (2 - 2 * side_ref[0], 2 * side_ref[0])
+    first = lax.axis_index("gz") * plane_count
+    side = lax.axis_index("gy") // 2 % 2
+    first_lines = (2 - 2 * side, 2 * side)
     for copy in small:
         copy.wait()
     for z in range(plane_count):
@@ -125,7 +126,7 @@
         lax.fori_loop(b * per_block, (b + 1) * per_block, one_plane, 0, unroll=True)
 
 
-def shear_x(volume, x_offsets, x_fracs, first_plane, side, classes, parts):
+def shear_x(volume, x_offsets, x_fracs, classes, parts):
     plane_count, rows, lanes = volume.shape
     blocks = 2 if plane_count % 2 == 0 else 1
     return pl.pallas_call(
@@ -133,7 +134,7 @@
         out_shape=[
             jax.ShapeDtypeStruct((plane_count, rows // parts, lanes), jnp.float32)
         ] * parts,
-        in_specs=[SMEM_SPEC] * 2 + [pl.BlockSpec(memory_space=pltpu.HBM)] * 3,
+        in_specs=[pl.BlockSpec(memory_space=pltpu.HBM)] * 3,
         out_specs=[VMEM_SPEC] * parts,
         scratch_shapes=[
             pltpu.VMEM(volume.shape, jnp.float32),
@@ -148,18 +149,17 @@
         compiler_params=pltpu.CompilerParams(vmem_limit_bytes=VMEM_LIMIT),
         name="shear_x",
     )(
-        first_plane.reshape(1),
-        side.reshape(1),
         *(pltpu.with_memory_space_constraint(v, pltpu.HBM) for v in (x_offsets, x_fracs, volume)),
     )
 
 
 def weights_kernel(
-    plane_count, depth, ny, shares, place_ref, shift_ref, frac_ref, slopes_ref, shifts_ref,
-    fracs_ref, mixing_ref, taps_ref, chosen_ref,
+    plane_count, depth, ny, shares, shift_ref, frac_ref, slopes_ref, shifts_ref, fracs_ref,
+    mixing_ref, taps_ref, chosen_ref,
 ):
     reach = plane_count + 2 * depth
-    even = place_ref[0] % 2 == 0
+    place = lax.axis_index("gz")
+    even = place % 2 == 0
     target = lax.broadcasted_iota(jnp.int32, (plane_count, reach), 0)
     column = lax.broadcasted_iota(jnp.int32, (plane_count, reach), 1)
     pair_start = jnp.where(even, plane_count, -depth)
@@ -185,7 +185,7 @@
     tilts = slopes_ref.shape[0]
     span = ny // 4
     entry = lax.broadcasted_iota(jnp.int32, chosen_ref.shape, 0)
-    plane = lax.broadcasted_iota(jnp.int32, chosen_ref.shape, 1) + place_ref[0] * plane_count
+    plane = lax.broadcasted_iota(jnp.int32, chosen_ref.shape, 1) + place * plane_count
     lift = entry // tilts - span
     tilt = entry - (lift + span) * tilts
     slope = jnp.zeros_like(tilt)
@@ -198,7 +198,7 @@
 
 
 def weights(
-    place, z_offsets, z_fracs, slopes, y_offsets, y_fracs, plane_count, depth, ny, shares
+    z_offsets, z_fracs, slopes, y_offsets, y_fracs, plane_count, depth, ny, shares
 ):
     width = y_offsets.shape[0]
     lifts = 2 * (ny // 4) + 1
@@ -209,18 +209,18 @@
             jax.ShapeDtypeStruct((width // LANES * 2 * ny, LANES), jnp.float32),
             jax.ShapeDtypeStruct((lifts * slopes.shape[0], plane_count), jnp.float32),
         ),
-        in_specs=[SMEM_SPEC] * 4 + [VMEM_SPEC] * 2,
+        in_specs=[SMEM_SPEC] * 3 + [VMEM_SPEC] * 2,
         out_specs=(VMEM_SPEC, VMEM_SPEC, VMEM_SPEC),
         compiler_params=pltpu.CompilerParams(vmem_limit_bytes=VMEM_LIMIT),
         name="weights",
     )(
-        place.reshape(1), z_offsets, z_fracs, slopes,
+        z_offsets, z_fracs, slopes,
         y_offsets.reshape(1, width), y_fracs.reshape(1, width),
     )
 
 
 def shear_z_kernel(
-    plane_count, depth, chips, row_ref, mixing_ref, pair_ref, own_ref, other_ref, *outs
+    plane_count, depth, chips, mixing_ref, pair_ref, own_ref, other_ref, *outs
 ):
     lanes = own_ref.shape[1]
     rows = own_ref.shape[0] // plane_count
@@ -231,7 +231,8 @@
     mixing = jnp.concatenate(
         [jnp.concatenate([high, high], axis=1), jnp.concatenate([low, low], axis=1)], axis=0
     )
-    core, chip_pair = row_ref[0] % 2, row_ref[0] // 4
+    own_row = lax.axis_index("gy")
+    core, chip_pair = own_row % 2, own_row // 4
     for index, out_ref in enumerate(outs):
         first = (core ^ (index % 2)) * (rows // 2) + (chip_pair ^ (index // 2))
         for tile in range(0, tiles, pair):
@@ -256,24 +257,29 @@
             )
 
 
-def shear_z(row, mixing, pair, own, other, chips):
+def shear_z(mixing, pair, own, other, chips):
     plane_count, rows, lanes = own.shape
     depth = pair.shape[0]
     width = rows * lanes // chips
     return pl.pallas_call(
         functools.partial(shear_z_kernel, plane_count, depth, chips),
         out_shape=[jax.ShapeDtypeStruct((plane_count, width), jnp.float32)] * chips,
-        in_specs=[SMEM_SPEC] + [VMEM_SPEC] * 4,
+        in_specs=[VMEM_SPEC] * 4,
         out_specs=[VMEM_SPEC] * chips,
         compiler_params=pltpu.CompilerParams(vmem_limit_bytes=VMEM_LIMIT),
         name="shear_z",
-    )(row.reshape(1), mixing, *(value.reshape(-1, lanes) for value in (pair, own, other)))
-
-
-def shear_y_kernel(ny, row_ref, taps_ref, *refs):
-    in_refs, own_refs, out_refs = refs[:ny][::-1], refs[ny:ny + 2], refs[ny + 2:]
+    )(mixing, *(value.reshape(-1, lanes) for value in (pair, own, other)))
+
+
+def start_order(ny):
+    return sorted(range(ny), key=lambda slot: (-(slot // 2 % 2), -(slot // 4), slot % 2, -slot))
+
+
+def shear_y_kernel(ny, taps_ref, *refs):
+    in_refs, out_refs = refs[:ny], refs[ny:]
+    in_refs = [in_refs[start_order(ny).index(slot)] for slot in range(ny)]
     plane_count, width = in_refs[0].shape
-    row = row_ref[0]
+    row = lax.axis_index("gy")
     for tile in range(width // LANES):
         lanes = slice(tile * LANES, (tile + 1) * LANES)
         first = tile * 2 * ny + ny - 1
@@ -290,45 +296,48 @@
                 for source in range(1, ny):
                     value = value + weight[source] * in_refs[source][planes, lanes]
                 if target < 2:
-                    own_refs[target][planes, lanes] = value
+                    out_refs[target][planes, lanes] = value
+                elif target < ny - 2:
+                    out_refs[target // 2 + 1][target % 2, planes, lanes] = value
                 else:
-                    out_refs[target // 2 - 1][target % 2, planes, lanes] = value
-
-
-def shear_y(row, taps, columns):
+                    out_refs[target - ny][planes, lanes] = value
+
+
+def shear_y(taps, columns):
     ny = len(columns)
     shape = columns[0].shape
-    out_shape = [jax.ShapeDtypeStruct(shape, jnp.float32)] * 2
-    out_shape += [jax.ShapeDtypeStruct((2, *shape), jnp.float32)] * (ny // 2 - 1)
+    single = [jax.ShapeDtypeStruct(shape, jnp.float32)] * 2
+    out_shape = single + [jax.ShapeDtypeStruct((2, *shape), jnp.float32)] * (ny // 2 - 2) + single
     return pl.pallas_call(
         functools.partial(shear_y_kernel, ny),
         out_shape=out_shape,
-        in_specs=[SMEM_SPEC] + [VMEM_SPEC] * (1 + ny),
+        in_specs=[VMEM_SPEC] * (1 + ny),
         out_specs=[VMEM_SPEC] * len(out_shape),
         compiler_params=pltpu.CompilerParams(vmem_limit_bytes=VMEM_LIMIT),
         name="shear_y",
-    )(row.reshape(1), taps, *columns[::-1])
+    )(taps, *(columns[slot] for slot in start_order(ny)))
 
 
 def collect_kernel(*refs):
-    out_ref = refs[-1]
-    for index, ref in enumerate(refs[:-1]):
-        out_ref[index] = ref[1]
+    count = len(refs) // 2
+    for source, target in zip(refs[:count], refs[count:]):
+        target[...] = source[1]
 
 
 def collect(landed):
     return pl.pallas_call(
         collect_kernel,
-        out_shape=jax.ShapeDtypeStruct((len(landed), *landed[0].shape[1:]), jnp.float32),
+        out_shape=[jax.ShapeDtypeStruct(v.shape[1:], jnp.float32) for v in landed],
         in_specs=[VMEM_SPEC] * len(landed),
-        out_specs=VMEM_SPEC,
+        out_specs=[VMEM_SPEC] * len(landed),
         compiler_params=pltpu.CompilerParams(vmem_limit_bytes=VMEM_LIMIT),
         name="collect",
     )(*landed)
 
 
-def project_kernel(chips, tilts, place_ref, row_ref, chosen_ref, *refs):
-    in_refs, share_refs, totals_ref = refs[:chips + 1], refs[chips + 1:-1], refs[-1]
+def project_kernel(chips, tilts, chosen_ref, *refs):
+    place, own_row = lax.axis_index("gz"), lax.axis_index("gy")
+    in_refs, share_refs, totals_ref = refs[:chips + 2], refs[chips + 2:-1], refs[-1]
     ny, shares = 2 * chips, len(share_refs)
     plane_count, width = in_refs[0].shape
     total_planes = plane_count * shares
@@ -343,14 +352,16 @@
     for source in range(ny):
         if source < 2:
             value = in_refs[source][...]
+        elif source < ny - 2:
+            value = in_refs[source // 2 + 1][source % 2]
         else:
-            value = in_refs[source // 2 + 1][source % 2]
+            value = in_refs[source - ny][...]
         sums = jnp.dot(
             chosen,
             jnp.concatenate(split_high_low(value), axis=0),
             preferred_element_type=jnp.float32,
         )
-        row = row_ref[0] ^ source
+        row = own_row ^ source
         for l in range(lifts):
             for tile in range(tiles):
                 start = pl.multiple_of(tile * per_tile + (row + 2 * span - l) * tilts, tilts)
@@ -359,7 +370,7 @@
                 ]
     per_share = tilts // shares
     for step, share_ref in enumerate(share_refs):
-        tilt = (place_ref[0] ^ step) * per_share
+        tilt = (place ^ step) * per_share
         for u in range(per_share):
             for tile in range(tiles):
                 share_ref[u, :, tile * LANES:(tile + 1) * LANES] = (
@@ -370,8 +381,8 @@
                 )
 
 
-def project(place, row, chosen, rotated, shares):
-    chips = len(rotated) - 1
+def project(chosen, rotated, shares):
+    chips = len(rotated) - 2
     ny = 2 * chips
     tilts = chosen.shape[0] // (2 * (ny // 4) + 1)
     width = rotated[0].shape[1]
@@ -380,21 +391,22 @@
     return pl.pallas_call(
         functools.partial(project_kernel, chips, tilts),
         out_shape=[share] * shares,
-        in_specs=[SMEM_SPEC] * 2 + [VMEM_SPEC] * (1 + len(rotated)),
+        in_specs=[VMEM_SPEC] * (1 + len(rotated)),
         out_specs=[VMEM_SPEC] * shares,
         scratch_shapes=[pltpu.VMEM(totals, jnp.float32)],
         compiler_params=pltpu.CompilerParams(vmem_limit_bytes=VMEM_LIMIT),
         name="project",
-    )(place.reshape(1), row.reshape(1), chosen, *rotated)
-
-
-def finish_kernel(slots, row_ref, *refs):
+    )(chosen, *rotated)
+
+
+def finish_kernel(slots, *refs):
+    row = lax.axis_index("gy")
     rotated_ref, sources = refs[-1], refs[:len(slots)]
     rows = rotated_ref.shape[0] // sources[0].shape[-2]
     for ref, (slot, index) in zip(sources, slots):
         plane_count, width = ref.shape[-2:]
         per_group = width // LANES
-        start = (row_ref[0] ^ slot) * per_group
+        start = (row ^ slot) * per_group
         source = ref if index is None else ref.at[index]
         for tile in range(per_group):
             rotated_ref[pl.ds(start + tile, plane_count, stride=rows), :] = source[
@@ -402,22 +414,23 @@
             ]
 
 
-def finish(row, own, early, late, landed):
-    chips = len(landed) + 1
+def finish(own, early, landed, late, direct):
+    chips = len(landed) + 2
     plane_count, width = own.shape
     slots = [(0, None), (1, None)]
-    slots += [(2 * step, 0) for step in range(1, chips)]
-    slots += [(2 * step + 1, step - 1) for step in range(1, chips)]
+    slots += [(2 * step, 0) for step in range(1, chips - 1)]
+    slots += [(2 * step + 1, None) for step in range(1, chips - 1)]
+    slots += [(2 * chips - 2, None), (2 * chips - 1, None)]
     return pl.pallas_call(
         functools.partial(finish_kernel, slots),
         out_shape=jax.ShapeDtypeStruct(
             (plane_count * 2 * chips * width // LANES, LANES), jnp.float32
         ),
-        in_specs=[SMEM_SPEC] + [VMEM_SPEC] * len(slots),
+        in_specs=[VMEM_SPEC] * len(slots),
         out_specs=VMEM_SPEC,
         compiler_params=pltpu.CompilerParams(vmem_limit_bytes=VMEM_LIMIT),
         name="finish",
-    )(row.reshape(1), own, early, *landed, *([late] * (chips - 1)))
+    )(own, early, *landed, *late, *direct)
 
 
 def add_kernel(*refs):
@@ -519,12 +532,12 @@
     rows = width_all // LANES
     col_local = width_all // groups
     place = lax.axis_index("gz").astype(jnp.int32)
-    row = lax.axis_index("gy").astype(jnp.int32)
     first_plane = place * plane_count
     chips = groups // 2
-    wide = col_local % LANES == 0 and col_local > LANES and chips % 2 == 0
+    even = chips % 4 == 0 and groups & (groups - 1) == 0 and shares & (shares - 1) == 0
+    wide = even and col_local % LANES == 0 and col_local > LANES and slopes.shape[0] % shares == 0
     sheared = shear_x(
-        volume.reshape(plane_count, rows, LANES), x_offsets, x_fracs, first_plane, row // 2 % 2,
+        volume.reshape(plane_count, rows, LANES), x_offsets, x_fracs,
         col_local // LANES if wide else 1, 2 if wide else 1,
     )
     if not wide:
@@ -533,7 +546,7 @@
             slopes,
         )
     mixing, taps, chosen = weights(
-        place, z_offsets, z_fracs, slopes, y_offsets, y_fracs, plane_count, depth, groups, shares
+        z_offsets, z_fracs, slopes, y_offsets, y_fracs, plane_count, depth, groups, shares
     )
     spare = plane_count - depth
     pair_first = jnp.where(place % 2 == 0, spare, 0)
@@ -546,20 +559,21 @@
             lax.ppermute(lax.dynamic_slice_in_dim(value, first, depth, 0), "gz", ends[parity])
             for parity, first in ((0, pair_first), (1, spare - pair_first))
         )
-        mixed = shear_z(row, mixing, pair, value, other, chips)
+        mixed = shear_z(mixing, pair, value, other, chips)
         mixing, *mixed = lax.optimization_barrier((mixing, *mixed))
         for index in reversed(range(chips)):
             step = 2 * (2 * (index // 2) + half) + index % 2
             columns[step] = swap(mixed[index], "gy", step) if step else mixed[index]
-    own, cross, *rotated = shear_y(row, taps, columns)
-    landed = [swap(value, "gy", 2 * step + 2) for step, value in enumerate(rotated)]
+    own, cross, *rotated = shear_y(taps, columns)
+    pairs, direct = rotated[:-2], rotated[-2:]
+    landed = [swap(value, "gy", 2 * step + 2) for step, value in enumerate(pairs)]
+    direct = [swap(value, "gy", groups - 2 + core) for core, value in enumerate(direct)]
     early = swap(cross, "gy", 1)
-    tilted = project(place, row, chosen, (own, cross, *rotated), shares)
-    tilted = [tilted[0]] + [swap(tilted[step], "gz", step) for step in range(1, shares)]
-    tilted, landed = lax.optimization_barrier((tilted, landed[::-1]))
-    landed = landed[::-1]
-    late = swap(collect(landed), "gy", 1)
-    rotated = finish(row, own, early, late, landed)
+    tilted = project(chosen, (own, cross, *rotated), shares)
+    tilted = [swap(tilted[step], "gz", step) for step in range(shares - 1, 0, -1)] + [tilted[0]]
+    late = [swap(value, "gy", 1) for value in collect(landed)]
+    tilted, direct, late = lax.optimization_barrier((tilted, direct, late))
+    rotated = finish(own, early, landed, late, direct)
     return (
         rotated.reshape(plane_count, row_local, width_all),
         jnp.swapaxes(add(tilted), 1, 2),

time: 47.5 us -> 46.5 us (0.979)
  waiting for transfers between devices: 11.6 us -> 10.7 us
    ppermute x15 -> x17, waiting for transfers between devices: 9 us -> 8.06 us  [swap(): lax.ppermute(value, axis, [(i, i ^ step) for i in range(lax.axis_size(axi...]
    ppermute x15 -> x17, starting transfers between devices: 16.3 us -> 16.3 us  [swap(): lax.ppermute(value, axis, [(i, i ^ step) for i in range(lax.axis_size(axi...]
  transfers between devices with their start and end apart: 19 -> 21, of which waited for: 10 -> 9; matrix products, arithmetic and copies ran while one was open for 0% -> 0% of each run, Pallas kernels for 6% -> 6%
where the time goes in v4:
time: 46.5 us; the launch traced here: 46.3 us
  starting transfers between devices  25.3 us (54%)
  waiting for transfers between devices  10.7 us (23%)
  Pallas kernels  7.55 us (16%)
  between operations  2.07 us (4%)
  local copies, waits for them, and re-layouts  0.75 us (2%)
    ppermute x17, starting transfers between devices, swap(): lax.ppermute(value, axis, [(i, i ^ step) for i in range(lax.axis_size(axi...  16.3 us
    ppermute x4, starting transfers between devices, local(): lax.ppermute(lax.dynamic_slice_in_dim(value, first, depth, 0), 'gz', ends...  9.02 us
    ppermute x17, waiting for transfers between devices, swap(): lax.ppermute(value, axis, [(i, i ^ step) for i in range(lax.axis_size(axi...  8.06 us
    pallas_call x1, Pallas kernels, shear_x(): pl.pallas_call(functools.partial(shear_x_kernel, classes), out_shape=[jax...  2.7 us
    ppermute x4, waiting for transfers between devices, local(): lax.ppermute(lax.dynamic_slice_in_dim(value, first, depth, 0), 'gz', ends...  2.59 us
    pallas_call x1, Pallas kernels, finish(): pl.pallas_call(functools.partial(finish_kernel, slots), out_shape=jax.Sha...  1.46 us
    pallas_call x2, Pallas kernels, shear_z(): pl.pallas_call(functools.partial(shear_z_kernel, plane_count, depth, chip...  1.04 us
    pallas_call x1, Pallas kernels, weights(): pl.pallas_call(functools.partial(weights_kernel, plane_count, depth, ny,...  0.95 us
  transfers between devices with their start and end apart: 21, of which 9 were waited for; matrix products, arithmetic and copies ran while one was open for 0% of the time, Pallas kernels for 6%

profile of v4, /device:TPU:0, one launch (start us, length us, event | category | flops | bytes accessed | tf_op | source)
XLA Modules:
  0.0 46.3 jit_solution(6247273235375052039)
XLA Ops:
  0.6 2.7 %shear_x.1 = (f32[40,16,128]{2,1,0:T(8,128)S(1)}, f32[40,16,128]{2,1,0:T(8,128)S(1)}) custom-call(s32[160]{0:T(256)} %shifts_hbm.1, f32[160]{0:T(256)} %fracs_hbm.1, f32[40,32,128]{2,1,0:T(8,128)} %bitcast.19), custom_call_target="tpu_custom_call" | custom-call | tf_op jit(solution)/shard_map/shear_x/pallas_call | solution.py:132
  3.4 0.7 %collective-permute-start.1 = (f32[36,16,128]{2,1,0:T(8,128)S(1)}, f32[36,16,128]{2,1,0:T(8,128)S(1)}, u32[]{:S(2)}, u32[]{:S(2)}) collective-permute-start(f32[36,16,128]{2,1,0:T(8,128)S(1)} %get-tuple-element.90), channel_id=1, source_target_pairs={{1,2},{2,1},{5,6},{6,5},{9,10},{10,9},{13,14},{14,13},{17,18},{18,... | collective-permute-start | bytes 884744 | tf_op jit(solution)/shard_map/ppermute | solution.py:559
  4.1 5.9 %collective-permute-start = (f32[36,16,128]{2,1,0:T(8,128)S(1)}, f32[36,16,128]{2,1,0:T(8,128)S(1)}, u32[]{:S(2)}, u32[]{:S(2)}) collective-permute-start(f32[36,16,128]{2,1,0:T(8,128)S(1)} %get-tuple-element.91), channel_id=1, source_target_pairs={{0,1},{1,0},{2,3},{3,2},{4,5},{5,4},{6,7},{7,6},{8,9},{9,8},{10,11... | collective-permute-start | bytes 884744 | tf_op jit(solution)/shard_map/ppermute | solution.py:559
  10.0 0.7 %collective-permute-start.7 = (f32[36,16,128]{2,1,0:T(8,128)S(1)}, f32[36,16,128]{2,1,0:T(8,128)S(1)}, u32[]{:S(2)}, u32[]{:S(2)}) collective-permute-start(f32[36,16,128]{2,1,0:T(8,128)S(1)} %get-tuple-element.88), channel_id=1, source_target_pairs={{1,2},{2,1},{5,6},{6,5},{9,10},{10,9},{13,14},{14,13},{17,18},{18,... | collective-permute-start | bytes 884744 | tf_op jit(solution)/shard_map/ppermute | solution.py:559
  10.7 1.8 %collective-permute-start.6 = (f32[36,16,128]{2,1,0:T(8,128)S(1)}, f32[36,16,128]{2,1,0:T(8,128)S(1)}, u32[]{:S(2)}, u32[]{:S(2)}) collective-permute-start(f32[36,16,128]{2,1,0:T(8,128)S(1)} %get-tuple-element.89), channel_id=1, source_target_pairs={{0,1},{1,0},{2,3},{3,2},{4,5},{5,4},{6,7},{7,6},{8,9},{9,8},{10,11... | collective-permute-start | bytes 884744 | tf_op jit(solution)/shard_map/ppermute | solution.py:559
  13.1 0.0 copy-start.1
  13.8 0.0 copy-start
  13.8 0.0 copy-start.2
  13.8 0.0 copy-done.1
  13.9 0.7 %copy-done = s32[512]{0:T(512)S(1)} copy-done((s32[512]{0:T(512)S(1)}, s32[512]{0:T(512)}, u32[]{:S(2)}) %copy-start) | copy-done | bytes 2072
  14.5 0.0 copy-done.2
  14.5 1.0 %weights.1 = (f32[40,112]{1,0:T(8,128)S(1)}, f32[64,128]{1,0:T(8,128)S(1)}, f32[40,40]{1,0:T(8,128)S(1)}) custom-call(s32[1]{0:T(128)S(6)} %copy.11.shift_ref, f32[1]{0:T(128)S(6)} %copy.12.frac_ref, s32[8]{0:T(128)S(1)} %copy-done.2, s32[1,512]{1,0:T(1,128)S(1)} %bitcast.17, f32[1,512]{1,0:T(1,128)S(1)} %bitcast.18), custom_call_target="tpu_custom_call" | custom-call | tf_op jit(solution)/shard_map/weights/pallas_call | solution.py:205
  15.5 0.0 collective-permute-done.1
  15.5 2.4 %collective-permute-done = f32[36,16,128]{2,1,0:T(8,128)S(1)} collective-permute-done((f32[36,16,128]{2,1,0:T(8,128)S(1)}, f32[36,16,128]{2,1,0:T(8,128)S(1)}, u32[]{:S(2)}, u32[]{:S(2)}) %collective-permute-start) | collective-permute-done | bytes 294944 | tf_op jit(solution)/shard_map/ppermute | solution.py:559
  17.9 0.5 %shear_z.2 = (f32[40,512]{1,0:T(8,128)S(1)}, f32[40,512]{1,0:T(8,128)S(1)}, f32[40,512]{1,0:T(8,128)S(1)}, f32[40,512]{1,0:T(8,128)S(1)}) custom-call(f32[40,112]{1,0:T(8,128)S(1)} %get-tuple-element.55.mixing_ref, f32[576,128]{1,0:T(8,128)S(1)} %bitcast.16, f32[640,128]{1,0:T(8,128)S(1)} %bitcast.12, f32[576,128]{1,0:T(8,128)S(1)} %bitcast.15), custom_call_target="tpu_custom_call" | custom-call | tf_op jit(solution)/shard_map/shear_z/pallas_call | solution.py:264
  18.4 2.5 %collective-permute-start.2 = (f32[40,512]{1,0:T(8,128)S(1)}, f32[40,512]{1,0:T(8,128)S(1)}, u32[]{:S(2)}, u32[]{:S(2)}) collective-permute-start(f32[40,512]{1,0:T(8,128)S(1)} %get-tuple-element.51), channel_id=1, source_target_pairs={{0,24},{4,28},{8,16},{12,20},{16,8},{20,12},{24,0},{28,4},{1,25},{... | collective-permute-start | bytes 245768 | tf_op jit(solution)/shard_map/ppermute | solution.py:524
  20.9 0.0 collective-permute-start.3
  20.9 0.5 %collective-permute-start.4 = (f32[40,512]{1,0:T(8,128)S(1)}, f32[40,512]{1,0:T(8,128)S(1)}, u32[]{:S(2)}, u32[]{:S(2)}) collective-permute-start(f32[40,512]{1,0:T(8,128)S(1)} %get-tuple-element.53), channel_id=1, source_target_pairs={{0,8},{4,12},{8,0},{12,4},{16,24},{20,28},{24,16},{28,20},{1,9},{5... | collective-permute-start | bytes 245768 | tf_op jit(solution)/shard_map/ppermute | solution.py:524
  21.4 0.0 collective-permute-done.7
  21.4 1.4 %collective-permute-start.5 = (f32[40,512]{1,0:T(8,128)S(1)}, f32[40,512]{1,0:T(8,128)S(1)}, u32[]{:S(2)}, u32[]{:S(2)}) collective-permute-start(f32[40,512]{1,0:T(8,128)S(1)} %get-tuple-element.54), channel_id=1, source_target_pairs={{0,12},{4,8},{8,4},{12,0},{16,28},{20,24},{24,20},{28,16},{1,13},{... | collective-permute-start | bytes 245768 | tf_op jit(solution)/shard_map/ppermute | solution.py:524
  22.9 0.2 collective-permute-done.6
  23.0 0.5 %shear_z.3 = (f32[40,512]{1,0:T(8,128)S(1)}, f32[40,512]{1,0:T(8,128)S(1)}, f32[40,512]{1,0:T(8,128)S(1)}, f32[40,512]{1,0:T(8,128)S(1)}) custom-call(f32[40,112]{1,0:T(8,128)S(1)} %get-tuple-element.55.mixing_ref, f32[576,128]{1,0:T(8,128)S(1)} %bitcast.14, f32[640,128]{1,0:T(8,128)S(1)} %bitcast.11, f32[576,128]{1,0:T(8,128)S(1)} %bitcast.13), custom_call_target="tpu_custom_call" | custom-call | tf_op jit(solution)/shard_map/shear_z/pallas_call | solution.py:264
  23.6 1.6 %collective-permute-start.8 = (f32[40,512]{1,0:T(8,128)S(1)}, f32[40,512]{1,0:T(8,128)S(1)}, u32[]{:S(2)}, u32[]{:S(2)}) collective-permute-start(f32[40,512]{1,0:T(8,128)S(1)} %get-tuple-element.61), channel_id=1, source_target_pairs={{0,16},{4,20},{8,24},{12,28},{16,0},{20,4},{24,8},{28,12},{1,17},{... | collective-permute-start | bytes 245768 | tf_op jit(solution)/shard_map/ppermute | solution.py:524
  25.1 0.0 collective-permute-done.2.refs_0_
  25.1 0.0 collective-permute-start.9
  25.2 1.4 %collective-permute-done.3.refs_1_ = f32[40,512]{1,0:T(8,128)S(1)} collective-permute-done((f32[40,512]{1,0:T(8,128)S(1)}, f32[40,512]{1,0:T(8,128)S(1)}, u32[]{:S(2)}, u32[]{:S(2)}) %collective-permute-start.3) | collective-permute-done | bytes 81952 | tf_op jit(solution)/shard_map/ppermute | solution.py:524
  26.5 0.0 collective-permute-start.10
  26.5 0.9 %collective-permute-done.4.refs_2_ = f32[40,512]{1,0:T(8,128)S(1)} collective-permute-done((f32[40,512]{1,0:T(8,128)S(1)}, f32[40,512]{1,0:T(8,128)S(1)}, u32[]{:S(2)}, u32[]{:S(2)}) %collective-permute-start.4) | collective-permute-done | bytes 81952 | tf_op jit(solution)/shard_map/ppermute | solution.py:524
  27.4 1.7 %collective-permute-done.5.refs_3_ = f32[40,512]{1,0:T(8,128)S(1)} collective-permute-done((f32[40,512]{1,0:T(8,128)S(1)}, f32[40,512]{1,0:T(8,128)S(1)}, u32[]{:S(2)}, u32[]{:S(2)}) %collective-permute-start.5) | collective-permute-done | bytes 81952 | tf_op jit(solution)/shard_map/ppermute | solution.py:524
  29.1 0.0 collective-permute-done.8.refs_4_
  29.1 0.8 %collective-permute-done.9.refs_5_ = f32[40,512]{1,0:T(8,128)S(1)} collective-permute-done((f32[40,512]{1,0:T(8,128)S(1)}, f32[40,512]{1,0:T(8,128)S(1)}, u32[]{:S(2)}, u32[]{:S(2)}) %collective-permute-start.9) | collective-permute-done | bytes 81952 | tf_op jit(solution)/shard_map/ppermute | solution.py:524
  29.9 0.0 collective-permute-done.10.refs_7_
  29.9 0.4 shear_y.1
  30.3 1.5 %collective-permute-start.12 = (f32[2,40,512]{2,1,0:T(8,128)S(1)}, f32[2,40,512]{2,1,0:T(8,128)S(1)}, u32[]{:S(2)}, u32[]{:S(2)}) collective-permute-start(f32[2,40,512]{2,1,0:T(8,128)S(1)} %get-tuple-element.67.refs_2_), channel_id=1, source_target_pairs={{0,8},{4,12},{8,0},{12,4},{16,24},{20,28},{24,16},{28,20},{1,9},{5... | collective-permute-start | bytes 491528 | tf_op jit(solution)/shard_map/ppermute | solution.py:524
  31.8 1.0 %collective-permute-start.13 = (f32[2,40,512]{2,1,0:T(8,128)S(1)}, f32[2,40,512]{2,1,0:T(8,128)S(1)}, u32[]{:S(2)}, u32[]{:S(2)}) collective-permute-start(f32[2,40,512]{2,1,0:T(8,128)S(1)} %get-tuple-element.68.refs_3_), channel_id=1, source_target_pairs={{0,16},{4,20},{8,24},{12,28},{16,0},{20,4},{24,8},{28,12},{1,17},{... | collective-permute-start | bytes 491528 | tf_op jit(solution)/shard_map/ppermute | solution.py:524
  32.8 0.3 project.1
  33.2 1.4 %collective-permute-start.14 = (f32[2,8,512]{2,1,0:T(8,128)S(1)}, f32[2,8,512]{2,1,0:T(8,128)S(1)}, u32[]{:S(2)}, u32[]{:S(2)}) collective-permute-start(f32[2,8,512]{2,1,0:T(8,128)S(1)} %get-tuple-element.72), channel_id=1, source_target_pairs={{0,3},{1,2},{2,1},{3,0},{4,7},{5,6},{6,5},{7,4},{8,11},{9,10},{10,... | collective-permute-start | bytes 98312 | tf_op jit(solution)/shard_map/ppermute | solution.py:524
  34.6 2.2 %collective-permute-start.15 = (f32[2,8,512]{2,1,0:T(8,128)S(1)}, f32[2,8,512]{2,1,0:T(8,128)S(1)}, u32[]{:S(2)}, u32[]{:S(2)}) collective-permute-start(f32[2,8,512]{2,1,0:T(8,128)S(1)} %get-tuple-element.73), channel_id=1, source_target_pairs={{0,2},{1,3},{2,0},{3,1},{4,6},{5,7},{6,4},{7,5},{8,10},{9,11},{10,... | collective-permute-start | bytes 98312 | tf_op jit(solution)/shard_map/ppermute | solution.py:524
  36.8 0.8 %collective-permute-start.16 = (f32[2,8,512]{2,1,0:T(8,128)S(1)}, f32[2,8,512]{2,1,0:T(8,128)S(1)}, u32[]{:S(2)}, u32[]{:S(2)}) collective-permute-start(f32[2,8,512]{2,1,0:T(8,128)S(1)} %get-tuple-element.74), channel_id=1, source_target_pairs={{0,1},{1,0},{2,3},{3,2},{4,5},{5,4},{6,7},{7,6},{8,9},{9,8},{10,11... | collective-permute-start | bytes 98312 | tf_op jit(solution)/shard_map/ppermute | solution.py:524
  37.6 0.0 collective-permute-done.12.refs_0_.refs_2_
  37.6 1.0 %collective-permute-start.17 = (f32[40,512]{1,0:T(8,128)S(1)}, f32[40,512]{1,0:T(8,128)S(1)}, u32[]{:S(2)}, u32[]{:S(2)}) collective-permute-start(f32[40,512]{1,0:T(8,128)S(1)} %get-tuple-element.70.refs_4_), channel_id=1, source_target_pairs={{0,24},{4,28},{8,16},{12,20},{16,8},{20,12},{24,0},{28,4},{1,25},{... | collective-permute-start | bytes 245768 | tf_op jit(solution)/shard_map/ppermute | solution.py:524
  38.7 0.0 collective-permute-done.13.refs_1_.refs_3_
  38.7 0.1 collective-permute-start.18
  38.8 0.4 collective-permute-done.14.refs_0_
  39.2 1.6 %collective-permute-start.19 = (f32[40,512]{1,0:T(8,128)S(1)}, f32[40,512]{1,0:T(8,128)S(1)}, u32[]{:S(2)}, u32[]{:S(2)}) collective-permute-start(f32[40,512]{1,0:T(8,128)S(1)} %get-tuple-element.76), channel_id=1, source_target_pairs={{0,4},{4,0},{8,12},{12,8},{16,20},{20,16},{24,28},{28,24},{1,5},{5... | collective-permute-start | bytes 245768 | tf_op jit(solution)/shard_map/ppermute | solution.py:524
  40.8 0.0 collective-permute-done.15.refs_1_
  40.8 0.1 collective-permute-start.20
  40.8 0.0 collective-permute-done.16.refs_2_
  40.8 0.4 collective-permute-start.11
  41.3 2.2 %collective-permute-done.17.refs_6_ = f32[40,512]{1,0:T(8,128)S(1)} collective-permute-done((f32[40,512]{1,0:T(8,128)S(1)}, f32[40,512]{1,0:T(8,128)S(1)}, u32[]{:S(2)}, u32[]{:S(2)}) %collective-permute-start.17) | collective-permute-done | bytes 81952 | tf_op jit(solution)/shard_map/ppermute | solution.py:524
  43.4 0.8 %collective-permute-done.18.refs_7_ = f32[40,512]{1,0:T(8,128)S(1)} collective-permute-done((f32[40,512]{1,0:T(8,128)S(1)}, f32[40,512]{1,0:T(8,128)S(1)}, u32[]{:S(2)}, u32[]{:S(2)}) %collective-permute-start.18) | collective-permute-done | bytes 81952 | tf_op jit(solution)/shard_map/ppermute | solution.py:524
  44.2 0.0 collective-permute-done.19.refs_4_
  44.2 0.0 collective-permute-done.20.refs_5_
  44.2 0.6 %add_shares.1 = f32[2,8,512]{2,1,0:T(8,128)} custom-call(f32[2,8,512]{2,1,0:T(8,128)S(1)} %collective-permute-done.14.refs_0_, f32[2,8,512]{2,1,0:T(8,128)S(1)} %collective-permute-done.15.refs_1_, f32[2,8,512]{2,1,0:T(8,128)S(1)} %collective-permute-done.16.refs_2_, f32[2,8,512]{2,1,0:T(8,128)S(1)} %get-tuple-element.85.refs_3_), custom_call_target="tpu_custom_call" | custom-call | tf_op jit(solution)/shard_map/add_shares/pallas_call | solution.py:444
  44.9 0.0 collective-permute-done.11.refs_1_
  44.9 1.5 %finish.1 = f32[1280,128]{1,0:T(8,128)} custom-call(f32[40,512]{1,0:T(8,128)S(1)} %get-tuple-element.65.refs_0_, f32[40,512]{1,0:T(8,128)S(1)} %collective-permute-done.11.refs_1_, f32[2,40,512]{2,1,0:T(8,128)S(1)} %collective-permute-done.12.refs_0_.refs_2_, f32[2,40,512]{2,1,0:T(8,128)S(1)} %collective-permute-done.13.refs_1_.refs_3_, ...), custom_call_target="tpu_custom_call" | custom-call | tf_op jit(solution)/shard_map/finish/pallas_call | solution.py:424
  (3 shorter events, 0.1 us)
Async XLA Ops:
  3.4 12.1 %collective-permute-start.1 = (f32[36,16,128]{2,1,0:T(8,128)S(1)}, f32[36,16,128]{2,1,0:T(8,128)S(1)}, u32[]{:S(2)}, u32[]{:S(2)}) collective-permute-start(f32[36,16,128]{2,1,0:T(8,128)S(1)} %get-tuple-element.90), channel_id=1, source_target_pairs={{1,2},{2,1},{5,6},{6,5},{9,10},{10,9},{13,14},{14,13},{17,18},{18,... | collective-permute-start | bytes 884744 | tf_op jit(solution)/shard_map/ppermute | solution.py:559
  4.1 13.8 %collective-permute-start = (f32[36,16,128]{2,1,0:T(8,128)S(1)}, f32[36,16,128]{2,1,0:T(8,128)S(1)}, u32[]{:S(2)}, u32[]{:S(2)}) collective-permute-start(f32[36,16,128]{2,1,0:T(8,128)S(1)} %get-tuple-element.91), channel_id=1, source_target_pairs={{0,1},{1,0},{2,3},{3,2},{4,5},{5,4},{6,7},{7,6},{8,9},{9,8},{10,11... | collective-permute-start | bytes 884744 | tf_op jit(solution)/shard_map/ppermute | solution.py:559
  10.0 11.4 %collective-permute-start.7 = (f32[36,16,128]{2,1,0:T(8,128)S(1)}, f32[36,16,128]{2,1,0:T(8,128)S(1)}, u32[]{:S(2)}, u32[]{:S(2)}) collective-permute-start(f32[36,16,128]{2,1,0:T(8,128)S(1)} %get-tuple-element.88), channel_id=1, source_target_pairs={{1,2},{2,1},{5,6},{6,5},{9,10},{10,9},{13,14},{14,13},{17,18},{18,... | collective-permute-start | bytes 884744 | tf_op jit(solution)/shard_map/ppermute | solution.py:559
  10.7 12.3 %collective-permute-start.6 = (f32[36,16,128]{2,1,0:T(8,128)S(1)}, f32[36,16,128]{2,1,0:T(8,128)S(1)}, u32[]{:S(2)}, u32[]{:S(2)}) collective-permute-start(f32[36,16,128]{2,1,0:T(8,128)S(1)} %get-tuple-element.89), channel_id=1, source_target_pairs={{0,1},{1,0},{2,3},{3,2},{4,5},{5,4},{6,7},{7,6},{8,9},{9,8},{10,11... | collective-permute-start | bytes 884744 | tf_op jit(solution)/shard_map/ppermute | solution.py:559
  13.1 0.7 %copy-start.1 = (f32[512]{0:T(512)S(1)}, f32[512]{0:T(512)}, u32[]{:S(2)}) copy-start(f32[512]{0:T(512)} %param.14) | copy-start | bytes 6148
  13.8 0.7 %copy-start = (s32[512]{0:T(512)S(1)}, s32[512]{0:T(512)}, u32[]{:S(2)}) copy-start(s32[512]{0:T(512)} %param.13) | copy-start | bytes 6148
  13.8 0.7 %copy-start.2 = (s32[8]{0:T(128)S(1)}, s32[8]{0:T(128)}, u32[]{:S(2)}) copy-start(s32[8]{0:T(128)} %slopes_ref.1) | copy-start | bytes 100
  18.4 6.8 %collective-permute-start.2 = (f32[40,512]{1,0:T(8,128)S(1)}, f32[40,512]{1,0:T(8,128)S(1)}, u32[]{:S(2)}, u32[]{:S(2)}) collective-permute-start(f32[40,512]{1,0:T(8,128)S(1)} %get-tuple-element.51), channel_id=1, source_target_pairs={{0,24},{4,28},{8,16},{12,20},{16,8},{20,12},{24,0},{28,4},{1,25},{... | collective-permute-start | bytes 245768 | tf_op jit(solution)/shard_map/ppermute | solution.py:524
  20.9 5.6 %collective-permute-start.3 = (f32[40,512]{1,0:T(8,128)S(1)}, f32[40,512]{1,0:T(8,128)S(1)}, u32[]{:S(2)}, u32[]{:S(2)}) collective-permute-start(f32[40,512]{1,0:T(8,128)S(1)} %get-tuple-element.52), channel_id=1, source_target_pairs={{0,28},{4,24},{8,20},{12,16},{16,12},{20,8},{24,4},{28,0},{1,29},{... | collective-permute-start | bytes 245768 | tf_op jit(solution)/shard_map/ppermute | solution.py:524
  20.9 6.5 %collective-permute-start.4 = (f32[40,512]{1,0:T(8,128)S(1)}, f32[40,512]{1,0:T(8,128)S(1)}, u32[]{:S(2)}, u32[]{:S(2)}) collective-permute-start(f32[40,512]{1,0:T(8,128)S(1)} %get-tuple-element.53), channel_id=1, source_target_pairs={{0,8},{4,12},{8,0},{12,4},{16,24},{20,28},{24,16},{28,20},{1,9},{5... | collective-permute-start | bytes 245768 | tf_op jit(solution)/shard_map/ppermute | solution.py:524
  21.4 7.6 %collective-permute-start.5 = (f32[40,512]{1,0:T(8,128)S(1)}, f32[40,512]{1,0:T(8,128)S(1)}, u32[]{:S(2)}, u32[]{:S(2)}) collective-permute-start(f32[40,512]{1,0:T(8,128)S(1)} %get-tuple-element.54), channel_id=1, source_target_pairs={{0,12},{4,8},{8,4},{12,0},{16,28},{20,24},{24,20},{28,16},{1,13},{... | collective-permute-start | bytes 245768 | tf_op jit(solution)/shard_map/ppermute | solution.py:524
  23.6 5.5 %collective-permute-start.8 = (f32[40,512]{1,0:T(8,128)S(1)}, f32[40,512]{1,0:T(8,128)S(1)}, u32[]{:S(2)}, u32[]{:S(2)}) collective-permute-start(f32[40,512]{1,0:T(8,128)S(1)} %get-tuple-element.61), channel_id=1, source_target_pairs={{0,16},{4,20},{8,24},{12,28},{16,0},{20,4},{24,8},{28,12},{1,17},{... | collective-permute-start | bytes 245768 | tf_op jit(solution)/shard_map/ppermute | solution.py:524
  25.1 4.7 %collective-permute-start.9 = (f32[40,512]{1,0:T(8,128)S(1)}, f32[40,512]{1,0:T(8,128)S(1)}, u32[]{:S(2)}, u32[]{:S(2)}) collective-permute-start(f32[40,512]{1,0:T(8,128)S(1)} %get-tuple-element.62), channel_id=1, source_target_pairs={{0,20},{4,16},{8,28},{12,24},{16,4},{20,0},{24,12},{28,8},{1,21},{... | collective-permute-start | bytes 245768 | tf_op jit(solution)/shard_map/ppermute | solution.py:524
  26.5 3.3 %collective-permute-start.10 = (f32[40,512]{1,0:T(8,128)S(1)}, f32[40,512]{1,0:T(8,128)S(1)}, u32[]{:S(2)}, u32[]{:S(2)}) collective-permute-start(f32[40,512]{1,0:T(8,128)S(1)} %get-tuple-element.64), channel_id=1, source_target_pairs={{0,4},{4,0},{8,12},{12,8},{16,20},{20,16},{24,28},{28,24},{1,5},{5... | collective-permute-start | bytes 245768 | tf_op jit(solution)/shard_map/ppermute | solution.py:524
  30.3 7.3 %collective-permute-start.12 = (f32[2,40,512]{2,1,0:T(8,128)S(1)}, f32[2,40,512]{2,1,0:T(8,128)S(1)}, u32[]{:S(2)}, u32[]{:S(2)}) collective-permute-start(f32[2,40,512]{2,1,0:T(8,128)S(1)} %get-tuple-element.67.refs_2_), channel_id=1, source_target_pairs={{0,8},{4,12},{8,0},{12,4},{16,24},{20,28},{24,16},{28,20},{1,9},{5... | collective-permute-start | bytes 491528 | tf_op jit(solution)/shard_map/ppermute | solution.py:524
  31.8 6.9 %collective-permute-start.13 = (f32[2,40,512]{2,1,0:T(8,128)S(1)}, f32[2,40,512]{2,1,0:T(8,128)S(1)}, u32[]{:S(2)}, u32[]{:S(2)}) collective-permute-start(f32[2,40,512]{2,1,0:T(8,128)S(1)} %get-tuple-element.68.refs_3_), channel_id=1, source_target_pairs={{0,16},{4,20},{8,24},{12,28},{16,0},{20,4},{24,8},{28,12},{1,17},{... | collective-permute-start | bytes 491528 | tf_op jit(solution)/shard_map/ppermute | solution.py:524
  33.2 6.0 %collective-permute-start.14 = (f32[2,8,512]{2,1,0:T(8,128)S(1)}, f32[2,8,512]{2,1,0:T(8,128)S(1)}, u32[]{:S(2)}, u32[]{:S(2)}) collective-permute-start(f32[2,8,512]{2,1,0:T(8,128)S(1)} %get-tuple-element.72), channel_id=1, source_target_pairs={{0,3},{1,2},{2,1},{3,0},{4,7},{5,6},{6,5},{7,4},{8,11},{9,10},{10,... | collective-permute-start | bytes 98312 | tf_op jit(solution)/shard_map/ppermute | solution.py:524
  34.6 6.2 %collective-permute-start.15 = (f32[2,8,512]{2,1,0:T(8,128)S(1)}, f32[2,8,512]{2,1,0:T(8,128)S(1)}, u32[]{:S(2)}, u32[]{:S(2)}) collective-permute-start(f32[2,8,512]{2,1,0:T(8,128)S(1)} %get-tuple-element.73), channel_id=1, source_target_pairs={{0,2},{1,3},{2,0},{3,1},{4,6},{5,7},{6,4},{7,5},{8,10},{9,11},{10,... | collective-permute-start | bytes 98312 | tf_op jit(solution)/shard_map/ppermute | solution.py:524
  36.8 4.1 %collective-permute-start.16 = (f32[2,8,512]{2,1,0:T(8,128)S(1)}, f32[2,8,512]{2,1,0:T(8,128)S(1)}, u32[]{:S(2)}, u32[]{:S(2)}) collective-permute-start(f32[2,8,512]{2,1,0:T(8,128)S(1)} %get-tuple-element.74), channel_id=1, source_target_pairs={{0,1},{1,0},{2,3},{3,2},{4,5},{5,4},{6,7},{7,6},{8,9},{9,8},{10,11... | collective-permute-start | bytes 98312 | tf_op jit(solution)/shard_map/ppermute | solution.py:524
  37.6 5.8 %collective-permute-start.17 = (f32[40,512]{1,0:T(8,128)S(1)}, f32[40,512]{1,0:T(8,128)S(1)}, u32[]{:S(2)}, u32[]{:S(2)}) collective-permute-start(f32[40,512]{1,0:T(8,128)S(1)} %get-tuple-element.70.refs_4_), channel_id=1, source_target_pairs={{0,24},{4,28},{8,16},{12,20},{16,8},{20,12},{24,0},{28,4},{1,25},{... | collective-permute-start | bytes 245768 | tf_op jit(solution)/shard_map/ppermute | solution.py:524
  38.7 5.6 %collective-permute-start.18 = (f32[40,512]{1,0:T(8,128)S(1)}, f32[40,512]{1,0:T(8,128)S(1)}, u32[]{:S(2)}, u32[]{:S(2)}) collective-permute-start(f32[40,512]{1,0:T(8,128)S(1)} %get-tuple-element.71.refs_5_), channel_id=1, source_target_pairs={{0,28},{4,24},{8,20},{12,16},{16,12},{20,8},{24,4},{28,0},{1,29},{... | collective-permute-start | bytes 245768 | tf_op jit(solution)/shard_map/ppermute | solution.py:524
  39.2 5.1 %collective-permute-start.19 = (f32[40,512]{1,0:T(8,128)S(1)}, f32[40,512]{1,0:T(8,128)S(1)}, u32[]{:S(2)}, u32[]{:S(2)}) collective-permute-start(f32[40,512]{1,0:T(8,128)S(1)} %get-tuple-element.76), channel_id=1, source_target_pairs={{0,4},{4,0},{8,12},{12,8},{16,20},{20,16},{24,28},{28,24},{1,5},{5... | collective-permute-start | bytes 245768 | tf_op jit(solution)/shard_map/ppermute | solution.py:524
  40.8 3.5 %collective-permute-start.20 = (f32[40,512]{1,0:T(8,128)S(1)}, f32[40,512]{1,0:T(8,128)S(1)}, u32[]{:S(2)}, u32[]{:S(2)}) collective-permute-start(f32[40,512]{1,0:T(8,128)S(1)} %get-tuple-element.77), channel_id=1, source_target_pairs={{0,4},{4,0},{8,12},{12,8},{16,20},{20,16},{24,28},{28,24},{1,5},{5... | collective-permute-start | bytes 245768 | tf_op jit(solution)/shard_map/ppermute | solution.py:524
  40.8 4.0 %collective-permute-start.11 = (f32[40,512]{1,0:T(8,128)S(1)}, f32[40,512]{1,0:T(8,128)S(1)}, u32[]{:S(2)}, u32[]{:S(2)}) collective-permute-start(f32[40,512]{1,0:T(8,128)S(1)} %get-tuple-element.66.refs_1_), channel_id=1, source_target_pairs={{0,4},{4,0},{8,12},{12,8},{16,20},{20,16},{24,28},{28,24},{1,5},{5... | collective-permute-start | bytes 245768 | tf_op jit(solution)/shard_map/ppermute | solution.py:524

commit v5 on v4

--- a/solution.py
+++ b/solution.py
@@ -280,7 +280,8 @@
     in_refs = [in_refs[start_order(ny).index(slot)] for slot in range(ny)]
     plane_count, width = in_refs[0].shape
     row = lax.axis_index("gy")
-    for tile in range(width // LANES):
+    tiles = width // LANES
+    for tile in range(tiles):
         lanes = slice(tile * LANES, (tile + 1) * LANES)
         first = tile * 2 * ny + ny - 1
         for target in range(ny):
@@ -295,17 +296,19 @@
                 value = weight[0] * in_refs[0][planes, lanes]
                 for source in range(1, ny):
                     value = value + weight[source] * in_refs[source][planes, lanes]
+                lines = pl.ds(block * 8 * tiles + tile, 8, stride=tiles)
                 if target < 2:
-                    out_refs[target][planes, lanes] = value
+                    out_refs[target][lines, :] = value
                 elif target < ny - 2:
-                    out_refs[target // 2 + 1][target % 2, planes, lanes] = value
+                    out_refs[target // 2 + 1][target % 2, lines, :] = value
                 else:
-                    out_refs[target - ny][planes, lanes] = value
+                    out_refs[target - ny][lines, :] = value
 
 
 def shear_y(taps, columns):
     ny = len(columns)
-    shape = columns[0].shape
+    plane_count, width = columns[0].shape
+    shape = (plane_count * width // LANES, LANES)
     single = [jax.ShapeDtypeStruct(shape, jnp.float32)] * 2
     out_shape = single + [jax.ShapeDtypeStruct((2, *shape), jnp.float32)] * (ny // 2 - 2) + single
     return pl.pallas_call(
@@ -339,10 +342,10 @@
     place, own_row = lax.axis_index("gz"), lax.axis_index("gy")
     in_refs, share_refs, totals_ref = refs[:chips + 2], refs[chips + 2:-1], refs[-1]
     ny, shares = 2 * chips, len(share_refs)
-    plane_count, width = in_refs[0].shape
+    plane_count = chosen_ref.shape[1]
     total_planes = plane_count * shares
     span = ny // 4
-    tiles = width // LANES
+    tiles = in_refs[0].shape[0] // plane_count
     lifts = 2 * span + 1
     chosen = chosen_ref[...].astype(jnp.bfloat16)
     chosen = jnp.concatenate([chosen, chosen], axis=1)
@@ -351,11 +354,14 @@
     totals_ref[...] = jnp.zeros(totals_ref.shape, jnp.float32)
     for source in range(ny):
         if source < 2:
-            value = in_refs[source][...]
+            ref = in_refs[source]
         elif source < ny - 2:
-            value = in_refs[source // 2 + 1][source % 2]
+            ref = in_refs[source // 2 + 1].at[source % 2]
         else:
-            value = in_refs[source - ny][...]
+            ref = in_refs[source - ny]
+        value = jnp.concatenate(
+            [ref[pl.ds(tile, plane_count, stride=tiles), :] for tile in range(tiles)], axis=1
+        )
         sums = jnp.dot(
             chosen,
             jnp.concatenate(split_high_low(value), axis=0),
@@ -385,7 +391,7 @@
     chips = len(rotated) - 2
     ny = 2 * chips
     tilts = chosen.shape[0] // (2 * (ny // 4) + 1)
-    width = rotated[0].shape[1]
+    width = rotated[0].shape[0] // chosen.shape[1] * LANES
     share = jax.ShapeDtypeStruct((tilts // shares, ny, width), jnp.float32)
     totals = (width // LANES * (ny + 2 * (ny // 4)) * tilts, LANES)
     return pl.pallas_call(
@@ -400,55 +406,48 @@
 
 
 def finish_kernel(slots, *refs):
+    sources, share_refs = refs[:len(slots)], refs[len(slots):-3]
+    rotated_ref, projections_ref, sems = refs[-3:]
     row = lax.axis_index("gy")
-    rotated_ref, sources = refs[-1], refs[:len(slots)]
-    rows = rotated_ref.shape[0] // sources[0].shape[-2]
-    for ref, (slot, index) in zip(sources, slots):
-        plane_count, width = ref.shape[-2:]
-        per_group = width // LANES
-        start = (row ^ slot) * per_group
-        source = ref if index is None else ref.at[index]
-        for tile in range(per_group):
-            rotated_ref[pl.ds(start + tile, plane_count, stride=rows), :] = source[
-                :, tile * LANES:(tile + 1) * LANES
-            ]
-
-
-def finish(own, early, landed, late, direct):
+    copies = [
+        pltpu.make_async_copy(
+            ref if index is None else ref.at[index], rotated_ref.at[:, row ^ slot], sems.at[slot]
+        )
+        for ref, (slot, index) in zip(sources, slots)
+    ]
+    for copy in copies:
+        copy.start()
+    total = share_refs[0][...]
+    for share_ref in share_refs[1:]:
+        total = total + share_ref[...]
+    projections_ref[...] = total
+    for copy in copies:
+        copy.wait()
+
+
+def finish(own, early, landed, late, direct, shares, plane_count):
     chips = len(landed) + 2
-    plane_count, width = own.shape
     slots = [(0, None), (1, None)]
     slots += [(2 * step, 0) for step in range(1, chips - 1)]
     slots += [(2 * step + 1, None) for step in range(1, chips - 1)]
     slots += [(2 * chips - 2, None), (2 * chips - 1, None)]
+    tiles = own.shape[0] // plane_count
+    sources = [
+        value.reshape(*value.shape[:-2], plane_count, tiles, LANES)
+        for value in (own, early, *landed, *late, *direct)
+    ]
     return pl.pallas_call(
         functools.partial(finish_kernel, slots),
-        out_shape=jax.ShapeDtypeStruct(
-            (plane_count * 2 * chips * width // LANES, LANES), jnp.float32
+        out_shape=(
+            jax.ShapeDtypeStruct((plane_count, 2 * chips, tiles, LANES), jnp.float32),
+            jax.ShapeDtypeStruct(shares[0].shape, jnp.float32),
         ),
-        in_specs=[VMEM_SPEC] * len(slots),
-        out_specs=VMEM_SPEC,
+        in_specs=[VMEM_SPEC] * (len(slots) + len(shares)),
+        out_specs=(pl.BlockSpec(memory_space=pltpu.HBM), VMEM_SPEC),
+        scratch_shapes=[pltpu.SemaphoreType.DMA((2 * chips,))],
         compiler_params=pltpu.CompilerParams(vmem_limit_bytes=VMEM_LIMIT),
         name="finish",
-    )(own, early, *landed, *late, *direct)
-
-
-def add_kernel(*refs):
-    total = refs[0][...]
-    for ref in refs[1:-1]:
-        total = total + ref[...]
-    refs[-1][...] = total
-
-
-def add(shares):
-    return pl.pallas_call(
-        add_kernel,
-        out_shape=jax.ShapeDtypeStruct(shares[0].shape, jnp.float32),
-        in_specs=[VMEM_SPEC] * len(shares),
-        out_specs=VMEM_SPEC,
-        compiler_params=pltpu.CompilerParams(vmem_limit_bytes=VMEM_LIMIT),
-        name="add_shares",
-    )(*shares)
+    )(*sources, *shares)
 
 
 def with_halo(value, sides, width):
@@ -573,10 +572,10 @@
     tilted = [swap(tilted[step], "gz", step) for step in range(shares - 1, 0, -1)] + [tilted[0]]
     late = [swap(value, "gy", 1) for value in collect(landed)]
     tilted, direct, late = lax.optimization_barrier((tilted, direct, late))
-    rotated = finish(own, early, landed, late, direct)
+    rotated, projections = finish(own, early, landed, late, direct, tilted, plane_count)
     return (
         rotated.reshape(plane_count, row_local, width_all),
-        jnp.swapaxes(add(tilted), 1, 2),
+        jnp.swapaxes(projections, 1, 2),
     )
 
 

time: 46.5 us -> 46 us (0.989)
  Pallas kernels: 7.55 us -> 6.98 us
    pallas_call x2 -> x1, Pallas kernels: 2.09 us -> 1.52 us  [finish(): pl.pallas_call(functools.partial(finish_kernel, slots), out_shape=(jax.Sh...]
  transfers between devices with their start and end apart: 21 -> 21, of which waited for: 9 -> 9; matrix products, arithmetic and copies ran while one was open for 0% -> 0% of each run, Pallas kernels for 6% -> 5%
where the time goes in v5:
time: 46 us; the launch traced here: 45.8 us
  starting transfers between devices  25.3 us (55%)
  waiting for transfers between devices  10.7 us (23%)
  Pallas kernels  6.98 us (15%)
  between operations  2.07 us (4%)
  local copies, waits for them, and re-layouts  0.75 us (2%)
    ppermute x17, starting transfers between devices, swap(): lax.ppermute(value, axis, [(i, i ^ step) for i in range(lax.axis_size(axi...  16.3 us
    ppermute x4, starting transfers between devices, local(): lax.ppermute(lax.dynamic_slice_in_dim(value, first, depth, 0), 'gz', ends...  9.02 us
    ppermute x17, waiting for transfers between devices, swap(): lax.ppermute(value, axis, [(i, i ^ step) for i in range(lax.axis_size(axi...  8.06 us
    pallas_call x1, Pallas kernels, shear_x(): pl.pallas_call(functools.partial(shear_x_kernel, classes), out_shape=[jax...  2.7 us
    ppermute x4, waiting for transfers between devices, local(): lax.ppermute(lax.dynamic_slice_in_dim(value, first, depth, 0), 'gz', ends...  2.59 us
    pallas_call x1, Pallas kernels, finish(): pl.pallas_call(functools.partial(finish_kernel, slots), out_shape=(jax.Sh...  1.52 us
    pallas_call x2, Pallas kernels, shear_z(): pl.pallas_call(functools.partial(shear_z_kernel, plane_count, depth, chip...  1.04 us
    pallas_call x1, Pallas kernels, weights(): pl.pallas_call(functools.partial(weights_kernel, plane_count, depth, ny,...  0.95 us
  transfers between devices with their start and end apart: 21, of which 9 were waited for; matrix products, arithmetic and copies ran while one was open for 0% of the time, Pallas kernels for 5%

profile of v5, /device:TPU:0, one launch (start us, length us, event | category | flops | bytes accessed | tf_op | source)
XLA Modules:
  0.0 45.8 jit_solution(16069464810606087655)
XLA Ops:
  0.6 2.7 %shear_x.1 = (f32[40,16,128]{2,1,0:T(8,128)S(1)}, f32[40,16,128]{2,1,0:T(8,128)S(1)}) custom-call(s32[160]{0:T(256)} %shifts_hbm.1, f32[160]{0:T(256)} %fracs_hbm.1, f32[40,32,128]{2,1,0:T(8,128)} %bitcast.35), custom_call_target="tpu_custom_call" | custom-call | tf_op jit(solution)/shard_map/shear_x/pallas_call | solution.py:132
  3.4 0.7 %collective-permute-start.1 = (f32[36,16,128]{2,1,0:T(8,128)S(1)}, f32[36,16,128]{2,1,0:T(8,128)S(1)}, u32[]{:S(2)}, u32[]{:S(2)}) collective-permute-start(f32[36,16,128]{2,1,0:T(8,128)S(1)} %get-tuple-element.94), channel_id=1, source_target_pairs={{1,2},{2,1},{5,6},{6,5},{9,10},{10,9},{13,14},{14,13},{17,18},{18,... | collective-permute-start | bytes 884744 | tf_op jit(solution)/shard_map/ppermute | solution.py:558
  4.1 5.9 %collective-permute-start = (f32[36,16,128]{2,1,0:T(8,128)S(1)}, f32[36,16,128]{2,1,0:T(8,128)S(1)}, u32[]{:S(2)}, u32[]{:S(2)}) collective-permute-start(f32[36,16,128]{2,1,0:T(8,128)S(1)} %get-tuple-element.95), channel_id=1, source_target_pairs={{0,1},{1,0},{2,3},{3,2},{4,5},{5,4},{6,7},{7,6},{8,9},{9,8},{10,11... | collective-permute-start | bytes 884744 | tf_op jit(solution)/shard_map/ppermute | solution.py:558
  10.0 0.7 %collective-permute-start.7 = (f32[36,16,128]{2,1,0:T(8,128)S(1)}, f32[36,16,128]{2,1,0:T(8,128)S(1)}, u32[]{:S(2)}, u32[]{:S(2)}) collective-permute-start(f32[36,16,128]{2,1,0:T(8,128)S(1)} %get-tuple-element.92), channel_id=1, source_target_pairs={{1,2},{2,1},{5,6},{6,5},{9,10},{10,9},{13,14},{14,13},{17,18},{18,... | collective-permute-start | bytes 884744 | tf_op jit(solution)/shard_map/ppermute | solution.py:558
  10.7 1.8 %collective-permute-start.6 = (f32[36,16,128]{2,1,0:T(8,128)S(1)}, f32[36,16,128]{2,1,0:T(8,128)S(1)}, u32[]{:S(2)}, u32[]{:S(2)}) collective-permute-start(f32[36,16,128]{2,1,0:T(8,128)S(1)} %get-tuple-element.93), channel_id=1, source_target_pairs={{0,1},{1,0},{2,3},{3,2},{4,5},{5,4},{6,7},{7,6},{8,9},{9,8},{10,11... | collective-permute-start | bytes 884744 | tf_op jit(solution)/shard_map/ppermute | solution.py:558
  13.1 0.0 copy-start.1
  13.8 0.0 copy-start
  13.8 0.0 copy-start.2
  13.8 0.0 copy-done.1
  13.8 0.7 %copy-done = s32[512]{0:T(512)S(1)} copy-done((s32[512]{0:T(512)S(1)}, s32[512]{0:T(512)}, u32[]{:S(2)}) %copy-start) | copy-done | bytes 2072
  14.5 0.0 copy-done.2
  14.5 1.0 %weights.1 = (f32[40,112]{1,0:T(8,128)S(1)}, f32[64,128]{1,0:T(8,128)S(1)}, f32[40,40]{1,0:T(8,128)S(1)}) custom-call(s32[1]{0:T(128)S(6)} %copy.11.shift_ref, f32[1]{0:T(128)S(6)} %copy.12.frac_ref, s32[8]{0:T(128)S(1)} %copy-done.2, s32[1,512]{1,0:T(1,128)S(1)} %bitcast.33, f32[1,512]{1,0:T(1,128)S(1)} %bitcast.34), custom_call_target="tpu_custom_call" | custom-call | tf_op jit(solution)/shard_map/weights/pallas_call | solution.py:205
  15.5 0.0 collective-permute-done.1
  15.5 2.4 %collective-permute-done = f32[36,16,128]{2,1,0:T(8,128)S(1)} collective-permute-done((f32[36,16,128]{2,1,0:T(8,128)S(1)}, f32[36,16,128]{2,1,0:T(8,128)S(1)}, u32[]{:S(2)}, u32[]{:S(2)}) %collective-permute-start) | collective-permute-done | bytes 294944 | tf_op jit(solution)/shard_map/ppermute | solution.py:558
  17.9 0.5 %shear_z.2 = (f32[40,512]{1,0:T(8,128)S(1)}, f32[40,512]{1,0:T(8,128)S(1)}, f32[40,512]{1,0:T(8,128)S(1)}, f32[40,512]{1,0:T(8,128)S(1)}) custom-call(f32[40,112]{1,0:T(8,128)S(1)} %get-tuple-element.57.mixing_ref, f32[576,128]{1,0:T(8,128)S(1)} %bitcast.27, f32[640,128]{1,0:T(8,128)S(1)} %bitcast.20, f32[576,128]{1,0:T(8,128)S(1)} %bitcast.26), custom_call_target="tpu_custom_call" | custom-call | tf_op jit(solution)/shard_map/shear_z/pallas_call | solution.py:264
  18.4 2.5 %collective-permute-start.2 = (f32[40,512]{1,0:T(8,128)S(1)}, f32[40,512]{1,0:T(8,128)S(1)}, u32[]{:S(2)}, u32[]{:S(2)}) collective-permute-start(f32[40,512]{1,0:T(8,128)S(1)} %get-tuple-element.53), channel_id=1, source_target_pairs={{0,24},{4,28},{8,16},{12,20},{16,8},{20,12},{24,0},{28,4},{1,25},{... | collective-permute-start | bytes 245768 | tf_op jit(solution)/shard_map/ppermute | solution.py:523
  20.9 0.0 collective-permute-start.3
  20.9 0.5 %collective-permute-start.4 = (f32[40,512]{1,0:T(8,128)S(1)}, f32[40,512]{1,0:T(8,128)S(1)}, u32[]{:S(2)}, u32[]{:S(2)}) collective-permute-start(f32[40,512]{1,0:T(8,128)S(1)} %get-tuple-element.55), channel_id=1, source_target_pairs={{0,8},{4,12},{8,0},{12,4},{16,24},{20,28},{24,16},{28,20},{1,9},{5... | collective-permute-start | bytes 245768 | tf_op jit(solution)/shard_map/ppermute | solution.py:523
  21.4 0.0 collective-permute-done.7
  21.4 1.4 %collective-permute-start.5 = (f32[40,512]{1,0:T(8,128)S(1)}, f32[40,512]{1,0:T(8,128)S(1)}, u32[]{:S(2)}, u32[]{:S(2)}) collective-permute-start(f32[40,512]{1,0:T(8,128)S(1)} %get-tuple-element.56), channel_id=1, source_target_pairs={{0,12},{4,8},{8,4},{12,0},{16,28},{20,24},{24,20},{28,16},{1,13},{... | collective-permute-start | bytes 245768 | tf_op jit(solution)/shard_map/ppermute | solution.py:523
  22.9 0.2 collective-permute-done.6
  23.0 0.5 %shear_z.3 = (f32[40,512]{1,0:T(8,128)S(1)}, f32[40,512]{1,0:T(8,128)S(1)}, f32[40,512]{1,0:T(8,128)S(1)}, f32[40,512]{1,0:T(8,128)S(1)}) custom-call(f32[40,112]{1,0:T(8,128)S(1)} %get-tuple-element.57.mixing_ref, f32[576,128]{1,0:T(8,128)S(1)} %bitcast.25, f32[640,128]{1,0:T(8,128)S(1)} %bitcast.19, f32[576,128]{1,0:T(8,128)S(1)} %bitcast.24), custom_call_target="tpu_custom_call" | custom-call | tf_op jit(solution)/shard_map/shear_z/pallas_call | solution.py:264
  23.6 1.6 %collective-permute-start.8 = (f32[40,512]{1,0:T(8,128)S(1)}, f32[40,512]{1,0:T(8,128)S(1)}, u32[]{:S(2)}, u32[]{:S(2)}) collective-permute-start(f32[40,512]{1,0:T(8,128)S(1)} %get-tuple-element.63), channel_id=1, source_target_pairs={{0,16},{4,20},{8,24},{12,28},{16,0},{20,4},{24,8},{28,12},{1,17},{... | collective-permute-start | bytes 245768 | tf_op jit(solution)/shard_map/ppermute | solution.py:523
  25.1 0.0 collective-permute-done.2.refs_0_
  25.1 0.0 collective-permute-start.9
  25.2 1.4 %collective-permute-done.3.refs_1_ = f32[40,512]{1,0:T(8,128)S(1)} collective-permute-done((f32[40,512]{1,0:T(8,128)S(1)}, f32[40,512]{1,0:T(8,128)S(1)}, u32[]{:S(2)}, u32[]{:S(2)}) %collective-permute-start.3) | collective-permute-done | bytes 81952 | tf_op jit(solution)/shard_map/ppermute | solution.py:523
  26.5 0.0 collective-permute-start.10
  26.5 0.9 %collective-permute-done.4.refs_2_ = f32[40,512]{1,0:T(8,128)S(1)} collective-permute-done((f32[40,512]{1,0:T(8,128)S(1)}, f32[40,512]{1,0:T(8,128)S(1)}, u32[]{:S(2)}, u32[]{:S(2)}) %collective-permute-start.4) | collective-permute-done | bytes 81952 | tf_op jit(solution)/shard_map/ppermute | solution.py:523
  27.4 1.7 %collective-permute-done.5.refs_3_ = f32[40,512]{1,0:T(8,128)S(1)} collective-permute-done((f32[40,512]{1,0:T(8,128)S(1)}, f32[40,512]{1,0:T(8,128)S(1)}, u32[]{:S(2)}, u32[]{:S(2)}) %collective-permute-start.5) | collective-permute-done | bytes 81952 | tf_op jit(solution)/shard_map/ppermute | solution.py:523
  29.1 0.0 collective-permute-done.8.refs_4_
  29.1 0.8 %collective-permute-done.9.refs_5_ = f32[40,512]{1,0:T(8,128)S(1)} collective-permute-done((f32[40,512]{1,0:T(8,128)S(1)}, f32[40,512]{1,0:T(8,128)S(1)}, u32[]{:S(2)}, u32[]{:S(2)}) %collective-permute-start.9) | collective-permute-done | bytes 81952 | tf_op jit(solution)/shard_map/ppermute | solution.py:523
  29.9 0.0 collective-permute-done.10.refs_7_
  29.9 0.4 shear_y.1
  30.3 1.5 %collective-permute-start.12 = (f32[2,160,128]{2,1,0:T(8,128)S(1)}, f32[2,160,128]{2,1,0:T(8,128)S(1)}, u32[]{:S(2)}, u32[]{:S(2)}) collective-permute-start(f32[2,160,128]{2,1,0:T(8,128)S(1)} %get-tuple-element.69.refs_2_), channel_id=1, source_target_pairs={{0,8},{4,12},{8,0},{12,4},{16,24},{20,28},{24,16},{28,20},{1,9},{5... | collective-permute-start | bytes 491528 | tf_op jit(solution)/shard_map/ppermute | solution.py:523
  31.8 1.0 %collective-permute-start.13 = (f32[2,160,128]{2,1,0:T(8,128)S(1)}, f32[2,160,128]{2,1,0:T(8,128)S(1)}, u32[]{:S(2)}, u32[]{:S(2)}) collective-permute-start(f32[2,160,128]{2,1,0:T(8,128)S(1)} %get-tuple-element.70.refs_3_), channel_id=1, source_target_pairs={{0,16},{4,20},{8,24},{12,28},{16,0},{20,4},{24,8},{28,12},{1,17},{... | collective-permute-start | bytes 491528 | tf_op jit(solution)/shard_map/ppermute | solution.py:523
  32.8 0.3 project.1
  33.2 1.4 %collective-permute-start.14 = (f32[2,8,512]{2,1,0:T(8,128)S(1)}, f32[2,8,512]{2,1,0:T(8,128)S(1)}, u32[]{:S(2)}, u32[]{:S(2)}) collective-permute-start(f32[2,8,512]{2,1,0:T(8,128)S(1)} %get-tuple-element.74), channel_id=1, source_target_pairs={{0,3},{1,2},{2,1},{3,0},{4,7},{5,6},{6,5},{7,4},{8,11},{9,10},{10,... | collective-permute-start | bytes 98312 | tf_op jit(solution)/shard_map/ppermute | solution.py:523
  34.6 2.2 %collective-permute-start.15 = (f32[2,8,512]{2,1,0:T(8,128)S(1)}, f32[2,8,512]{2,1,0:T(8,128)S(1)}, u32[]{:S(2)}, u32[]{:S(2)}) collective-permute-start(f32[2,8,512]{2,1,0:T(8,128)S(1)} %get-tuple-element.75), channel_id=1, source_target_pairs={{0,2},{1,3},{2,0},{3,1},{4,6},{5,7},{6,4},{7,5},{8,10},{9,11},{10,... | collective-permute-start | bytes 98312 | tf_op jit(solution)/shard_map/ppermute | solution.py:523
  36.8 0.8 %collective-permute-start.16 = (f32[2,8,512]{2,1,0:T(8,128)S(1)}, f32[2,8,512]{2,1,0:T(8,128)S(1)}, u32[]{:S(2)}, u32[]{:S(2)}) collective-permute-start(f32[2,8,512]{2,1,0:T(8,128)S(1)} %get-tuple-element.76), channel_id=1, source_target_pairs={{0,1},{1,0},{2,3},{3,2},{4,5},{5,4},{6,7},{7,6},{8,9},{9,8},{10,11... | collective-permute-start | bytes 98312 | tf_op jit(solution)/shard_map/ppermute | solution.py:523
  37.6 0.0 collective-permute-done.12.refs_0_
  37.6 1.0 %collective-permute-start.17 = (f32[160,128]{1,0:T(8,128)S(1)}, f32[160,128]{1,0:T(8,128)S(1)}, u32[]{:S(2)}, u32[]{:S(2)}) collective-permute-start(f32[160,128]{1,0:T(8,128)S(1)} %get-tuple-element.72.refs_4_), channel_id=1, source_target_pairs={{0,24},{4,28},{8,16},{12,20},{16,8},{20,12},{24,0},{28,4},{1,25},{... | collective-permute-start | bytes 245768 | tf_op jit(solution)/shard_map/ppermute | solution.py:523
  38.7 0.0 collective-permute-done.13.refs_1_
  38.7 0.1 collective-permute-start.18
  38.8 0.4 collective-permute-done.14.refs_8_
  39.2 1.6 %collective-permute-start.19 = (f32[160,128]{1,0:T(8,128)S(1)}, f32[160,128]{1,0:T(8,128)S(1)}, u32[]{:S(2)}, u32[]{:S(2)}) collective-permute-start(f32[160,128]{1,0:T(8,128)S(1)} %get-tuple-element.78), channel_id=1, source_target_pairs={{0,4},{4,0},{8,12},{12,8},{16,20},{20,16},{24,28},{28,24},{1,5},{5... | collective-permute-start | bytes 245768 | tf_op jit(solution)/shard_map/ppermute | solution.py:523
  40.8 0.0 collective-permute-done.15.refs_9_
  40.8 0.1 collective-permute-start.20
  40.8 0.0 collective-permute-done.16.refs_10_
  40.9 0.4 collective-permute-start.11
  41.3 2.2 %collective-permute-done.17 = f32[160,128]{1,0:T(8,128)S(1)} collective-permute-done((f32[160,128]{1,0:T(8,128)S(1)}, f32[160,128]{1,0:T(8,128)S(1)}, u32[]{:S(2)}, u32[]{:S(2)}) %collective-permute-start.17) | collective-permute-done | bytes 81952 | tf_op jit(solution)/shard_map/ppermute | solution.py:523
  43.4 0.8 %collective-permute-done.18 = f32[160,128]{1,0:T(8,128)S(1)} collective-permute-done((f32[160,128]{1,0:T(8,128)S(1)}, f32[160,128]{1,0:T(8,128)S(1)}, u32[]{:S(2)}, u32[]{:S(2)}) %collective-permute-start.18) | collective-permute-done | bytes 81952 | tf_op jit(solution)/shard_map/ppermute | solution.py:523
  44.2 0.0 collective-permute-done.19
  44.2 0.0 collective-permute-done.20
  44.2 0.0 collective-permute-done.11
  44.2 1.5 %finish.1 = (f32[40,8,4,128]{3,2,1,0:T(4,128)}, f32[2,8,512]{2,1,0:T(8,128)}) custom-call(f32[40,4,128]{2,1,0:T(4,128)S(1)} %bitcast.23, f32[40,4,128]{2,1,0:T(4,128)S(1)} %bitcast.32, f32[2,40,4,128]{3,2,1,0:T(4,128)S(1)} %bitcast.21, f32[2,40,4,128]{3,2,1,0:T(4,128)S(1)} %bitcast.22, f32[40,4,128]{2,1,0:T(4,128)S(1)} %bitcast.30, ...), custom_call_target="tpu_custom_call" | custom-call | tf_op jit(solution)/shard_map/finish/pallas_call | solution.py:439
  (3 shorter events, 0.1 us)
Async XLA Ops:
  3.4 12.0 %collective-permute-start.1 = (f32[36,16,128]{2,1,0:T(8,128)S(1)}, f32[36,16,128]{2,1,0:T(8,128)S(1)}, u32[]{:S(2)}, u32[]{:S(2)}) collective-permute-start(f32[36,16,128]{2,1,0:T(8,128)S(1)} %get-tuple-element.94), channel_id=1, source_target_pairs={{1,2},{2,1},{5,6},{6,5},{9,10},{10,9},{13,14},{14,13},{17,18},{18,... | collective-permute-start | bytes 884744 | tf_op jit(solution)/shard_map/ppermute | solution.py:558
  4.1 13.8 %collective-permute-start = (f32[36,16,128]{2,1,0:T(8,128)S(1)}, f32[36,16,128]{2,1,0:T(8,128)S(1)}, u32[]{:S(2)}, u32[]{:S(2)}) collective-permute-start(f32[36,16,128]{2,1,0:T(8,128)S(1)} %get-tuple-element.95), channel_id=1, source_target_pairs={{0,1},{1,0},{2,3},{3,2},{4,5},{5,4},{6,7},{7,6},{8,9},{9,8},{10,11... | collective-permute-start | bytes 884744 | tf_op jit(solution)/shard_map/ppermute | solution.py:558
  10.0 11.4 %collective-permute-start.7 = (f32[36,16,128]{2,1,0:T(8,128)S(1)}, f32[36,16,128]{2,1,0:T(8,128)S(1)}, u32[]{:S(2)}, u32[]{:S(2)}) collective-permute-start(f32[36,16,128]{2,1,0:T(8,128)S(1)} %get-tuple-element.92), channel_id=1, source_target_pairs={{1,2},{2,1},{5,6},{6,5},{9,10},{10,9},{13,14},{14,13},{17,18},{18,... | collective-permute-start | bytes 884744 | tf_op jit(solution)/shard_map/ppermute | solution.py:558
  10.7 12.3 %collective-permute-start.6 = (f32[36,16,128]{2,1,0:T(8,128)S(1)}, f32[36,16,128]{2,1,0:T(8,128)S(1)}, u32[]{:S(2)}, u32[]{:S(2)}) collective-permute-start(f32[36,16,128]{2,1,0:T(8,128)S(1)} %get-tuple-element.93), channel_id=1, source_target_pairs={{0,1},{1,0},{2,3},{3,2},{4,5},{5,4},{6,7},{7,6},{8,9},{9,8},{10,11... | collective-permute-start | bytes 884744 | tf_op jit(solution)/shard_map/ppermute | solution.py:558
  13.1 0.7 %copy-start.1 = (f32[512]{0:T(512)S(1)}, f32[512]{0:T(512)}, u32[]{:S(2)}) copy-start(f32[512]{0:T(512)} %param.14) | copy-start | bytes 6148
  13.8 0.7 %copy-start = (s32[512]{0:T(512)S(1)}, s32[512]{0:T(512)}, u32[]{:S(2)}) copy-start(s32[512]{0:T(512)} %param.13) | copy-start | bytes 6148
  13.8 0.7 %copy-start.2 = (s32[8]{0:T(128)S(1)}, s32[8]{0:T(128)}, u32[]{:S(2)}) copy-start(s32[8]{0:T(128)} %slopes_ref.1) | copy-start | bytes 100
  18.4 6.8 %collective-permute-start.2 = (f32[40,512]{1,0:T(8,128)S(1)}, f32[40,512]{1,0:T(8,128)S(1)}, u32[]{:S(2)}, u32[]{:S(2)}) collective-permute-start(f32[40,512]{1,0:T(8,128)S(1)} %get-tuple-element.53), channel_id=1, source_target_pairs={{0,24},{4,28},{8,16},{12,20},{16,8},{20,12},{24,0},{28,4},{1,25},{... | collective-permute-start | bytes 245768 | tf_op jit(solution)/shard_map/ppermute | solution.py:523
  20.9 5.6 %collective-permute-start.3 = (f32[40,512]{1,0:T(8,128)S(1)}, f32[40,512]{1,0:T(8,128)S(1)}, u32[]{:S(2)}, u32[]{:S(2)}) collective-permute-start(f32[40,512]{1,0:T(8,128)S(1)} %get-tuple-element.54), channel_id=1, source_target_pairs={{0,28},{4,24},{8,20},{12,16},{16,12},{20,8},{24,4},{28,0},{1,29},{... | collective-permute-start | bytes 245768 | tf_op jit(solution)/shard_map/ppermute | solution.py:523
  20.9 6.5 %collective-permute-start.4 = (f32[40,512]{1,0:T(8,128)S(1)}, f32[40,512]{1,0:T(8,128)S(1)}, u32[]{:S(2)}, u32[]{:S(2)}) collective-permute-start(f32[40,512]{1,0:T(8,128)S(1)} %get-tuple-element.55), channel_id=1, source_target_pairs={{0,8},{4,12},{8,0},{12,4},{16,24},{20,28},{24,16},{28,20},{1,9},{5... | collective-permute-start | bytes 245768 | tf_op jit(solution)/shard_map/ppermute | solution.py:523
  21.4 7.6 %collective-permute-start.5 = (f32[40,512]{1,0:T(8,128)S(1)}, f32[40,512]{1,0:T(8,128)S(1)}, u32[]{:S(2)}, u32[]{:S(2)}) collective-permute-start(f32[40,512]{1,0:T(8,128)S(1)} %get-tuple-element.56), channel_id=1, source_target_pairs={{0,12},{4,8},{8,4},{12,0},{16,28},{20,24},{24,20},{28,16},{1,13},{... | collective-permute-start | bytes 245768 | tf_op jit(solution)/shard_map/ppermute | solution.py:523
  23.6 5.5 %collective-permute-start.8 = (f32[40,512]{1,0:T(8,128)S(1)}, f32[40,512]{1,0:T(8,128)S(1)}, u32[]{:S(2)}, u32[]{:S(2)}) collective-permute-start(f32[40,512]{1,0:T(8,128)S(1)} %get-tuple-element.63), channel_id=1, source_target_pairs={{0,16},{4,20},{8,24},{12,28},{16,0},{20,4},{24,8},{28,12},{1,17},{... | collective-permute-start | bytes 245768 | tf_op jit(solution)/shard_map/ppermute | solution.py:523
  25.1 4.7 %collective-permute-start.9 = (f32[40,512]{1,0:T(8,128)S(1)}, f32[40,512]{1,0:T(8,128)S(1)}, u32[]{:S(2)}, u32[]{:S(2)}) collective-permute-start(f32[40,512]{1,0:T(8,128)S(1)} %get-tuple-element.64), channel_id=1, source_target_pairs={{0,20},{4,16},{8,28},{12,24},{16,4},{20,0},{24,12},{28,8},{1,21},{... | collective-permute-start | bytes 245768 | tf_op jit(solution)/shard_map/ppermute | solution.py:523
  26.5 3.3 %collective-permute-start.10 = (f32[40,512]{1,0:T(8,128)S(1)}, f32[40,512]{1,0:T(8,128)S(1)}, u32[]{:S(2)}, u32[]{:S(2)}) collective-permute-start(f32[40,512]{1,0:T(8,128)S(1)} %get-tuple-element.66), channel_id=1, source_target_pairs={{0,4},{4,0},{8,12},{12,8},{16,20},{20,16},{24,28},{28,24},{1,5},{5... | collective-permute-start | bytes 245768 | tf_op jit(solution)/shard_map/ppermute | solution.py:523
  30.3 7.3 %collective-permute-start.12 = (f32[2,160,128]{2,1,0:T(8,128)S(1)}, f32[2,160,128]{2,1,0:T(8,128)S(1)}, u32[]{:S(2)}, u32[]{:S(2)}) collective-permute-start(f32[2,160,128]{2,1,0:T(8,128)S(1)} %get-tuple-element.69.refs_2_), channel_id=1, source_target_pairs={{0,8},{4,12},{8,0},{12,4},{16,24},{20,28},{24,16},{28,20},{1,9},{5... | collective-permute-start | bytes 491528 | tf_op jit(solution)/shard_map/ppermute | solution.py:523
  31.8 6.9 %collective-permute-start.13 = (f32[2,160,128]{2,1,0:T(8,128)S(1)}, f32[2,160,128]{2,1,0:T(8,128)S(1)}, u32[]{:S(2)}, u32[]{:S(2)}) collective-permute-start(f32[2,160,128]{2,1,0:T(8,128)S(1)} %get-tuple-element.70.refs_3_), channel_id=1, source_target_pairs={{0,16},{4,20},{8,24},{12,28},{16,0},{20,4},{24,8},{28,12},{1,17},{... | collective-permute-start | bytes 491528 | tf_op jit(solution)/shard_map/ppermute | solution.py:523
  33.2 6.0 %collective-permute-start.14 = (f32[2,8,512]{2,1,0:T(8,128)S(1)}, f32[2,8,512]{2,1,0:T(8,128)S(1)}, u32[]{:S(2)}, u32[]{:S(2)}) collective-permute-start(f32[2,8,512]{2,1,0:T(8,128)S(1)} %get-tuple-element.74), channel_id=1, source_target_pairs={{0,3},{1,2},{2,1},{3,0},{4,7},{5,6},{6,5},{7,4},{8,11},{9,10},{10,... | collective-permute-start | bytes 98312 | tf_op jit(solution)/shard_map/ppermute | solution.py:523
  34.6 6.2 %collective-permute-start.15 = (f32[2,8,512]{2,1,0:T(8,128)S(1)}, f32[2,8,512]{2,1,0:T(8,128)S(1)}, u32[]{:S(2)}, u32[]{:S(2)}) collective-permute-start(f32[2,8,512]{2,1,0:T(8,128)S(1)} %get-tuple-element.75), channel_id=1, source_target_pairs={{0,2},{1,3},{2,0},{3,1},{4,6},{5,7},{6,4},{7,5},{8,10},{9,11},{10,... | collective-permute-start | bytes 98312 | tf_op jit(solution)/shard_map/ppermute | solution.py:523
  36.8 4.1 %collective-permute-start.16 = (f32[2,8,512]{2,1,0:T(8,128)S(1)}, f32[2,8,512]{2,1,0:T(8,128)S(1)}, u32[]{:S(2)}, u32[]{:S(2)}) collective-permute-start(f32[2,8,512]{2,1,0:T(8,128)S(1)} %get-tuple-element.76), channel_id=1, source_target_pairs={{0,1},{1,0},{2,3},{3,2},{4,5},{5,4},{6,7},{7,6},{8,9},{9,8},{10,11... | collective-permute-start | bytes 98312 | tf_op jit(solution)/shard_map/ppermute | solution.py:523
  37.6 5.8 %collective-permute-start.17 = (f32[160,128]{1,0:T(8,128)S(1)}, f32[160,128]{1,0:T(8,128)S(1)}, u32[]{:S(2)}, u32[]{:S(2)}) collective-permute-start(f32[160,128]{1,0:T(8,128)S(1)} %get-tuple-element.72.refs_4_), channel_id=1, source_target_pairs={{0,24},{4,28},{8,16},{12,20},{16,8},{20,12},{24,0},{28,4},{1,25},{... | collective-permute-start | bytes 245768 | tf_op jit(solution)/shard_map/ppermute | solution.py:523
  38.7 5.6 %collective-permute-start.18 = (f32[160,128]{1,0:T(8,128)S(1)}, f32[160,128]{1,0:T(8,128)S(1)}, u32[]{:S(2)}, u32[]{:S(2)}) collective-permute-start(f32[160,128]{1,0:T(8,128)S(1)} %get-tuple-element.73.refs_5_), channel_id=1, source_target_pairs={{0,28},{4,24},{8,20},{12,16},{16,12},{20,8},{24,4},{28,0},{1,29},{... | collective-permute-start | bytes 245768 | tf_op jit(solution)/shard_map/ppermute | solution.py:523
  39.2 5.1 %collective-permute-start.19 = (f32[160,128]{1,0:T(8,128)S(1)}, f32[160,128]{1,0:T(8,128)S(1)}, u32[]{:S(2)}, u32[]{:S(2)}) collective-permute-start(f32[160,128]{1,0:T(8,128)S(1)} %get-tuple-element.78), channel_id=1, source_target_pairs={{0,4},{4,0},{8,12},{12,8},{16,20},{20,16},{24,28},{28,24},{1,5},{5... | collective-permute-start | bytes 245768 | tf_op jit(solution)/shard_map/ppermute | solution.py:523
  40.8 3.5 %collective-permute-start.20 = (f32[160,128]{1,0:T(8,128)S(1)}, f32[160,128]{1,0:T(8,128)S(1)}, u32[]{:S(2)}, u32[]{:S(2)}) collective-permute-start(f32[160,128]{1,0:T(8,128)S(1)} %get-tuple-element.79), channel_id=1, source_target_pairs={{0,4},{4,0},{8,12},{12,8},{16,20},{20,16},{24,28},{28,24},{1,5},{5... | collective-permute-start | bytes 245768 | tf_op jit(solution)/shard_map/ppermute | solution.py:523
  40.9 3.4 %collective-permute-start.11 = (f32[160,128]{1,0:T(8,128)S(1)}, f32[160,128]{1,0:T(8,128)S(1)}, u32[]{:S(2)}, u32[]{:S(2)}) collective-permute-start(f32[160,128]{1,0:T(8,128)S(1)} %get-tuple-element.68.refs_1_), channel_id=1, source_target_pairs={{0,4},{4,0},{8,12},{12,8},{16,20},{20,16},{24,28},{28,24},{1,5},{5... | collective-permute-start | bytes 245768 | tf_op jit(solution)/shard_map/ppermute | solution.py:523

commit v6 on v5

--- a/solution.py
+++ b/solution.py
@@ -297,20 +297,18 @@
                 for source in range(1, ny):
                     value = value + weight[source] * in_refs[source][planes, lanes]
                 lines = pl.ds(block * 8 * tiles + tile, 8, stride=tiles)
-                if target < 2:
+                if target < 4:
                     out_refs[target][lines, :] = value
-                elif target < ny - 2:
-                    out_refs[target // 2 + 1][target % 2, lines, :] = value
                 else:
-                    out_refs[target - ny][lines, :] = value
+                    out_refs[target // 2 + 2][target % 2, lines, :] = value
 
 
 def shear_y(taps, columns):
     ny = len(columns)
     plane_count, width = columns[0].shape
     shape = (plane_count * width // LANES, LANES)
-    single = [jax.ShapeDtypeStruct(shape, jnp.float32)] * 2
-    out_shape = single + [jax.ShapeDtypeStruct((2, *shape), jnp.float32)] * (ny // 2 - 2) + single
+    out_shape = [jax.ShapeDtypeStruct(shape, jnp.float32)] * 4
+    out_shape += [jax.ShapeDtypeStruct((2, *shape), jnp.float32)] * (ny // 2 - 2)
     return pl.pallas_call(
         functools.partial(shear_y_kernel, ny),
         out_shape=out_shape,
@@ -338,10 +336,10 @@
     )(*landed)
 
 
-def project_kernel(chips, tilts, chosen_ref, *refs):
+def project_kernel(chips, tilts, shares, chosen_ref, *refs):
     place, own_row = lax.axis_index("gz"), lax.axis_index("gy")
-    in_refs, share_refs, totals_ref = refs[:chips + 2], refs[chips + 2:-1], refs[-1]
-    ny, shares = 2 * chips, len(share_refs)
+    in_refs, share_ref, totals_ref = refs[:chips + 2], refs[-2], refs[-1]
+    ny = 2 * chips
     plane_count = chosen_ref.shape[1]
     total_planes = plane_count * shares
     span = ny // 4
@@ -353,12 +351,10 @@
     per_tile = (ny + 2 * span) * tilts
     totals_ref[...] = jnp.zeros(totals_ref.shape, jnp.float32)
     for source in range(ny):
-        if source < 2:
+        if source < 4:
             ref = in_refs[source]
-        elif source < ny - 2:
-            ref = in_refs[source // 2 + 1].at[source % 2]
         else:
-            ref = in_refs[source - ny]
+            ref = in_refs[source // 2 + 2].at[source % 2]
         value = jnp.concatenate(
             [ref[pl.ds(tile, plane_count, stride=tiles), :] for tile in range(tiles)], axis=1
         )
@@ -375,11 +371,11 @@
                     l * tilts:(l + 1) * tilts, tile * LANES:(tile + 1) * LANES
                 ]
     per_share = tilts // shares
-    for step, share_ref in enumerate(share_refs):
-        tilt = (place ^ step) * per_share
+    for step in range(shares):
+        tilt = step * per_share
         for u in range(per_share):
             for tile in range(tiles):
-                share_ref[u, :, tile * LANES:(tile + 1) * LANES] = (
+                share_ref[step, u, :, tile * LANES:(tile + 1) * LANES] = (
                     totals_ref[
                         pl.ds(tile * per_tile + span * tilts + tilt + u, ny, stride=tilts), :
                     ]
@@ -392,13 +388,13 @@
     ny = 2 * chips
     tilts = chosen.shape[0] // (2 * (ny // 4) + 1)
     width = rotated[0].shape[0] // chosen.shape[1] * LANES
-    share = jax.ShapeDtypeStruct((tilts // shares, ny, width), jnp.float32)
+    share = jax.ShapeDtypeStruct((shares, tilts // shares, ny, width), jnp.float32)
     totals = (width // LANES * (ny + 2 * (ny // 4)) * tilts, LANES)
     return pl.pallas_call(
-        functools.partial(project_kernel, chips, tilts),
-        out_shape=[share] * shares,
+        functools.partial(project_kernel, chips, tilts, shares),
+        out_shape=share,
         in_specs=[VMEM_SPEC] * (1 + len(rotated)),
-        out_specs=[VMEM_SPEC] * shares,
+        out_specs=VMEM_SPEC,
         scratch_shapes=[pltpu.VMEM(totals, jnp.float32)],
         compiler_params=pltpu.CompilerParams(vmem_limit_bytes=VMEM_LIMIT),
         name="project",
@@ -417,9 +413,9 @@
     ]
     for copy in copies:
         copy.start()
-    total = share_refs[0][...]
-    for share_ref in share_refs[1:]:
-        total = total + share_ref[...]
+    total = share_refs[0][0]
+    for share in range(1, share_refs[0].shape[0]):
+        total = total + share_refs[0][share]
     projections_ref[...] = total
     for copy in copies:
         copy.wait()
@@ -427,20 +423,19 @@
 
 def finish(own, early, landed, late, direct, shares, plane_count):
     chips = len(landed) + 2
-    slots = [(0, None), (1, None)]
-    slots += [(2 * step, 0) for step in range(1, chips - 1)]
-    slots += [(2 * step + 1, None) for step in range(1, chips - 1)]
-    slots += [(2 * chips - 2, None), (2 * chips - 1, None)]
+    slots = [(slot, None) for slot in range(4)]
+    slots += [(2 * step, 0) for step in range(2, chips)]
+    slots += [(2 * step + 1, None) for step in range(2, chips)]
     tiles = own.shape[0] // plane_count
     sources = [
         value.reshape(*value.shape[:-2], plane_count, tiles, LANES)
-        for value in (own, early, *landed, *late, *direct)
+        for value in (own, early, *direct, *landed, *late)
     ]
     return pl.pallas_call(
         functools.partial(finish_kernel, slots),
         out_shape=(
             jax.ShapeDtypeStruct((plane_count, 2 * chips, tiles, LANES), jnp.float32),
-            jax.ShapeDtypeStruct(shares[0].shape, jnp.float32),
+            jax.ShapeDtypeStruct(shares[0].shape[1:], jnp.float32),
         ),
         in_specs=[VMEM_SPEC] * (len(slots) + len(shares)),
         out_specs=(pl.BlockSpec(memory_space=pltpu.HBM), VMEM_SPEC),
@@ -564,14 +559,14 @@
             step = 2 * (2 * (index // 2) + half) + index % 2
             columns[step] = swap(mixed[index], "gy", step) if step else mixed[index]
     own, cross, *rotated = shear_y(taps, columns)
-    pairs, direct = rotated[:-2], rotated[-2:]
-    landed = [swap(value, "gy", 2 * step + 2) for step, value in enumerate(pairs)]
-    direct = [swap(value, "gy", groups - 2 + core) for core, value in enumerate(direct)]
+    direct, pairs = rotated[:2], rotated[2:]
+    landed = [swap(value, "gy", 2 * step + 4) for step, value in enumerate(pairs)]
+    direct = [swap(value, "gy", 2 + core) for core, value in enumerate(direct)]
     early = swap(cross, "gy", 1)
     tilted = project(chosen, (own, cross, *rotated), shares)
-    tilted = [swap(tilted[step], "gz", step) for step in range(shares - 1, 0, -1)] + [tilted[0]]
+    tilted = [lax.all_to_all(tilted, "gz", split_axis=0, concat_axis=0, tiled=True)]
     late = [swap(value, "gy", 1) for value in collect(landed)]
-    tilted, direct, late = lax.optimization_barrier((tilted, direct, late))
+    tilted, late, direct = lax.optimization_barrier((tilted, late, direct))
     rotated, projections = finish(own, early, landed, late, direct, tilted, plane_count)
     return (
         rotated.reshape(plane_count, row_local, width_all),

time: 46 us -> 45.5 us (0.989)
  starting transfers between devices: 25.3 us -> 22.9 us
  waiting for transfers between devices: 10.7 us -> 11.8 us
  Pallas kernels: 6.98 us -> 7.63 us
    ppermute x17 -> x14, starting transfers between devices: 16.3 us -> 10.6 us  [swap(): lax.ppermute(value, axis, [(i, i ^ step) for i in range(lax.axis_size(axi...]
    all_to_all x0 -> x1, starting transfers between devices: none -> 3.33 us  [local(): lax.all_to_all(tilted, 'gz', split_axis=0, concat_axis=0, tiled=True)]
    pallas_call x1, Pallas kernels: 0.34 us -> 1 us  [project(): pl.pallas_call(functools.partial(project_kernel, chips, tilts, shares), o...]
    all_to_all x0 -> x1, waiting for transfers between devices: none -> 0.57 us  [local(): lax.all_to_all(tilted, 'gz', split_axis=0, concat_axis=0, tiled=True)]
    ppermute x17 -> x14, waiting for transfers between devices: 8.06 us -> 8.62 us  [swap(): lax.ppermute(value, axis, [(i, i ^ step) for i in range(lax.axis_size(axi...]
  transfers between devices with their start and end apart: 21 -> 19, of which waited for: 9 -> 10; matrix products, arithmetic and copies ran while one was open for 0% -> 0% of each run, Pallas kernels for 5% -> 7%
where the time goes in v6:
time: 45.5 us; the launch traced here: 45.2 us
  starting transfers between devices  22.9 us (50%)
  waiting for transfers between devices  11.8 us (26%)
  Pallas kernels  7.63 us (17%)
  between operations  2.08 us (5%)
  local copies, waits for them, and re-layouts  0.75 us (2%)
    ppermute x14, starting transfers between devices, swap(): lax.ppermute(value, axis, [(i, i ^ step) for i in range(lax.axis_size(axi...  10.6 us
    ppermute x4, starting transfers between devices, local(): lax.ppermute(lax.dynamic_slice_in_dim(value, first, depth, 0), 'gz', ends...  9.02 us
    ppermute x14, waiting for transfers between devices, swap(): lax.ppermute(value, axis, [(i, i ^ step) for i in range(lax.axis_size(axi...  8.62 us
    all_to_all x1, starting transfers between devices, local(): lax.all_to_all(tilted, 'gz', split_axis=0, concat_axis=0, tiled=True)  3.33 us
    pallas_call x1, Pallas kernels, shear_x(): pl.pallas_call(functools.partial(shear_x_kernel, classes), out_shape=[jax...  2.7 us
    ppermute x4, waiting for transfers between devices, local(): lax.ppermute(lax.dynamic_slice_in_dim(value, first, depth, 0), 'gz', ends...  2.59 us
    pallas_call x1, Pallas kernels, finish(): pl.pallas_call(functools.partial(finish_kernel, slots), out_shape=(jax.Sh...  1.52 us
    pallas_call x2, Pallas kernels, shear_z(): pl.pallas_call(functools.partial(shear_z_kernel, plane_count, depth, chip...  1.05 us
  transfers between devices with their start and end apart: 19, of which 10 were waited for; matrix products, arithmetic and copies ran while one was open for 0% of the time, Pallas kernels for 7%

profile of v6, /device:TPU:0, one launch (start us, length us, event | category | flops | bytes accessed | tf_op | source)
XLA Modules:
  0.0 45.2 jit_solution(4729485935501193884)
XLA Ops:
  0.6 2.7 %shear_x.1 = (f32[40,16,128]{2,1,0:T(8,128)S(1)}, f32[40,16,128]{2,1,0:T(8,128)S(1)}) custom-call(s32[160]{0:T(256)} %shifts_hbm.1, f32[160]{0:T(256)} %fracs_hbm.1, f32[40,32,128]{2,1,0:T(8,128)} %bitcast.35), custom_call_target="tpu_custom_call" | custom-call | tf_op jit(solution)/shard_map/shear_x/pallas_call | solution.py:132
  3.4 0.7 %collective-permute-start.1 = (f32[36,16,128]{2,1,0:T(8,128)S(1)}, f32[36,16,128]{2,1,0:T(8,128)S(1)}, u32[]{:S(2)}, u32[]{:S(2)}) collective-permute-start(f32[36,16,128]{2,1,0:T(8,128)S(1)} %get-tuple-element.80), channel_id=1, source_target_pairs={{1,2},{2,1},{5,6},{6,5},{9,10},{10,9},{13,14},{14,13},{17,18},{18,... | collective-permute-start | bytes 884744 | tf_op jit(solution)/shard_map/ppermute | solution.py:553
  4.1 5.9 %collective-permute-start = (f32[36,16,128]{2,1,0:T(8,128)S(1)}, f32[36,16,128]{2,1,0:T(8,128)S(1)}, u32[]{:S(2)}, u32[]{:S(2)}) collective-permute-start(f32[36,16,128]{2,1,0:T(8,128)S(1)} %get-tuple-element.81), channel_id=1, source_target_pairs={{0,1},{1,0},{2,3},{3,2},{4,5},{5,4},{6,7},{7,6},{8,9},{9,8},{10,11... | collective-permute-start | bytes 884744 | tf_op jit(solution)/shard_map/ppermute | solution.py:553
  10.0 0.7 %collective-permute-start.7 = (f32[36,16,128]{2,1,0:T(8,128)S(1)}, f32[36,16,128]{2,1,0:T(8,128)S(1)}, u32[]{:S(2)}, u32[]{:S(2)}) collective-permute-start(f32[36,16,128]{2,1,0:T(8,128)S(1)} %get-tuple-element.78), channel_id=1, source_target_pairs={{1,2},{2,1},{5,6},{6,5},{9,10},{10,9},{13,14},{14,13},{17,18},{18,... | collective-permute-start | bytes 884744 | tf_op jit(solution)/shard_map/ppermute | solution.py:553
  10.7 1.8 %collective-permute-start.6 = (f32[36,16,128]{2,1,0:T(8,128)S(1)}, f32[36,16,128]{2,1,0:T(8,128)S(1)}, u32[]{:S(2)}, u32[]{:S(2)}) collective-permute-start(f32[36,16,128]{2,1,0:T(8,128)S(1)} %get-tuple-element.79), channel_id=1, source_target_pairs={{0,1},{1,0},{2,3},{3,2},{4,5},{5,4},{6,7},{7,6},{8,9},{9,8},{10,11... | collective-permute-start | bytes 884744 | tf_op jit(solution)/shard_map/ppermute | solution.py:553
  13.1 0.0 copy-start.1
  13.8 0.0 copy-start
  13.8 0.0 copy-start.2
  13.8 0.0 copy-done.1
  13.9 0.7 %copy-done = s32[512]{0:T(512)S(1)} copy-done((s32[512]{0:T(512)S(1)}, s32[512]{0:T(512)}, u32[]{:S(2)}) %copy-start) | copy-done | bytes 2072
  14.5 0.0 copy-done.2
  14.5 1.0 %weights.1 = (f32[40,112]{1,0:T(8,128)S(1)}, f32[64,128]{1,0:T(8,128)S(1)}, f32[40,40]{1,0:T(8,128)S(1)}) custom-call(s32[1]{0:T(128)S(6)} %copy.11.shift_ref, f32[1]{0:T(128)S(6)} %copy.12.frac_ref, s32[8]{0:T(128)S(1)} %copy-done.2, s32[1,512]{1,0:T(1,128)S(1)} %bitcast.33, f32[1,512]{1,0:T(1,128)S(1)} %bitcast.34), custom_call_target="tpu_custom_call" | custom-call | tf_op jit(solution)/shard_map/weights/pallas_call | solution.py:205
  15.5 0.0 collective-permute-done.1
  15.5 2.4 %collective-permute-done = f32[36,16,128]{2,1,0:T(8,128)S(1)} collective-permute-done((f32[36,16,128]{2,1,0:T(8,128)S(1)}, f32[36,16,128]{2,1,0:T(8,128)S(1)}, u32[]{:S(2)}, u32[]{:S(2)}) %collective-permute-start) | collective-permute-done | bytes 294944 | tf_op jit(solution)/shard_map/ppermute | solution.py:553
  17.9 0.5 %shear_z.2 = (f32[40,512]{1,0:T(8,128)S(1)}, f32[40,512]{1,0:T(8,128)S(1)}, f32[40,512]{1,0:T(8,128)S(1)}, f32[40,512]{1,0:T(8,128)S(1)}) custom-call(f32[40,112]{1,0:T(8,128)S(1)} %get-tuple-element.50.mixing_ref, f32[576,128]{1,0:T(8,128)S(1)} %bitcast.27, f32[640,128]{1,0:T(8,128)S(1)} %bitcast.20, f32[576,128]{1,0:T(8,128)S(1)} %bitcast.26), custom_call_target="tpu_custom_call" | custom-call | tf_op jit(solution)/shard_map/shear_z/pallas_call | solution.py:264
  18.4 2.5 %collective-permute-start.2 = (f32[40,512]{1,0:T(8,128)S(1)}, f32[40,512]{1,0:T(8,128)S(1)}, u32[]{:S(2)}, u32[]{:S(2)}) collective-permute-start(f32[40,512]{1,0:T(8,128)S(1)} %get-tuple-element.46), channel_id=1, source_target_pairs={{0,24},{4,28},{8,16},{12,20},{16,8},{20,12},{24,0},{28,4},{1,25},{... | collective-permute-start | bytes 245768 | tf_op jit(solution)/shard_map/ppermute | solution.py:518
  20.9 0.0 collective-permute-start.3
  20.9 0.5 %collective-permute-start.4 = (f32[40,512]{1,0:T(8,128)S(1)}, f32[40,512]{1,0:T(8,128)S(1)}, u32[]{:S(2)}, u32[]{:S(2)}) collective-permute-start(f32[40,512]{1,0:T(8,128)S(1)} %get-tuple-element.48), channel_id=1, source_target_pairs={{0,8},{4,12},{8,0},{12,4},{16,24},{20,28},{24,16},{28,20},{1,9},{5... | collective-permute-start | bytes 245768 | tf_op jit(solution)/shard_map/ppermute | solution.py:518
  21.4 0.0 collective-permute-done.7
  21.4 1.4 %collective-permute-start.5 = (f32[40,512]{1,0:T(8,128)S(1)}, f32[40,512]{1,0:T(8,128)S(1)}, u32[]{:S(2)}, u32[]{:S(2)}) collective-permute-start(f32[40,512]{1,0:T(8,128)S(1)} %get-tuple-element.49), channel_id=1, source_target_pairs={{0,12},{4,8},{8,4},{12,0},{16,28},{20,24},{24,20},{28,16},{1,13},{... | collective-permute-start | bytes 245768 | tf_op jit(solution)/shard_map/ppermute | solution.py:518
  22.9 0.2 collective-permute-done.6
  23.0 0.5 %shear_z.3 = (f32[40,512]{1,0:T(8,128)S(1)}, f32[40,512]{1,0:T(8,128)S(1)}, f32[40,512]{1,0:T(8,128)S(1)}, f32[40,512]{1,0:T(8,128)S(1)}) custom-call(f32[40,112]{1,0:T(8,128)S(1)} %get-tuple-element.50.mixing_ref, f32[576,128]{1,0:T(8,128)S(1)} %bitcast.25, f32[640,128]{1,0:T(8,128)S(1)} %bitcast.19, f32[576,128]{1,0:T(8,128)S(1)} %bitcast.24), custom_call_target="tpu_custom_call" | custom-call | tf_op jit(solution)/shard_map/shear_z/pallas_call | solution.py:264
  23.6 1.6 %collective-permute-start.8 = (f32[40,512]{1,0:T(8,128)S(1)}, f32[40,512]{1,0:T(8,128)S(1)}, u32[]{:S(2)}, u32[]{:S(2)}) collective-permute-start(f32[40,512]{1,0:T(8,128)S(1)} %get-tuple-element.56), channel_id=1, source_target_pairs={{0,16},{4,20},{8,24},{12,28},{16,0},{20,4},{24,8},{28,12},{1,17},{... | collective-permute-start | bytes 245768 | tf_op jit(solution)/shard_map/ppermute | solution.py:518
  25.1 0.0 collective-permute-done.2.refs_0_
  25.1 0.0 collective-permute-start.9
  25.2 1.4 %collective-permute-done.3.refs_1_ = f32[40,512]{1,0:T(8,128)S(1)} collective-permute-done((f32[40,512]{1,0:T(8,128)S(1)}, f32[40,512]{1,0:T(8,128)S(1)}, u32[]{:S(2)}, u32[]{:S(2)}) %collective-permute-start.3) | collective-permute-done | bytes 81952 | tf_op jit(solution)/shard_map/ppermute | solution.py:518
  26.5 0.0 collective-permute-start.10
  26.5 0.9 %collective-permute-done.4.refs_2_ = f32[40,512]{1,0:T(8,128)S(1)} collective-permute-done((f32[40,512]{1,0:T(8,128)S(1)}, f32[40,512]{1,0:T(8,128)S(1)}, u32[]{:S(2)}, u32[]{:S(2)}) %collective-permute-start.4) | collective-permute-done | bytes 81952 | tf_op jit(solution)/shard_map/ppermute | solution.py:518
  27.4 1.7 %collective-permute-done.5.refs_3_ = f32[40,512]{1,0:T(8,128)S(1)} collective-permute-done((f32[40,512]{1,0:T(8,128)S(1)}, f32[40,512]{1,0:T(8,128)S(1)}, u32[]{:S(2)}, u32[]{:S(2)}) %collective-permute-start.5) | collective-permute-done | bytes 81952 | tf_op jit(solution)/shard_map/ppermute | solution.py:518
  29.1 0.0 collective-permute-done.8.refs_4_
  29.1 0.8 %collective-permute-done.9.refs_5_ = f32[40,512]{1,0:T(8,128)S(1)} collective-permute-done((f32[40,512]{1,0:T(8,128)S(1)}, f32[40,512]{1,0:T(8,128)S(1)}, u32[]{:S(2)}, u32[]{:S(2)}) %collective-permute-start.9) | collective-permute-done | bytes 81952 | tf_op jit(solution)/shard_map/ppermute | solution.py:518
  29.9 0.0 collective-permute-done.10.refs_7_
  29.9 0.4 shear_y.1
  30.3 0.6 %collective-permute-start.12 = (f32[2,160,128]{2,1,0:T(8,128)S(1)}, f32[2,160,128]{2,1,0:T(8,128)S(1)}, u32[]{:S(2)}, u32[]{:S(2)}) collective-permute-start(f32[2,160,128]{2,1,0:T(8,128)S(1)} %get-tuple-element.65.refs_4_), channel_id=1, source_target_pairs={{0,16},{4,20},{8,24},{12,28},{16,0},{20,4},{24,8},{28,12},{1,17},{... | collective-permute-start | bytes 491528 | tf_op jit(solution)/shard_map/ppermute | solution.py:518
  30.9 2.4 %collective-permute-start.13 = (f32[2,160,128]{2,1,0:T(8,128)S(1)}, f32[2,160,128]{2,1,0:T(8,128)S(1)}, u32[]{:S(2)}, u32[]{:S(2)}) collective-permute-start(f32[2,160,128]{2,1,0:T(8,128)S(1)} %get-tuple-element.66.refs_5_), channel_id=1, source_target_pairs={{0,24},{4,28},{8,16},{12,20},{16,8},{20,12},{24,0},{28,4},{1,25},{... | collective-permute-start | bytes 491528 | tf_op jit(solution)/shard_map/ppermute | solution.py:518
  33.2 1.0 %project.1 = f32[4,2,8,512]{3,2,1,0:T(8,128)} custom-call(f32[40,40]{1,0:T(8,128)S(1)} %get-tuple-element.62.chosen_ref, f32[160,128]{1,0:T(8,128)S(1)} %get-tuple-element.60.refs_0_, f32[160,128]{1,0:T(8,128)S(1)} %get-tuple-element.61.refs_1_, f32[160,128]{1,0:T(8,128)S(1)} %get-tuple-element.63.refs_2_, f32[160,128]{1,0:T(8,128)S(1)} %get-tuple-element.64.refs_3_, ...), custom_call_target="tpu_custom_call" | custom-call | tf_op jit(solution)/shard_map/project/pallas_call | solution.py:393
  34.2 3.3 %all-to-all-start = ((f32[4,2,8,512]{3,2,1,0:T(8,128)}), f32[4,2,8,512]{3,2,1,0:T(8,128)S(1)}, u32[]{:S(2)}, u32[]{:S(2)}) async-start(f32[4,2,8,512]{3,2,1,0:T(8,128)} %project.1), calls=%async_computation | async-start | bytes 262144 | tf_op jit(solution)/shard_map/all_to_all | solution.py:567
  37.6 0.7 %collective-permute-start.16 = (f32[160,128]{1,0:T(8,128)S(1)}, f32[160,128]{1,0:T(8,128)S(1)}, u32[]{:S(2)}, u32[]{:S(2)}) collective-permute-start(f32[160,128]{1,0:T(8,128)S(1)} %get-tuple-element.63.refs_2_), channel_id=1, source_target_pairs={{0,8},{4,12},{8,0},{12,4},{16,24},{20,28},{24,16},{28,20},{1,9},{5... | collective-permute-start | bytes 245768 | tf_op jit(solution)/shard_map/ppermute | solution.py:518
  38.3 0.2 collective-permute-start.17
  38.5 1.6 %collective-permute-done.12.refs_0_ = f32[2,160,128]{2,1,0:T(8,128)S(1)} collective-permute-done((f32[2,160,128]{2,1,0:T(8,128)S(1)}, f32[2,160,128]{2,1,0:T(8,128)S(1)}, u32[]{:S(2)}, u32[]{:S(2)}) %collective-permute-start.12) | collective-permute-done | bytes 163872 | tf_op jit(solution)/shard_map/ppermute | solution.py:518
  40.1 0.0 collective-permute-done.13.refs_1_
  40.1 0.1 collective-permute-start.14
  40.2 0.5 %collective-permute-start.15 = (f32[160,128]{1,0:T(8,128)S(1)}, f32[160,128]{1,0:T(8,128)S(1)}, u32[]{:S(2)}, u32[]{:S(2)}) collective-permute-start(f32[160,128]{1,0:T(8,128)S(1)} %get-tuple-element.68), channel_id=1, source_target_pairs={{0,4},{4,0},{8,12},{12,8},{16,20},{20,16},{24,28},{28,24},{1,5},{5... | collective-permute-start | bytes 245768 | tf_op jit(solution)/shard_map/ppermute | solution.py:518
  40.7 0.1 collective-permute-start.11
  40.8 2.1 %collective-permute-done.16 = f32[160,128]{1,0:T(8,128)S(1)} collective-permute-done((f32[160,128]{1,0:T(8,128)S(1)}, f32[160,128]{1,0:T(8,128)S(1)}, u32[]{:S(2)}, u32[]{:S(2)}) %collective-permute-start.16) | collective-permute-done | bytes 81952 | tf_op jit(solution)/shard_map/ppermute | solution.py:518
  42.9 0.2 collective-permute-done.17
  43.1 0.6 %all-to-all-done.refs_8_ = f32[4,2,8,512]{3,2,1,0:T(8,128)S(1)} async-done(((f32[4,2,8,512]{3,2,1,0:T(8,128)}), f32[4,2,8,512]{3,2,1,0:T(8,128)S(1)}, u32[]{:S(2)}, u32[]{:S(2)}) %all-to-all-start) | async-done | bytes 131104 | tf_op jit(solution)/shard_map/all_to_all | solution.py:567
  43.6 0.0 collective-permute-done.14
  43.6 0.0 collective-permute-done.15
  43.6 0.0 collective-permute-done.11
  43.6 1.5 %finish.1 = (f32[40,8,4,128]{3,2,1,0:T(4,128)}, f32[2,8,512]{2,1,0:T(8,128)}) custom-call(f32[40,4,128]{2,1,0:T(4,128)S(1)} %bitcast.23, f32[40,4,128]{2,1,0:T(4,128)S(1)} %bitcast.32, f32[40,4,128]{2,1,0:T(4,128)S(1)} %bitcast.28, f32[40,4,128]{2,1,0:T(4,128)S(1)} %bitcast.29, f32[2,40,4,128]{3,2,1,0:T(4,128)S(1)} %bitcast.21, ...), custom_call_target="tpu_custom_call" | custom-call | tf_op jit(solution)/shard_map/finish/pallas_call | solution.py:434
  (3 shorter events, 0.1 us)
Async XLA Ops:
  3.4 12.1 %collective-permute-start.1 = (f32[36,16,128]{2,1,0:T(8,128)S(1)}, f32[36,16,128]{2,1,0:T(8,128)S(1)}, u32[]{:S(2)}, u32[]{:S(2)}) collective-permute-start(f32[36,16,128]{2,1,0:T(8,128)S(1)} %get-tuple-element.80), channel_id=1, source_target_pairs={{1,2},{2,1},{5,6},{6,5},{9,10},{10,9},{13,14},{14,13},{17,18},{18,... | collective-permute-start | bytes 884744 | tf_op jit(solution)/shard_map/ppermute | solution.py:553
  4.1 13.8 %collective-permute-start = (f32[36,16,128]{2,1,0:T(8,128)S(1)}, f32[36,16,128]{2,1,0:T(8,128)S(1)}, u32[]{:S(2)}, u32[]{:S(2)}) collective-permute-start(f32[36,16,128]{2,1,0:T(8,128)S(1)} %get-tuple-element.81), channel_id=1, source_target_pairs={{0,1},{1,0},{2,3},{3,2},{4,5},{5,4},{6,7},{7,6},{8,9},{9,8},{10,11... | collective-permute-start | bytes 884744 | tf_op jit(solution)/shard_map/ppermute | solution.py:553
  10.0 11.4 %collective-permute-start.7 = (f32[36,16,128]{2,1,0:T(8,128)S(1)}, f32[36,16,128]{2,1,0:T(8,128)S(1)}, u32[]{:S(2)}, u32[]{:S(2)}) collective-permute-start(f32[36,16,128]{2,1,0:T(8,128)S(1)} %get-tuple-element.78), channel_id=1, source_target_pairs={{1,2},{2,1},{5,6},{6,5},{9,10},{10,9},{13,14},{14,13},{17,18},{18,... | collective-permute-start | bytes 884744 | tf_op jit(solution)/shard_map/ppermute | solution.py:553
  10.7 12.3 %collective-permute-start.6 = (f32[36,16,128]{2,1,0:T(8,128)S(1)}, f32[36,16,128]{2,1,0:T(8,128)S(1)}, u32[]{:S(2)}, u32[]{:S(2)}) collective-permute-start(f32[36,16,128]{2,1,0:T(8,128)S(1)} %get-tuple-element.79), channel_id=1, source_target_pairs={{0,1},{1,0},{2,3},{3,2},{4,5},{5,4},{6,7},{7,6},{8,9},{9,8},{10,11... | collective-permute-start | bytes 884744 | tf_op jit(solution)/shard_map/ppermute | solution.py:553
  13.1 0.7 %copy-start.1 = (f32[512]{0:T(512)S(1)}, f32[512]{0:T(512)}, u32[]{:S(2)}) copy-start(f32[512]{0:T(512)} %param.14) | copy-start | bytes 6148
  13.8 0.7 %copy-start = (s32[512]{0:T(512)S(1)}, s32[512]{0:T(512)}, u32[]{:S(2)}) copy-start(s32[512]{0:T(512)} %param.13) | copy-start | bytes 6148
  13.8 0.7 %copy-start.2 = (s32[8]{0:T(128)S(1)}, s32[8]{0:T(128)}, u32[]{:S(2)}) copy-start(s32[8]{0:T(128)} %slopes_ref.1) | copy-start | bytes 100
  18.4 6.8 %collective-permute-start.2 = (f32[40,512]{1,0:T(8,128)S(1)}, f32[40,512]{1,0:T(8,128)S(1)}, u32[]{:S(2)}, u32[]{:S(2)}) collective-permute-start(f32[40,512]{1,0:T(8,128)S(1)} %get-tuple-element.46), channel_id=1, source_target_pairs={{0,24},{4,28},{8,16},{12,20},{16,8},{20,12},{24,0},{28,4},{1,25},{... | collective-permute-start | bytes 245768 | tf_op jit(solution)/shard_map/ppermute | solution.py:518
  20.9 5.6 %collective-permute-start.3 = (f32[40,512]{1,0:T(8,128)S(1)}, f32[40,512]{1,0:T(8,128)S(1)}, u32[]{:S(2)}, u32[]{:S(2)}) collective-permute-start(f32[40,512]{1,0:T(8,128)S(1)} %get-tuple-element.47), channel_id=1, source_target_pairs={{0,28},{4,24},{8,20},{12,16},{16,12},{20,8},{24,4},{28,0},{1,29},{... | collective-permute-start | bytes 245768 | tf_op jit(solution)/shard_map/ppermute | solution.py:518
  20.9 6.5 %collective-permute-start.4 = (f32[40,512]{1,0:T(8,128)S(1)}, f32[40,512]{1,0:T(8,128)S(1)}, u32[]{:S(2)}, u32[]{:S(2)}) collective-permute-start(f32[40,512]{1,0:T(8,128)S(1)} %get-tuple-element.48), channel_id=1, source_target_pairs={{0,8},{4,12},{8,0},{12,4},{16,24},{20,28},{24,16},{28,20},{1,9},{5... | collective-permute-start | bytes 245768 | tf_op jit(solution)/shard_map/ppermute | solution.py:518
  21.4 7.6 %collective-permute-start.5 = (f32[40,512]{1,0:T(8,128)S(1)}, f32[40,512]{1,0:T(8,128)S(1)}, u32[]{:S(2)}, u32[]{:S(2)}) collective-permute-start(f32[40,512]{1,0:T(8,128)S(1)} %get-tuple-element.49), channel_id=1, source_target_pairs={{0,12},{4,8},{8,4},{12,0},{16,28},{20,24},{24,20},{28,16},{1,13},{... | collective-permute-start | bytes 245768 | tf_op jit(solution)/shard_map/ppermute | solution.py:518
  23.6 5.5 %collective-permute-start.8 = (f32[40,512]{1,0:T(8,128)S(1)}, f32[40,512]{1,0:T(8,128)S(1)}, u32[]{:S(2)}, u32[]{:S(2)}) collective-permute-start(f32[40,512]{1,0:T(8,128)S(1)} %get-tuple-element.56), channel_id=1, source_target_pairs={{0,16},{4,20},{8,24},{12,28},{16,0},{20,4},{24,8},{28,12},{1,17},{... | collective-permute-start | bytes 245768 | tf_op jit(solution)/shard_map/ppermute | solution.py:518
  25.1 4.7 %collective-permute-start.9 = (f32[40,512]{1,0:T(8,128)S(1)}, f32[40,512]{1,0:T(8,128)S(1)}, u32[]{:S(2)}, u32[]{:S(2)}) collective-permute-start(f32[40,512]{1,0:T(8,128)S(1)} %get-tuple-element.57), channel_id=1, source_target_pairs={{0,20},{4,16},{8,28},{12,24},{16,4},{20,0},{24,12},{28,8},{1,21},{... | collective-permute-start | bytes 245768 | tf_op jit(solution)/shard_map/ppermute | solution.py:518
  26.5 3.3 %collective-permute-start.10 = (f32[40,512]{1,0:T(8,128)S(1)}, f32[40,512]{1,0:T(8,128)S(1)}, u32[]{:S(2)}, u32[]{:S(2)}) collective-permute-start(f32[40,512]{1,0:T(8,128)S(1)} %get-tuple-element.59), channel_id=1, source_target_pairs={{0,4},{4,0},{8,12},{12,8},{16,20},{20,16},{24,28},{28,24},{1,5},{5... | collective-permute-start | bytes 245768 | tf_op jit(solution)/shard_map/ppermute | solution.py:518
  30.3 9.8 %collective-permute-start.12 = (f32[2,160,128]{2,1,0:T(8,128)S(1)}, f32[2,160,128]{2,1,0:T(8,128)S(1)}, u32[]{:S(2)}, u32[]{:S(2)}) collective-permute-start(f32[2,160,128]{2,1,0:T(8,128)S(1)} %get-tuple-element.65.refs_4_), channel_id=1, source_target_pairs={{0,16},{4,20},{8,24},{12,28},{16,0},{20,4},{24,8},{28,12},{1,17},{... | collective-permute-start | bytes 491528 | tf_op jit(solution)/shard_map/ppermute | solution.py:518
  30.9 9.2 %collective-permute-start.13 = (f32[2,160,128]{2,1,0:T(8,128)S(1)}, f32[2,160,128]{2,1,0:T(8,128)S(1)}, u32[]{:S(2)}, u32[]{:S(2)}) collective-permute-start(f32[2,160,128]{2,1,0:T(8,128)S(1)} %get-tuple-element.66.refs_5_), channel_id=1, source_target_pairs={{0,24},{4,28},{8,16},{12,20},{16,8},{20,12},{24,0},{28,4},{1,25},{... | collective-permute-start | bytes 491528 | tf_op jit(solution)/shard_map/ppermute | solution.py:518
  34.2 9.4 %all-to-all-start = ((f32[4,2,8,512]{3,2,1,0:T(8,128)}), f32[4,2,8,512]{3,2,1,0:T(8,128)S(1)}, u32[]{:S(2)}, u32[]{:S(2)}) async-start(f32[4,2,8,512]{3,2,1,0:T(8,128)} %project.1), calls=%async_computation | async-start | bytes 262144 | tf_op jit(solution)/shard_map/all_to_all | solution.py:567
  37.6 5.3 %collective-permute-start.16 = (f32[160,128]{1,0:T(8,128)S(1)}, f32[160,128]{1,0:T(8,128)S(1)}, u32[]{:S(2)}, u32[]{:S(2)}) collective-permute-start(f32[160,128]{1,0:T(8,128)S(1)} %get-tuple-element.63.refs_2_), channel_id=1, source_target_pairs={{0,8},{4,12},{8,0},{12,4},{16,24},{20,28},{24,16},{28,20},{1,9},{5... | collective-permute-start | bytes 245768 | tf_op jit(solution)/shard_map/ppermute | solution.py:518
  38.3 4.7 %collective-permute-start.17 = (f32[160,128]{1,0:T(8,128)S(1)}, f32[160,128]{1,0:T(8,128)S(1)}, u32[]{:S(2)}, u32[]{:S(2)}) collective-permute-start(f32[160,128]{1,0:T(8,128)S(1)} %get-tuple-element.64.refs_3_), channel_id=1, source_target_pairs={{0,12},{4,8},{8,4},{12,0},{16,28},{20,24},{24,20},{28,16},{1,13},{... | collective-permute-start | bytes 245768 | tf_op jit(solution)/shard_map/ppermute | solution.py:518
  40.1 3.5 %collective-permute-start.14 = (f32[160,128]{1,0:T(8,128)S(1)}, f32[160,128]{1,0:T(8,128)S(1)}, u32[]{:S(2)}, u32[]{:S(2)}) collective-permute-start(f32[160,128]{1,0:T(8,128)S(1)} %get-tuple-element.67), channel_id=1, source_target_pairs={{0,4},{4,0},{8,12},{12,8},{16,20},{20,16},{24,28},{28,24},{1,5},{5... | collective-permute-start | bytes 245768 | tf_op jit(solution)/shard_map/ppermute | solution.py:518
  40.2 3.4 %collective-permute-start.15 = (f32[160,128]{1,0:T(8,128)S(1)}, f32[160,128]{1,0:T(8,128)S(1)}, u32[]{:S(2)}, u32[]{:S(2)}) collective-permute-start(f32[160,128]{1,0:T(8,128)S(1)} %get-tuple-element.68), channel_id=1, source_target_pairs={{0,4},{4,0},{8,12},{12,8},{16,20},{20,16},{24,28},{28,24},{1,5},{5... | collective-permute-start | bytes 245768 | tf_op jit(solution)/shard_map/ppermute | solution.py:518
  40.7 3.0 %collective-permute-start.11 = (f32[160,128]{1,0:T(8,128)S(1)}, f32[160,128]{1,0:T(8,128)S(1)}, u32[]{:S(2)}, u32[]{:S(2)}) collective-permute-start(f32[160,128]{1,0:T(8,128)S(1)} %get-tuple-element.61.refs_1_), channel_id=1, source_target_pairs={{0,4},{4,0},{8,12},{12,8},{16,20},{20,16},{24,28},{28,24},{1,5},{5... | collective-permute-start | bytes 245768 | tf_op jit(solution)/shard_map/ppermute | solution.py:518

commit v7 on v6

--- a/solution.py
+++ b/solution.py
@@ -44,36 +44,29 @@
 def shear_x_kernel(
     classes, shifts_hbm, fracs_hbm, planes_hbm, *rest
 ):
-    out_refs = rest[:-8]
-    planes_ref, margin_ref, base_ref, lines_ref, shifts_ref, fracs_ref, small_sem, plane_sem = (
-        rest[-8:]
-    )
-    plane_count, rows, lanes = planes_ref.shape
+    out_refs = rest[:-7]
+    margin_ref, base_ref, lines_ref, shifts_ref, fracs_ref, small_sem, plane_sem = rest[-7:]
+    plane_count, rows, lanes = lines_ref.shape
     per_class = rows // classes
     before, after = 8, margin_ref.shape[1] - rows - 8
-    blocks = plane_sem.shape[0]
-    per_block = plane_count // blocks
     small = [
         pltpu.make_async_copy(shifts_hbm, shifts_ref, small_sem.at[0]),
         pltpu.make_async_copy(fracs_hbm, fracs_ref, small_sem.at[1]),
     ]
-    large = [
-        pltpu.make_async_copy(
-            planes_hbm.at[b * per_block:(b + 1) * per_block],
-            planes_ref.at[b * per_block:(b + 1) * per_block],
-            plane_sem.at[b],
-        )
-        for b in range(blocks)
-    ]
-    for copy in small + large:
+    large = pltpu.make_async_copy(
+        planes_hbm, margin_ref.at[:, before:before + rows, :], plane_sem.at[0]
+    )
+    for copy in small:
         copy.start()
+    large.start()
     line = lax.broadcasted_iota(jnp.int32, (lanes, lanes), 0)
     lane = lax.broadcasted_iota(jnp.int32, (lanes, lanes), 1)
     own_side = lane <= line
     tap = (lanes - lax.broadcasted_iota(jnp.int32, (plane_count, lanes), 1)) % lanes
     lane_of_row = lax.broadcasted_iota(jnp.int32, (per_class, lanes), 1)
-    zeros = jnp.zeros((8, lanes), jnp.float32)
     first = lax.axis_index("gz") * plane_count
+    margin_ref[:, 0:before, :] = jnp.zeros((plane_count, before, lanes), jnp.float32)
+    margin_ref[:, before + rows:, :] = jnp.zeros((plane_count, after, lanes), jnp.float32)
     side = lax.axis_index("gy") // 2 % 2
     first_lines = (2 - 2 * side, 2 * side)
     for copy in small:
@@ -83,9 +76,6 @@
     base_ref[...] = tap_weight_in_kernel(tap - BELOW, base_ref[...])
 
     def one_plane(z, carry):
-        margin_ref[z, 0:before, :] = zeros
-        margin_ref[z, before:before + rows, :] = planes_ref[z]
-        margin_ref[z, before + rows:before + rows + after, :] = zeros
         spread = pltpu.roll(
             jnp.broadcast_to(base_ref[pl.ds(z, 1), :], (lanes, lanes)),
             0, 1, stride=1, stride_axis=0,
@@ -121,14 +111,12 @@
                 ]
         return carry
 
-    for b in range(blocks):
-        large[b].wait()
-        lax.fori_loop(b * per_block, (b + 1) * per_block, one_plane, 0, unroll=True)
+    large.wait()
+    lax.fori_loop(0, plane_count, one_plane, 0, unroll=True)
 
 
 def shear_x(volume, x_offsets, x_fracs, classes, parts):
     plane_count, rows, lanes = volume.shape
-    blocks = 2 if plane_count % 2 == 0 else 1
     return pl.pallas_call(
         functools.partial(shear_x_kernel, classes),
         out_shape=[
@@ -137,14 +125,13 @@
         in_specs=[pl.BlockSpec(memory_space=pltpu.HBM)] * 3,
         out_specs=[VMEM_SPEC] * parts,
         scratch_shapes=[
-            pltpu.VMEM(volume.shape, jnp.float32),
             pltpu.VMEM((plane_count, rows + 16, lanes), jnp.float32),
             pltpu.VMEM((plane_count, lanes), jnp.float32),
             pltpu.VMEM(volume.shape, jnp.float32),
             pltpu.SMEM(x_offsets.shape, jnp.int32),
             pltpu.SMEM(x_fracs.shape, jnp.float32),
             pltpu.SemaphoreType.DMA((2,)),
-            pltpu.SemaphoreType.DMA((blocks,)),
+            pltpu.SemaphoreType.DMA((1,)),
         ],
         compiler_params=pltpu.CompilerParams(vmem_limit_bytes=VMEM_LIMIT),
         name="shear_x",
@@ -401,48 +388,84 @@
     )(chosen, *rotated)
 
 
-def finish_kernel(slots, *refs):
-    sources, share_refs = refs[:len(slots)], refs[len(slots):-3]
-    rotated_ref, projections_ref, sems = refs[-3:]
+def place_kernel(slots, *refs):
+    rotated_ref, sems = refs[-2:]
     row = lax.axis_index("gy")
     copies = [
         pltpu.make_async_copy(
-            ref if index is None else ref.at[index], rotated_ref.at[:, row ^ slot], sems.at[slot]
-        )
-        for ref, (slot, index) in zip(sources, slots)
+            ref if index is None else ref.at[index], rotated_ref.at[:, row ^ slot], sems.at[place]
+        )
+        for place, (ref, (slot, index)) in enumerate(zip(refs, slots))
     ]
     for copy in copies:
         copy.start()
-    total = share_refs[0][0]
-    for share in range(1, share_refs[0].shape[0]):
-        total = total + share_refs[0][share]
-    projections_ref[...] = total
     for copy in copies:
         copy.wait()
 
 
-def finish(own, early, landed, late, direct, shares, plane_count):
+def in_columns(value, plane_count):
+    return value.reshape(
+        *value.shape[:-2], plane_count, value.shape[-2] // plane_count, value.shape[-1]
+    )
+
+
+def place_first(own, landed, plane_count):
     chips = len(landed) + 2
-    slots = [(slot, None) for slot in range(4)]
-    slots += [(2 * step, 0) for step in range(2, chips)]
-    slots += [(2 * step + 1, None) for step in range(2, chips)]
-    tiles = own.shape[0] // plane_count
-    sources = [
-        value.reshape(*value.shape[:-2], plane_count, tiles, LANES)
-        for value in (own, early, *direct, *landed, *late)
+    slots = [(0, None)] + [(2 * step, 0) for step in range(2, chips)]
+    sources = [in_columns(value, plane_count) for value in (own, *landed)]
+    return pl.pallas_call(
+        functools.partial(place_kernel, slots),
+        out_shape=jax.ShapeDtypeStruct(
+            (plane_count, 2 * chips, *sources[0].shape[-2:]), jnp.float32
+        ),
+        in_specs=[VMEM_SPEC] * len(slots),
+        out_specs=pl.BlockSpec(memory_space=pltpu.HBM),
+        scratch_shapes=[pltpu.SemaphoreType.DMA((len(slots),))],
+        compiler_params=pltpu.CompilerParams(vmem_limit_bytes=VMEM_LIMIT),
+        name="place_first",
+    )(*sources)
+
+
+def finish_kernel(slots, *refs):
+    share_ref = refs[len(slots)]
+    rotated_ref, projections_ref, total_ref, sems = refs[-4:]
+    row = lax.axis_index("gy")
+    copies = [
+        pltpu.make_async_copy(ref, rotated_ref.at[:, row ^ slot], sems.at[place])
+        for place, (ref, slot) in enumerate(zip(refs, slots))
     ]
+    for copy in copies:
+        copy.start()
+    total = share_ref[0]
+    for share in range(1, share_ref.shape[0]):
+        total = total + share_ref[share]
+    total_ref[...] = total
+    copies.append(pltpu.make_async_copy(total_ref, projections_ref, sems.at[len(slots)]))
+    copies[-1].start()
+    for copy in copies:
+        copy.wait()
+
+
+def finish(placed, early, late, direct, shares, plane_count):
+    chips = len(late) + 2
+    slots = [1, 2, 3] + [2 * step + 1 for step in range(2, chips)]
+    sources = [in_columns(value, plane_count) for value in (early, *direct, *late)]
     return pl.pallas_call(
         functools.partial(finish_kernel, slots),
         out_shape=(
-            jax.ShapeDtypeStruct((plane_count, 2 * chips, tiles, LANES), jnp.float32),
-            jax.ShapeDtypeStruct(shares[0].shape[1:], jnp.float32),
+            jax.ShapeDtypeStruct(placed.shape, jnp.float32),
+            jax.ShapeDtypeStruct(shares.shape[1:], jnp.float32),
         ),
-        in_specs=[VMEM_SPEC] * (len(slots) + len(shares)),
-        out_specs=(pl.BlockSpec(memory_space=pltpu.HBM), VMEM_SPEC),
-        scratch_shapes=[pltpu.SemaphoreType.DMA((2 * chips,))],
+        in_specs=[VMEM_SPEC] * (len(slots) + 1) + [pl.BlockSpec(memory_space=pltpu.HBM)],
+        out_specs=[pl.BlockSpec(memory_space=pltpu.HBM)] * 2,
+        scratch_shapes=[
+            pltpu.VMEM(shares.shape[1:], jnp.float32),
+            pltpu.SemaphoreType.DMA((len(slots) + 1,)),
+        ],
+        input_output_aliases={len(slots) + 1: 0},
         compiler_params=pltpu.CompilerParams(vmem_limit_bytes=VMEM_LIMIT),
         name="finish",
-    )(*sources, *shares)
+    )(*sources, shares, placed)
 
 
 def with_halo(value, sides, width):
@@ -565,9 +588,10 @@
     early = swap(cross, "gy", 1)
     tilted = project(chosen, (own, cross, *rotated), shares)
     tilted = [lax.all_to_all(tilted, "gz", split_axis=0, concat_axis=0, tiled=True)]
-    late = [swap(value, "gy", 1) for value in collect(landed)]
+    late = [swap(value, "gy", 1) for value in collect(landed[::-1])][::-1]
     tilted, late, direct = lax.optimization_barrier((tilted, late, direct))
-    rotated, projections = finish(own, early, landed, late, direct, tilted, plane_count)
+    placed = place_first(own, landed, plane_count)
+    rotated, projections = finish(placed, early, late, direct, tilted[0], plane_count)
     return (
         rotated.reshape(plane_count, row_local, width_all),
         jnp.swapaxes(projections, 1, 2),

time: 45.5 us -> 44.5 us (0.978)
  waiting for transfers between devices: 11.8 us -> 11.1 us
    ppermute x14, waiting for transfers between devices: 8.62 us -> 7.9 us  [swap(): lax.ppermute(value, axis, [(i, i ^ step) for i in range(lax.axis_size(axi...]
    pallas_call x0 -> x1, Pallas kernels: none -> 0.71 us  [place_first(): pl.pallas_call(functools.partial(place_kernel, slots), out_shape=jax.Shap...]
    pallas_call x1, Pallas kernels: 1.52 us -> 0.82 us  [finish(): pl.pallas_call(functools.partial(finish_kernel, slots), out_shape=(jax.Sh...]
  transfers between devices with their start and end apart: 19 -> 19, of which waited for: 10 -> 10; matrix products, arithmetic and copies ran while one was open for 0% -> 0% of each run, Pallas kernels for 7% -> 8%
where the time goes in v7:
time: 44.5 us; the launch traced here: 44.2 us
  starting transfers between devices  22.9 us (51%)
  waiting for transfers between devices  11.1 us (25%)
  Pallas kernels  7.42 us (17%)
  between operations  2.09 us (5%)
  local copies, waits for them, and re-layouts  0.75 us (2%)
    ppermute x14, starting transfers between devices, swap(): lax.ppermute(value, axis, [(i, i ^ step) for i in range(lax.axis_size(axi...  10.6 us
    ppermute x4, starting transfers between devices, local(): lax.ppermute(lax.dynamic_slice_in_dim(value, first, depth, 0), 'gz', ends...  9.03 us
    ppermute x14, waiting for transfers between devices, swap(): lax.ppermute(value, axis, [(i, i ^ step) for i in range(lax.axis_size(axi...  7.9 us
    all_to_all x1, starting transfers between devices, local(): lax.all_to_all(tilted, 'gz', split_axis=0, concat_axis=0, tiled=True)  3.32 us
    ppermute x4, waiting for transfers between devices, local(): lax.ppermute(lax.dynamic_slice_in_dim(value, first, depth, 0), 'gz', ends...  2.6 us
    pallas_call x1, Pallas kernels, shear_x(): pl.pallas_call(functools.partial(shear_x_kernel, classes), out_shape=[jax...  2.49 us
    pallas_call x2, Pallas kernels, shear_z(): pl.pallas_call(functools.partial(shear_z_kernel, plane_count, depth, chip...  1.05 us
    pallas_call x1, Pallas kernels, project(): pl.pallas_call(functools.partial(project_kernel, chips, tilts, shares), o...  1 us
  transfers between devices with their start and end apart: 19, of which 10 were waited for; matrix products, arithmetic and copies ran while one was open for 0% of the time, Pallas kernels for 8%

profile of v7, /device:TPU:0, one launch (start us, length us, event | category | flops | bytes accessed | tf_op | source)
XLA Modules:
  0.0 44.2 jit_solution(1940053672699434746)
XLA Ops:
  0.6 2.5 %shear_x.1 = (f32[40,16,128]{2,1,0:T(8,128)S(1)}, f32[40,16,128]{2,1,0:T(8,128)S(1)}) custom-call(s32[160]{0:T(256)} %shifts_hbm.1, f32[160]{0:T(256)} %fracs_hbm.1, f32[40,32,128]{2,1,0:T(8,128)} %bitcast.36), custom_call_target="tpu_custom_call" | custom-call | tf_op jit(solution)/shard_map/shear_x/pallas_call | solution.py:120
  3.2 0.7 %collective-permute-start.1 = (f32[36,16,128]{2,1,0:T(8,128)S(1)}, f32[36,16,128]{2,1,0:T(8,128)S(1)}, u32[]{:S(2)}, u32[]{:S(2)}) collective-permute-start(f32[36,16,128]{2,1,0:T(8,128)S(1)} %get-tuple-element.80), channel_id=1, source_target_pairs={{1,2},{2,1},{5,6},{6,5},{9,10},{10,9},{13,14},{14,13},{17,18},{18,... | collective-permute-start | bytes 884744 | tf_op jit(solution)/shard_map/ppermute | solution.py:576
  3.9 5.9 %collective-permute-start = (f32[36,16,128]{2,1,0:T(8,128)S(1)}, f32[36,16,128]{2,1,0:T(8,128)S(1)}, u32[]{:S(2)}, u32[]{:S(2)}) collective-permute-start(f32[36,16,128]{2,1,0:T(8,128)S(1)} %get-tuple-element.81), channel_id=1, source_target_pairs={{0,1},{1,0},{2,3},{3,2},{4,5},{5,4},{6,7},{7,6},{8,9},{9,8},{10,11... | collective-permute-start | bytes 884744 | tf_op jit(solution)/shard_map/ppermute | solution.py:576
  9.8 0.7 %collective-permute-start.7 = (f32[36,16,128]{2,1,0:T(8,128)S(1)}, f32[36,16,128]{2,1,0:T(8,128)S(1)}, u32[]{:S(2)}, u32[]{:S(2)}) collective-permute-start(f32[36,16,128]{2,1,0:T(8,128)S(1)} %get-tuple-element.78), channel_id=1, source_target_pairs={{1,2},{2,1},{5,6},{6,5},{9,10},{10,9},{13,14},{14,13},{17,18},{18,... | collective-permute-start | bytes 884744 | tf_op jit(solution)/shard_map/ppermute | solution.py:576
  10.5 1.8 %collective-permute-start.6 = (f32[36,16,128]{2,1,0:T(8,128)S(1)}, f32[36,16,128]{2,1,0:T(8,128)S(1)}, u32[]{:S(2)}, u32[]{:S(2)}) collective-permute-start(f32[36,16,128]{2,1,0:T(8,128)S(1)} %get-tuple-element.79), channel_id=1, source_target_pairs={{0,1},{1,0},{2,3},{3,2},{4,5},{5,4},{6,7},{7,6},{8,9},{9,8},{10,11... | collective-permute-start | bytes 884744 | tf_op jit(solution)/shard_map/ppermute | solution.py:576
  12.9 0.0 copy-start.1
  13.6 0.0 copy-start
  13.6 0.0 copy-start.2
  13.6 0.0 copy-done.1
  13.6 0.7 %copy-done = s32[512]{0:T(512)S(1)} copy-done((s32[512]{0:T(512)S(1)}, s32[512]{0:T(512)}, u32[]{:S(2)}) %copy-start) | copy-done | bytes 2072
  14.3 0.0 copy-done.2
  14.3 1.0 %weights.1 = (f32[40,112]{1,0:T(8,128)S(1)}, f32[64,128]{1,0:T(8,128)S(1)}, f32[40,40]{1,0:T(8,128)S(1)}) custom-call(s32[1]{0:T(128)S(6)} %copy.13.shift_ref, f32[1]{0:T(128)S(6)} %copy.14.frac_ref, s32[8]{0:T(128)S(1)} %copy-done.2, s32[1,512]{1,0:T(1,128)S(1)} %bitcast.33, f32[1,512]{1,0:T(1,128)S(1)} %bitcast.34), custom_call_target="tpu_custom_call" | custom-call | tf_op jit(solution)/shard_map/weights/pallas_call | solution.py:192
  15.2 0.0 collective-permute-done.1
  15.3 2.4 %collective-permute-done = f32[36,16,128]{2,1,0:T(8,128)S(1)} collective-permute-done((f32[36,16,128]{2,1,0:T(8,128)S(1)}, f32[36,16,128]{2,1,0:T(8,128)S(1)}, u32[]{:S(2)}, u32[]{:S(2)}) %collective-permute-start) | collective-permute-done | bytes 294944 | tf_op jit(solution)/shard_map/ppermute | solution.py:576
  17.7 0.5 %shear_z.2 = (f32[40,512]{1,0:T(8,128)S(1)}, f32[40,512]{1,0:T(8,128)S(1)}, f32[40,512]{1,0:T(8,128)S(1)}, f32[40,512]{1,0:T(8,128)S(1)}) custom-call(f32[40,112]{1,0:T(8,128)S(1)} %get-tuple-element.50.mixing_ref, f32[576,128]{1,0:T(8,128)S(1)} %bitcast.27, f32[640,128]{1,0:T(8,128)S(1)} %bitcast.20, f32[576,128]{1,0:T(8,128)S(1)} %bitcast.26), custom_call_target="tpu_custom_call" | custom-call | tf_op jit(solution)/shard_map/shear_z/pallas_call | solution.py:251
  18.2 2.5 %collective-permute-start.2 = (f32[40,512]{1,0:T(8,128)S(1)}, f32[40,512]{1,0:T(8,128)S(1)}, u32[]{:S(2)}, u32[]{:S(2)}) collective-permute-start(f32[40,512]{1,0:T(8,128)S(1)} %get-tuple-element.46), channel_id=1, source_target_pairs={{0,24},{4,28},{8,16},{12,20},{16,8},{20,12},{24,0},{28,4},{1,25},{... | collective-permute-start | bytes 245768 | tf_op jit(solution)/shard_map/ppermute | solution.py:541
  20.7 0.0 collective-permute-start.3
  20.7 0.5 %collective-permute-start.4 = (f32[40,512]{1,0:T(8,128)S(1)}, f32[40,512]{1,0:T(8,128)S(1)}, u32[]{:S(2)}, u32[]{:S(2)}) collective-permute-start(f32[40,512]{1,0:T(8,128)S(1)} %get-tuple-element.48), channel_id=1, source_target_pairs={{0,8},{4,12},{8,0},{12,4},{16,24},{20,28},{24,16},{28,20},{1,9},{5... | collective-permute-start | bytes 245768 | tf_op jit(solution)/shard_map/ppermute | solution.py:541
  21.2 0.0 collective-permute-done.7
  21.2 1.4 %collective-permute-start.5 = (f32[40,512]{1,0:T(8,128)S(1)}, f32[40,512]{1,0:T(8,128)S(1)}, u32[]{:S(2)}, u32[]{:S(2)}) collective-permute-start(f32[40,512]{1,0:T(8,128)S(1)} %get-tuple-element.49), channel_id=1, source_target_pairs={{0,12},{4,8},{8,4},{12,0},{16,28},{20,24},{24,20},{28,16},{1,13},{... | collective-permute-start | bytes 245768 | tf_op jit(solution)/shard_map/ppermute | solution.py:541
  22.6 0.2 collective-permute-done.6
  22.8 0.5 %shear_z.3 = (f32[40,512]{1,0:T(8,128)S(1)}, f32[40,512]{1,0:T(8,128)S(1)}, f32[40,512]{1,0:T(8,128)S(1)}, f32[40,512]{1,0:T(8,128)S(1)}) custom-call(f32[40,112]{1,0:T(8,128)S(1)} %get-tuple-element.50.mixing_ref, f32[576,128]{1,0:T(8,128)S(1)} %bitcast.25, f32[640,128]{1,0:T(8,128)S(1)} %bitcast.19, f32[576,128]{1,0:T(8,128)S(1)} %bitcast.24), custom_call_target="tpu_custom_call" | custom-call | tf_op jit(solution)/shard_map/shear_z/pallas_call | solution.py:251
  23.4 1.6 %collective-permute-start.8 = (f32[40,512]{1,0:T(8,128)S(1)}, f32[40,512]{1,0:T(8,128)S(1)}, u32[]{:S(2)}, u32[]{:S(2)}) collective-permute-start(f32[40,512]{1,0:T(8,128)S(1)} %get-tuple-element.56), channel_id=1, source_target_pairs={{0,16},{4,20},{8,24},{12,28},{16,0},{20,4},{24,8},{28,12},{1,17},{... | collective-permute-start | bytes 245768 | tf_op jit(solution)/shard_map/ppermute | solution.py:541
  24.9 0.0 collective-permute-done.2.refs_0_
  24.9 0.0 collective-permute-start.9
  24.9 1.4 %collective-permute-done.3.refs_1_ = f32[40,512]{1,0:T(8,128)S(1)} collective-permute-done((f32[40,512]{1,0:T(8,128)S(1)}, f32[40,512]{1,0:T(8,128)S(1)}, u32[]{:S(2)}, u32[]{:S(2)}) %collective-permute-start.3) | collective-permute-done | bytes 81952 | tf_op jit(solution)/shard_map/ppermute | solution.py:541
  26.3 0.0 collective-permute-start.10
  26.3 0.9 %collective-permute-done.4.refs_2_ = f32[40,512]{1,0:T(8,128)S(1)} collective-permute-done((f32[40,512]{1,0:T(8,128)S(1)}, f32[40,512]{1,0:T(8,128)S(1)}, u32[]{:S(2)}, u32[]{:S(2)}) %collective-permute-start.4) | collective-permute-done | bytes 81952 | tf_op jit(solution)/shard_map/ppermute | solution.py:541
  27.2 1.7 %collective-permute-done.5.refs_3_ = f32[40,512]{1,0:T(8,128)S(1)} collective-permute-done((f32[40,512]{1,0:T(8,128)S(1)}, f32[40,512]{1,0:T(8,128)S(1)}, u32[]{:S(2)}, u32[]{:S(2)}) %collective-permute-start.5) | collective-permute-done | bytes 81952 | tf_op jit(solution)/shard_map/ppermute | solution.py:541
  28.9 0.0 collective-permute-done.8.refs_4_
  28.9 0.8 %collective-permute-done.9.refs_5_ = f32[40,512]{1,0:T(8,128)S(1)} collective-permute-done((f32[40,512]{1,0:T(8,128)S(1)}, f32[40,512]{1,0:T(8,128)S(1)}, u32[]{:S(2)}, u32[]{:S(2)}) %collective-permute-start.9) | collective-permute-done | bytes 81952 | tf_op jit(solution)/shard_map/ppermute | solution.py:541
  29.7 0.0 collective-permute-done.10.refs_7_
  29.7 0.4 shear_y.1
  30.1 0.6 %collective-permute-start.13 = (f32[2,160,128]{2,1,0:T(8,128)S(1)}, f32[2,160,128]{2,1,0:T(8,128)S(1)}, u32[]{:S(2)}, u32[]{:S(2)}) collective-permute-start(f32[2,160,128]{2,1,0:T(8,128)S(1)} %get-tuple-element.65.refs_4_), channel_id=1, source_target_pairs={{0,16},{4,20},{8,24},{12,28},{16,0},{20,4},{24,8},{28,12},{1,17},{... | collective-permute-start | bytes 491528 | tf_op jit(solution)/shard_map/ppermute | solution.py:541
  30.7 2.4 %collective-permute-start.12 = (f32[2,160,128]{2,1,0:T(8,128)S(1)}, f32[2,160,128]{2,1,0:T(8,128)S(1)}, u32[]{:S(2)}, u32[]{:S(2)}) collective-permute-start(f32[2,160,128]{2,1,0:T(8,128)S(1)} %get-tuple-element.66.refs_5_), channel_id=1, source_target_pairs={{0,24},{4,28},{8,16},{12,20},{16,8},{20,12},{24,0},{28,4},{1,25},{... | collective-permute-start | bytes 491528 | tf_op jit(solution)/shard_map/ppermute | solution.py:541
  33.0 1.0 %project.1 = f32[4,2,8,512]{3,2,1,0:T(8,128)} custom-call(f32[40,40]{1,0:T(8,128)S(1)} %get-tuple-element.61.chosen_ref, f32[160,128]{1,0:T(8,128)S(1)} %get-tuple-element.62.refs_0_, f32[160,128]{1,0:T(8,128)S(1)} %get-tuple-element.60.refs_1_, f32[160,128]{1,0:T(8,128)S(1)} %get-tuple-element.63.refs_2_, f32[160,128]{1,0:T(8,128)S(1)} %get-tuple-element.64.refs_3_, ...), custom_call_target="tpu_custom_call" | custom-call | tf_op jit(solution)/shard_map/project/pallas_call | solution.py:380
  34.0 3.3 %all-to-all-start = ((f32[4,2,8,512]{3,2,1,0:T(8,128)}), f32[4,2,8,512]{3,2,1,0:T(8,128)S(1)}, u32[]{:S(2)}, u32[]{:S(2)}) async-start(f32[4,2,8,512]{3,2,1,0:T(8,128)} %project.1), calls=%async_computation | async-start | bytes 262144 | tf_op jit(solution)/shard_map/all_to_all | solution.py:590
  37.4 0.7 %collective-permute-start.16 = (f32[160,128]{1,0:T(8,128)S(1)}, f32[160,128]{1,0:T(8,128)S(1)}, u32[]{:S(2)}, u32[]{:S(2)}) collective-permute-start(f32[160,128]{1,0:T(8,128)S(1)} %get-tuple-element.63.refs_2_), channel_id=1, source_target_pairs={{0,8},{4,12},{8,0},{12,4},{16,24},{20,28},{24,16},{28,20},{1,9},{5... | collective-permute-start | bytes 245768 | tf_op jit(solution)/shard_map/ppermute | solution.py:541
  38.1 0.2 collective-permute-start.17
  38.3 1.6 %collective-permute-done.13.refs_1_ = f32[2,160,128]{2,1,0:T(8,128)S(1)} collective-permute-done((f32[2,160,128]{2,1,0:T(8,128)S(1)}, f32[2,160,128]{2,1,0:T(8,128)S(1)}, u32[]{:S(2)}, u32[]{:S(2)}) %collective-permute-start.13) | collective-permute-done | bytes 163872 | tf_op jit(solution)/shard_map/ppermute | solution.py:541
  39.9 0.0 collective-permute-done.12.refs_0_
  39.9 0.1 collective-permute-start.14
  40.0 0.5 %collective-permute-start.15 = (f32[160,128]{1,0:T(8,128)S(1)}, f32[160,128]{1,0:T(8,128)S(1)}, u32[]{:S(2)}, u32[]{:S(2)}) collective-permute-start(f32[160,128]{1,0:T(8,128)S(1)} %get-tuple-element.68), channel_id=1, source_target_pairs={{0,4},{4,0},{8,12},{12,8},{16,20},{20,16},{24,28},{28,24},{1,5},{5... | collective-permute-start | bytes 245768 | tf_op jit(solution)/shard_map/ppermute | solution.py:541
  40.5 0.1 collective-permute-start.11
  40.5 0.7 %place_first.1.refs_6_ = f32[40,8,4,128]{3,2,1,0:T(4,128)} custom-call(f32[40,4,128]{2,1,0:T(4,128)S(1)} %bitcast.23, f32[2,40,4,128]{3,2,1,0:T(4,128)S(1)} %bitcast.21, f32[2,40,4,128]{3,2,1,0:T(4,128)S(1)} %bitcast.22), custom_call_target="tpu_custom_call" | custom-call | tf_op jit(solution)/shard_map/place_first/pallas_call | solution.py:416
  41.3 1.4 %collective-permute-done.16 = f32[160,128]{1,0:T(8,128)S(1)} collective-permute-done((f32[160,128]{1,0:T(8,128)S(1)}, f32[160,128]{1,0:T(8,128)S(1)}, u32[]{:S(2)}, u32[]{:S(2)}) %collective-permute-start.16) | collective-permute-done | bytes 81952 | tf_op jit(solution)/shard_map/ppermute | solution.py:541
  42.7 0.2 collective-permute-done.17
  42.8 0.6 %all-to-all-done.refs_5_ = f32[4,2,8,512]{3,2,1,0:T(8,128)S(1)} async-done(((f32[4,2,8,512]{3,2,1,0:T(8,128)}), f32[4,2,8,512]{3,2,1,0:T(8,128)S(1)}, u32[]{:S(2)}, u32[]{:S(2)}) %all-to-all-start) | async-done | bytes 131104 | tf_op jit(solution)/shard_map/all_to_all | solution.py:590
  43.4 0.0 collective-permute-done.14
  43.4 0.0 collective-permute-done.15
  43.4 0.0 collective-permute-done.11
  43.4 0.8 %finish.1 = (f32[40,8,4,128]{3,2,1,0:T(4,128)}, f32[2,8,512]{2,1,0:T(8,128)}) custom-call(f32[40,4,128]{2,1,0:T(4,128)S(1)} %bitcast.32, f32[40,4,128]{2,1,0:T(4,128)S(1)} %bitcast.28, f32[40,4,128]{2,1,0:T(4,128)S(1)} %bitcast.29, f32[40,4,128]{2,1,0:T(4,128)S(1)} %bitcast.30, f32[40,4,128]{2,1,0:T(4,128)S(1)} %bitcast.31, ...), custom_call_target="tpu_custom_call", output_to_operand_aliasing={{0}: (6, {})} | custom-call | tf_op jit(solution)/shard_map/finish/pallas_call | solution.py:453
  (3 shorter events, 0.1 us)
Async XLA Ops:
  3.2 12.1 %collective-permute-start.1 = (f32[36,16,128]{2,1,0:T(8,128)S(1)}, f32[36,16,128]{2,1,0:T(8,128)S(1)}, u32[]{:S(2)}, u32[]{:S(2)}) collective-permute-start(f32[36,16,128]{2,1,0:T(8,128)S(1)} %get-tuple-element.80), channel_id=1, source_target_pairs={{1,2},{2,1},{5,6},{6,5},{9,10},{10,9},{13,14},{14,13},{17,18},{18,... | collective-permute-start | bytes 884744 | tf_op jit(solution)/shard_map/ppermute | solution.py:576
  3.9 13.8 %collective-permute-start = (f32[36,16,128]{2,1,0:T(8,128)S(1)}, f32[36,16,128]{2,1,0:T(8,128)S(1)}, u32[]{:S(2)}, u32[]{:S(2)}) collective-permute-start(f32[36,16,128]{2,1,0:T(8,128)S(1)} %get-tuple-element.81), channel_id=1, source_target_pairs={{0,1},{1,0},{2,3},{3,2},{4,5},{5,4},{6,7},{7,6},{8,9},{9,8},{10,11... | collective-permute-start | bytes 884744 | tf_op jit(solution)/shard_map/ppermute | solution.py:576
  9.8 11.4 %collective-permute-start.7 = (f32[36,16,128]{2,1,0:T(8,128)S(1)}, f32[36,16,128]{2,1,0:T(8,128)S(1)}, u32[]{:S(2)}, u32[]{:S(2)}) collective-permute-start(f32[36,16,128]{2,1,0:T(8,128)S(1)} %get-tuple-element.78), channel_id=1, source_target_pairs={{1,2},{2,1},{5,6},{6,5},{9,10},{10,9},{13,14},{14,13},{17,18},{18,... | collective-permute-start | bytes 884744 | tf_op jit(solution)/shard_map/ppermute | solution.py:576
  10.5 12.3 %collective-permute-start.6 = (f32[36,16,128]{2,1,0:T(8,128)S(1)}, f32[36,16,128]{2,1,0:T(8,128)S(1)}, u32[]{:S(2)}, u32[]{:S(2)}) collective-permute-start(f32[36,16,128]{2,1,0:T(8,128)S(1)} %get-tuple-element.79), channel_id=1, source_target_pairs={{0,1},{1,0},{2,3},{3,2},{4,5},{5,4},{6,7},{7,6},{8,9},{9,8},{10,11... | collective-permute-start | bytes 884744 | tf_op jit(solution)/shard_map/ppermute | solution.py:576
  12.9 0.7 %copy-start.1 = (f32[512]{0:T(512)S(1)}, f32[512]{0:T(512)}, u32[]{:S(2)}) copy-start(f32[512]{0:T(512)} %param.14) | copy-start | bytes 6148
  13.6 0.7 %copy-start = (s32[512]{0:T(512)S(1)}, s32[512]{0:T(512)}, u32[]{:S(2)}) copy-start(s32[512]{0:T(512)} %param.13) | copy-start | bytes 6148
  13.6 0.7 %copy-start.2 = (s32[8]{0:T(128)S(1)}, s32[8]{0:T(128)}, u32[]{:S(2)}) copy-start(s32[8]{0:T(128)} %slopes_ref.1) | copy-start | bytes 100
  18.2 6.8 %collective-permute-start.2 = (f32[40,512]{1,0:T(8,128)S(1)}, f32[40,512]{1,0:T(8,128)S(1)}, u32[]{:S(2)}, u32[]{:S(2)}) collective-permute-start(f32[40,512]{1,0:T(8,128)S(1)} %get-tuple-element.46), channel_id=1, source_target_pairs={{0,24},{4,28},{8,16},{12,20},{16,8},{20,12},{24,0},{28,4},{1,25},{... | collective-permute-start | bytes 245768 | tf_op jit(solution)/shard_map/ppermute | solution.py:541
  20.7 5.6 %collective-permute-start.3 = (f32[40,512]{1,0:T(8,128)S(1)}, f32[40,512]{1,0:T(8,128)S(1)}, u32[]{:S(2)}, u32[]{:S(2)}) collective-permute-start(f32[40,512]{1,0:T(8,128)S(1)} %get-tuple-element.47), channel_id=1, source_target_pairs={{0,28},{4,24},{8,20},{12,16},{16,12},{20,8},{24,4},{28,0},{1,29},{... | collective-permute-start | bytes 245768 | tf_op jit(solution)/shard_map/ppermute | solution.py:541
  20.7 6.5 %collective-permute-start.4 = (f32[40,512]{1,0:T(8,128)S(1)}, f32[40,512]{1,0:T(8,128)S(1)}, u32[]{:S(2)}, u32[]{:S(2)}) collective-permute-start(f32[40,512]{1,0:T(8,128)S(1)} %get-tuple-element.48), channel_id=1, source_target_pairs={{0,8},{4,12},{8,0},{12,4},{16,24},{20,28},{24,16},{28,20},{1,9},{5... | collective-permute-start | bytes 245768 | tf_op jit(solution)/shard_map/ppermute | solution.py:541
  21.2 7.6 %collective-permute-start.5 = (f32[40,512]{1,0:T(8,128)S(1)}, f32[40,512]{1,0:T(8,128)S(1)}, u32[]{:S(2)}, u32[]{:S(2)}) collective-permute-start(f32[40,512]{1,0:T(8,128)S(1)} %get-tuple-element.49), channel_id=1, source_target_pairs={{0,12},{4,8},{8,4},{12,0},{16,28},{20,24},{24,20},{28,16},{1,13},{... | collective-permute-start | bytes 245768 | tf_op jit(solution)/shard_map/ppermute | solution.py:541
  23.4 5.5 %collective-permute-start.8 = (f32[40,512]{1,0:T(8,128)S(1)}, f32[40,512]{1,0:T(8,128)S(1)}, u32[]{:S(2)}, u32[]{:S(2)}) collective-permute-start(f32[40,512]{1,0:T(8,128)S(1)} %get-tuple-element.56), channel_id=1, source_target_pairs={{0,16},{4,20},{8,24},{12,28},{16,0},{20,4},{24,8},{28,12},{1,17},{... | collective-permute-start | bytes 245768 | tf_op jit(solution)/shard_map/ppermute | solution.py:541
  24.9 4.7 %collective-permute-start.9 = (f32[40,512]{1,0:T(8,128)S(1)}, f32[40,512]{1,0:T(8,128)S(1)}, u32[]{:S(2)}, u32[]{:S(2)}) collective-permute-start(f32[40,512]{1,0:T(8,128)S(1)} %get-tuple-element.57), channel_id=1, source_target_pairs={{0,20},{4,16},{8,28},{12,24},{16,4},{20,0},{24,12},{28,8},{1,21},{... | collective-permute-start | bytes 245768 | tf_op jit(solution)/shard_map/ppermute | solution.py:541
  26.3 3.3 %collective-permute-start.10 = (f32[40,512]{1,0:T(8,128)S(1)}, f32[40,512]{1,0:T(8,128)S(1)}, u32[]{:S(2)}, u32[]{:S(2)}) collective-permute-start(f32[40,512]{1,0:T(8,128)S(1)} %get-tuple-element.59), channel_id=1, source_target_pairs={{0,4},{4,0},{8,12},{12,8},{16,20},{20,16},{24,28},{28,24},{1,5},{5... | collective-permute-start | bytes 245768 | tf_op jit(solution)/shard_map/ppermute | solution.py:541
  30.1 9.8 %collective-permute-start.13 = (f32[2,160,128]{2,1,0:T(8,128)S(1)}, f32[2,160,128]{2,1,0:T(8,128)S(1)}, u32[]{:S(2)}, u32[]{:S(2)}) collective-permute-start(f32[2,160,128]{2,1,0:T(8,128)S(1)} %get-tuple-element.65.refs_4_), channel_id=1, source_target_pairs={{0,16},{4,20},{8,24},{12,28},{16,0},{20,4},{24,8},{28,12},{1,17},{... | collective-permute-start | bytes 491528 | tf_op jit(solution)/shard_map/ppermute | solution.py:541
  30.7 9.2 %collective-permute-start.12 = (f32[2,160,128]{2,1,0:T(8,128)S(1)}, f32[2,160,128]{2,1,0:T(8,128)S(1)}, u32[]{:S(2)}, u32[]{:S(2)}) collective-permute-start(f32[2,160,128]{2,1,0:T(8,128)S(1)} %get-tuple-element.66.refs_5_), channel_id=1, source_target_pairs={{0,24},{4,28},{8,16},{12,20},{16,8},{20,12},{24,0},{28,4},{1,25},{... | collective-permute-start | bytes 491528 | tf_op jit(solution)/shard_map/ppermute | solution.py:541
  34.0 9.4 %all-to-all-start = ((f32[4,2,8,512]{3,2,1,0:T(8,128)}), f32[4,2,8,512]{3,2,1,0:T(8,128)S(1)}, u32[]{:S(2)}, u32[]{:S(2)}) async-start(f32[4,2,8,512]{3,2,1,0:T(8,128)} %project.1), calls=%async_computation | async-start | bytes 262144 | tf_op jit(solution)/shard_map/all_to_all | solution.py:590
  37.4 5.3 %collective-permute-start.16 = (f32[160,128]{1,0:T(8,128)S(1)}, f32[160,128]{1,0:T(8,128)S(1)}, u32[]{:S(2)}, u32[]{:S(2)}) collective-permute-start(f32[160,128]{1,0:T(8,128)S(1)} %get-tuple-element.63.refs_2_), channel_id=1, source_target_pairs={{0,8},{4,12},{8,0},{12,4},{16,24},{20,28},{24,16},{28,20},{1,9},{5... | collective-permute-start | bytes 245768 | tf_op jit(solution)/shard_map/ppermute | solution.py:541
  38.1 4.7 %collective-permute-start.17 = (f32[160,128]{1,0:T(8,128)S(1)}, f32[160,128]{1,0:T(8,128)S(1)}, u32[]{:S(2)}, u32[]{:S(2)}) collective-permute-start(f32[160,128]{1,0:T(8,128)S(1)} %get-tuple-element.64.refs_3_), channel_id=1, source_target_pairs={{0,12},{4,8},{8,4},{12,0},{16,28},{20,24},{24,20},{28,16},{1,13},{... | collective-permute-start | bytes 245768 | tf_op jit(solution)/shard_map/ppermute | solution.py:541
  39.9 3.5 %collective-permute-start.14 = (f32[160,128]{1,0:T(8,128)S(1)}, f32[160,128]{1,0:T(8,128)S(1)}, u32[]{:S(2)}, u32[]{:S(2)}) collective-permute-start(f32[160,128]{1,0:T(8,128)S(1)} %get-tuple-element.67), channel_id=1, source_target_pairs={{0,4},{4,0},{8,12},{12,8},{16,20},{20,16},{24,28},{28,24},{1,5},{5... | collective-permute-start | bytes 245768 | tf_op jit(solution)/shard_map/ppermute | solution.py:541
  40.0 3.4 %collective-permute-start.15 = (f32[160,128]{1,0:T(8,128)S(1)}, f32[160,128]{1,0:T(8,128)S(1)}, u32[]{:S(2)}, u32[]{:S(2)}) collective-permute-start(f32[160,128]{1,0:T(8,128)S(1)} %get-tuple-element.68), channel_id=1, source_target_pairs={{0,4},{4,0},{8,12},{12,8},{16,20},{20,16},{24,28},{28,24},{1,5},{5... | collective-permute-start | bytes 245768 | tf_op jit(solution)/shard_map/ppermute | solution.py:541
  40.5 2.9 %collective-permute-start.11 = (f32[160,128]{1,0:T(8,128)S(1)}, f32[160,128]{1,0:T(8,128)S(1)}, u32[]{:S(2)}, u32[]{:S(2)}) collective-permute-start(f32[160,128]{1,0:T(8,128)S(1)} %get-tuple-element.60.refs_1_), channel_id=1, source_target_pairs={{0,4},{4,0},{8,12},{12,8},{16,20},{20,16},{24,28},{28,24},{1,5},{5... | collective-permute-start | bytes 245768 | tf_op jit(solution)/shard_map/ppermute | solution.py:541

commit v8 on v7

--- a/solution.py
+++ b/solution.py
@@ -589,7 +589,7 @@
     tilted = project(chosen, (own, cross, *rotated), shares)
     tilted = [lax.all_to_all(tilted, "gz", split_axis=0, concat_axis=0, tiled=True)]
     late = [swap(value, "gy", 1) for value in collect(landed[::-1])][::-1]
-    tilted, late, direct = lax.optimization_barrier((tilted, late, direct))
+    tilted, direct, late = lax.optimization_barrier((tilted, direct, late))
     placed = place_first(own, landed, plane_count)
     rotated, projections = finish(placed, early, late, direct, tilted[0], plane_count)
     return (

time: 44.5 us -> 44.5 us (level)
  no operation moved by 1% of the time
where the time goes in v8:
time: 44.5 us; the launch traced here: 44.2 us
  starting transfers between devices  22.9 us (51%)
  waiting for transfers between devices  11.1 us (25%)
  Pallas kernels  7.42 us (17%)
  between operations  2.09 us (5%)
  local copies, waits for them, and re-layouts  0.75 us (2%)
    ppermute x14, starting transfers between devices, swap(): lax.ppermute(value, axis, [(i, i ^ step) for i in range(lax.axis_size(axi...  10.6 us
    ppermute x4, starting transfers between devices, local(): lax.ppermute(lax.dynamic_slice_in_dim(value, first, depth, 0), 'gz', ends...  9.03 us
    ppermute x14, waiting for transfers between devices, swap(): lax.ppermute(value, axis, [(i, i ^ step) for i in range(lax.axis_size(axi...  7.91 us
    all_to_all x1, starting transfers between devices, local(): lax.all_to_all(tilted, 'gz', split_axis=0, concat_axis=0, tiled=True)  3.32 us
    ppermute x4, waiting for transfers between devices, local(): lax.ppermute(lax.dynamic_slice_in_dim(value, first, depth, 0), 'gz', ends...  2.59 us
    pallas_call x1, Pallas kernels, shear_x(): pl.pallas_call(functools.partial(shear_x_kernel, classes), out_shape=[jax...  2.49 us
    pallas_call x2, Pallas kernels, shear_z(): pl.pallas_call(functools.partial(shear_z_kernel, plane_count, depth, chip...  1.05 us
    pallas_call x1, Pallas kernels, project(): pl.pallas_call(functools.partial(project_kernel, chips, tilts, shares), o...  1 us
  transfers between devices with their start and end apart: 19, of which 10 were waited for; matrix products, arithmetic and copies ran while one was open for 0% of the time, Pallas kernels for 8%

profile of v8, /device:TPU:0, one launch (start us, length us, event | category | flops | bytes accessed | tf_op | source)
XLA Modules:
  0.0 44.2 jit_solution(1940053672699434746)
XLA Ops:
  0.6 2.5 %shear_x.1 = (f32[40,16,128]{2,1,0:T(8,128)S(1)}, f32[40,16,128]{2,1,0:T(8,128)S(1)}) custom-call(s32[160]{0:T(256)} %shifts_hbm.1, f32[160]{0:T(256)} %fracs_hbm.1, f32[40,32,128]{2,1,0:T(8,128)} %bitcast.36), custom_call_target="tpu_custom_call" | custom-call | tf_op jit(solution)/shard_map/shear_x/pallas_call | solution.py:120
  3.2 0.7 %collective-permute-start.1 = (f32[36,16,128]{2,1,0:T(8,128)S(1)}, f32[36,16,128]{2,1,0:T(8,128)S(1)}, u32[]{:S(2)}, u32[]{:S(2)}) collective-permute-start(f32[36,16,128]{2,1,0:T(8,128)S(1)} %get-tuple-element.80), channel_id=1, source_target_pairs={{1,2},{2,1},{5,6},{6,5},{9,10},{10,9},{13,14},{14,13},{17,18},{18,... | collective-permute-start | bytes 884744 | tf_op jit(solution)/shard_map/ppermute | solution.py:576
  3.9 5.9 %collective-permute-start = (f32[36,16,128]{2,1,0:T(8,128)S(1)}, f32[36,16,128]{2,1,0:T(8,128)S(1)}, u32[]{:S(2)}, u32[]{:S(2)}) collective-permute-start(f32[36,16,128]{2,1,0:T(8,128)S(1)} %get-tuple-element.81), channel_id=1, source_target_pairs={{0,1},{1,0},{2,3},{3,2},{4,5},{5,4},{6,7},{7,6},{8,9},{9,8},{10,11... | collective-permute-start | bytes 884744 | tf_op jit(solution)/shard_map/ppermute | solution.py:576
  9.8 0.7 %collective-permute-start.7 = (f32[36,16,128]{2,1,0:T(8,128)S(1)}, f32[36,16,128]{2,1,0:T(8,128)S(1)}, u32[]{:S(2)}, u32[]{:S(2)}) collective-permute-start(f32[36,16,128]{2,1,0:T(8,128)S(1)} %get-tuple-element.78), channel_id=1, source_target_pairs={{1,2},{2,1},{5,6},{6,5},{9,10},{10,9},{13,14},{14,13},{17,18},{18,... | collective-permute-start | bytes 884744 | tf_op jit(solution)/shard_map/ppermute | solution.py:576
  10.5 1.8 %collective-permute-start.6 = (f32[36,16,128]{2,1,0:T(8,128)S(1)}, f32[36,16,128]{2,1,0:T(8,128)S(1)}, u32[]{:S(2)}, u32[]{:S(2)}) collective-permute-start(f32[36,16,128]{2,1,0:T(8,128)S(1)} %get-tuple-element.79), channel_id=1, source_target_pairs={{0,1},{1,0},{2,3},{3,2},{4,5},{5,4},{6,7},{7,6},{8,9},{9,8},{10,11... | collective-permute-start | bytes 884744 | tf_op jit(solution)/shard_map/ppermute | solution.py:576
  12.9 0.0 copy-start.1
  13.6 0.0 copy-start
  13.6 0.0 copy-start.2
  13.6 0.0 copy-done.1
  13.6 0.7 %copy-done = s32[512]{0:T(512)S(1)} copy-done((s32[512]{0:T(512)S(1)}, s32[512]{0:T(512)}, u32[]{:S(2)}) %copy-start) | copy-done | bytes 2072
  14.3 0.0 copy-done.2
  14.3 1.0 %weights.1 = (f32[40,112]{1,0:T(8,128)S(1)}, f32[64,128]{1,0:T(8,128)S(1)}, f32[40,40]{1,0:T(8,128)S(1)}) custom-call(s32[1]{0:T(128)S(6)} %copy.13.shift_ref, f32[1]{0:T(128)S(6)} %copy.14.frac_ref, s32[8]{0:T(128)S(1)} %copy-done.2, s32[1,512]{1,0:T(1,128)S(1)} %bitcast.33, f32[1,512]{1,0:T(1,128)S(1)} %bitcast.34), custom_call_target="tpu_custom_call" | custom-call | tf_op jit(solution)/shard_map/weights/pallas_call | solution.py:192
  15.2 0.0 collective-permute-done.1
  15.3 2.4 %collective-permute-done = f32[36,16,128]{2,1,0:T(8,128)S(1)} collective-permute-done((f32[36,16,128]{2,1,0:T(8,128)S(1)}, f32[36,16,128]{2,1,0:T(8,128)S(1)}, u32[]{:S(2)}, u32[]{:S(2)}) %collective-permute-start) | collective-permute-done | bytes 294944 | tf_op jit(solution)/shard_map/ppermute | solution.py:576
  17.7 0.5 %shear_z.2 = (f32[40,512]{1,0:T(8,128)S(1)}, f32[40,512]{1,0:T(8,128)S(1)}, f32[40,512]{1,0:T(8,128)S(1)}, f32[40,512]{1,0:T(8,128)S(1)}) custom-call(f32[40,112]{1,0:T(8,128)S(1)} %get-tuple-element.50.mixing_ref, f32[576,128]{1,0:T(8,128)S(1)} %bitcast.27, f32[640,128]{1,0:T(8,128)S(1)} %bitcast.20, f32[576,128]{1,0:T(8,128)S(1)} %bitcast.26), custom_call_target="tpu_custom_call" | custom-call | tf_op jit(solution)/shard_map/shear_z/pallas_call | solution.py:251
  18.2 2.5 %collective-permute-start.2 = (f32[40,512]{1,0:T(8,128)S(1)}, f32[40,512]{1,0:T(8,128)S(1)}, u32[]{:S(2)}, u32[]{:S(2)}) collective-permute-start(f32[40,512]{1,0:T(8,128)S(1)} %get-tuple-element.46), channel_id=1, source_target_pairs={{0,24},{4,28},{8,16},{12,20},{16,8},{20,12},{24,0},{28,4},{1,25},{... | collective-permute-start | bytes 245768 | tf_op jit(solution)/shard_map/ppermute | solution.py:541
  20.7 0.0 collective-permute-start.3
  20.7 0.5 %collective-permute-start.4 = (f32[40,512]{1,0:T(8,128)S(1)}, f32[40,512]{1,0:T(8,128)S(1)}, u32[]{:S(2)}, u32[]{:S(2)}) collective-permute-start(f32[40,512]{1,0:T(8,128)S(1)} %get-tuple-element.48), channel_id=1, source_target_pairs={{0,8},{4,12},{8,0},{12,4},{16,24},{20,28},{24,16},{28,20},{1,9},{5... | collective-permute-start | bytes 245768 | tf_op jit(solution)/shard_map/ppermute | solution.py:541
  21.2 0.0 collective-permute-done.7
  21.2 1.4 %collective-permute-start.5 = (f32[40,512]{1,0:T(8,128)S(1)}, f32[40,512]{1,0:T(8,128)S(1)}, u32[]{:S(2)}, u32[]{:S(2)}) collective-permute-start(f32[40,512]{1,0:T(8,128)S(1)} %get-tuple-element.49), channel_id=1, source_target_pairs={{0,12},{4,8},{8,4},{12,0},{16,28},{20,24},{24,20},{28,16},{1,13},{... | collective-permute-start | bytes 245768 | tf_op jit(solution)/shard_map/ppermute | solution.py:541
  22.6 0.2 collective-permute-done.6
  22.8 0.5 %shear_z.3 = (f32[40,512]{1,0:T(8,128)S(1)}, f32[40,512]{1,0:T(8,128)S(1)}, f32[40,512]{1,0:T(8,128)S(1)}, f32[40,512]{1,0:T(8,128)S(1)}) custom-call(f32[40,112]{1,0:T(8,128)S(1)} %get-tuple-element.50.mixing_ref, f32[576,128]{1,0:T(8,128)S(1)} %bitcast.25, f32[640,128]{1,0:T(8,128)S(1)} %bitcast.19, f32[576,128]{1,0:T(8,128)S(1)} %bitcast.24), custom_call_target="tpu_custom_call" | custom-call | tf_op jit(solution)/shard_map/shear_z/pallas_call | solution.py:251
  23.4 1.6 %collective-permute-start.8 = (f32[40,512]{1,0:T(8,128)S(1)}, f32[40,512]{1,0:T(8,128)S(1)}, u32[]{:S(2)}, u32[]{:S(2)}) collective-permute-start(f32[40,512]{1,0:T(8,128)S(1)} %get-tuple-element.56), channel_id=1, source_target_pairs={{0,16},{4,20},{8,24},{12,28},{16,0},{20,4},{24,8},{28,12},{1,17},{... | collective-permute-start | bytes 245768 | tf_op jit(solution)/shard_map/ppermute | solution.py:541
  24.9 0.0 collective-permute-done.2.refs_0_
  24.9 0.0 collective-permute-start.9
  24.9 1.3 %collective-permute-done.3.refs_1_ = f32[40,512]{1,0:T(8,128)S(1)} collective-permute-done((f32[40,512]{1,0:T(8,128)S(1)}, f32[40,512]{1,0:T(8,128)S(1)}, u32[]{:S(2)}, u32[]{:S(2)}) %collective-permute-start.3) | collective-permute-done | bytes 81952 | tf_op jit(solution)/shard_map/ppermute | solution.py:541
  26.2 0.0 collective-permute-start.10
  26.2 1.0 %collective-permute-done.4.refs_2_ = f32[40,512]{1,0:T(8,128)S(1)} collective-permute-done((f32[40,512]{1,0:T(8,128)S(1)}, f32[40,512]{1,0:T(8,128)S(1)}, u32[]{:S(2)}, u32[]{:S(2)}) %collective-permute-start.4) | collective-permute-done | bytes 81952 | tf_op jit(solution)/shard_map/ppermute | solution.py:541
  27.2 1.7 %collective-permute-done.5.refs_3_ = f32[40,512]{1,0:T(8,128)S(1)} collective-permute-done((f32[40,512]{1,0:T(8,128)S(1)}, f32[40,512]{1,0:T(8,128)S(1)}, u32[]{:S(2)}, u32[]{:S(2)}) %collective-permute-start.5) | collective-permute-done | bytes 81952 | tf_op jit(solution)/shard_map/ppermute | solution.py:541
  28.9 0.0 collective-permute-done.8.refs_4_
  28.9 0.8 %collective-permute-done.9.refs_5_ = f32[40,512]{1,0:T(8,128)S(1)} collective-permute-done((f32[40,512]{1,0:T(8,128)S(1)}, f32[40,512]{1,0:T(8,128)S(1)}, u32[]{:S(2)}, u32[]{:S(2)}) %collective-permute-start.9) | collective-permute-done | bytes 81952 | tf_op jit(solution)/shard_map/ppermute | solution.py:541
  29.7 0.0 collective-permute-done.10.refs_7_
  29.7 0.4 shear_y.1
  30.1 0.6 %collective-permute-start.15 = (f32[2,160,128]{2,1,0:T(8,128)S(1)}, f32[2,160,128]{2,1,0:T(8,128)S(1)}, u32[]{:S(2)}, u32[]{:S(2)}) collective-permute-start(f32[2,160,128]{2,1,0:T(8,128)S(1)} %get-tuple-element.65.refs_4_), channel_id=1, source_target_pairs={{0,16},{4,20},{8,24},{12,28},{16,0},{20,4},{24,8},{28,12},{1,17},{... | collective-permute-start | bytes 491528 | tf_op jit(solution)/shard_map/ppermute | solution.py:541
  30.7 2.4 %collective-permute-start.14 = (f32[2,160,128]{2,1,0:T(8,128)S(1)}, f32[2,160,128]{2,1,0:T(8,128)S(1)}, u32[]{:S(2)}, u32[]{:S(2)}) collective-permute-start(f32[2,160,128]{2,1,0:T(8,128)S(1)} %get-tuple-element.66.refs_5_), channel_id=1, source_target_pairs={{0,24},{4,28},{8,16},{12,20},{16,8},{20,12},{24,0},{28,4},{1,25},{... | collective-permute-start | bytes 491528 | tf_op jit(solution)/shard_map/ppermute | solution.py:541
  33.0 1.0 %project.1 = f32[4,2,8,512]{3,2,1,0:T(8,128)} custom-call(f32[40,40]{1,0:T(8,128)S(1)} %get-tuple-element.61.chosen_ref, f32[160,128]{1,0:T(8,128)S(1)} %get-tuple-element.62.refs_0_, f32[160,128]{1,0:T(8,128)S(1)} %get-tuple-element.60.refs_1_, f32[160,128]{1,0:T(8,128)S(1)} %get-tuple-element.63.refs_2_, f32[160,128]{1,0:T(8,128)S(1)} %get-tuple-element.64.refs_3_, ...), custom_call_target="tpu_custom_call" | custom-call | tf_op jit(solution)/shard_map/project/pallas_call | solution.py:380
  34.0 3.3 %all-to-all-start = ((f32[4,2,8,512]{3,2,1,0:T(8,128)}), f32[4,2,8,512]{3,2,1,0:T(8,128)S(1)}, u32[]{:S(2)}, u32[]{:S(2)}) async-start(f32[4,2,8,512]{3,2,1,0:T(8,128)} %project.1), calls=%async_computation | async-start | bytes 262144 | tf_op jit(solution)/shard_map/all_to_all | solution.py:590
  37.4 0.7 %collective-permute-start.12 = (f32[160,128]{1,0:T(8,128)S(1)}, f32[160,128]{1,0:T(8,128)S(1)}, u32[]{:S(2)}, u32[]{:S(2)}) collective-permute-start(f32[160,128]{1,0:T(8,128)S(1)} %get-tuple-element.63.refs_2_), channel_id=1, source_target_pairs={{0,8},{4,12},{8,0},{12,4},{16,24},{20,28},{24,16},{28,20},{1,9},{5... | collective-permute-start | bytes 245768 | tf_op jit(solution)/shard_map/ppermute | solution.py:541
  38.1 0.2 collective-permute-start.13
  38.3 1.6 %collective-permute-done.15.refs_1_ = f32[2,160,128]{2,1,0:T(8,128)S(1)} collective-permute-done((f32[2,160,128]{2,1,0:T(8,128)S(1)}, f32[2,160,128]{2,1,0:T(8,128)S(1)}, u32[]{:S(2)}, u32[]{:S(2)}) %collective-permute-start.15) | collective-permute-done | bytes 163872 | tf_op jit(solution)/shard_map/ppermute | solution.py:541
  39.9 0.0 collective-permute-done.14.refs_0_
  39.9 0.1 collective-permute-start.16
  40.0 0.5 %collective-permute-start.17 = (f32[160,128]{1,0:T(8,128)S(1)}, f32[160,128]{1,0:T(8,128)S(1)}, u32[]{:S(2)}, u32[]{:S(2)}) collective-permute-start(f32[160,128]{1,0:T(8,128)S(1)} %get-tuple-element.68), channel_id=1, source_target_pairs={{0,4},{4,0},{8,12},{12,8},{16,20},{20,16},{24,28},{28,24},{1,5},{5... | collective-permute-start | bytes 245768 | tf_op jit(solution)/shard_map/ppermute | solution.py:541
  40.5 0.1 collective-permute-start.11
  40.5 0.7 %place_first.1.refs_6_ = f32[40,8,4,128]{3,2,1,0:T(4,128)} custom-call(f32[40,4,128]{2,1,0:T(4,128)S(1)} %bitcast.23, f32[2,40,4,128]{3,2,1,0:T(4,128)S(1)} %bitcast.21, f32[2,40,4,128]{3,2,1,0:T(4,128)S(1)} %bitcast.22), custom_call_target="tpu_custom_call" | custom-call | tf_op jit(solution)/shard_map/place_first/pallas_call | solution.py:416
  41.3 1.4 %collective-permute-done.12 = f32[160,128]{1,0:T(8,128)S(1)} collective-permute-done((f32[160,128]{1,0:T(8,128)S(1)}, f32[160,128]{1,0:T(8,128)S(1)}, u32[]{:S(2)}, u32[]{:S(2)}) %collective-permute-start.12) | collective-permute-done | bytes 81952 | tf_op jit(solution)/shard_map/ppermute | solution.py:541
  42.6 0.2 collective-permute-done.13
  42.8 0.6 %all-to-all-done.refs_5_ = f32[4,2,8,512]{3,2,1,0:T(8,128)S(1)} async-done(((f32[4,2,8,512]{3,2,1,0:T(8,128)}), f32[4,2,8,512]{3,2,1,0:T(8,128)S(1)}, u32[]{:S(2)}, u32[]{:S(2)}) %all-to-all-start) | async-done | bytes 131104 | tf_op jit(solution)/shard_map/all_to_all | solution.py:590
  43.4 0.0 collective-permute-done.16
  43.4 0.0 collective-permute-done.17
  43.4 0.0 collective-permute-done.11
  43.4 0.8 %finish.1 = (f32[40,8,4,128]{3,2,1,0:T(4,128)}, f32[2,8,512]{2,1,0:T(8,128)}) custom-call(f32[40,4,128]{2,1,0:T(4,128)S(1)} %bitcast.32, f32[40,4,128]{2,1,0:T(4,128)S(1)} %bitcast.28, f32[40,4,128]{2,1,0:T(4,128)S(1)} %bitcast.29, f32[40,4,128]{2,1,0:T(4,128)S(1)} %bitcast.30, f32[40,4,128]{2,1,0:T(4,128)S(1)} %bitcast.31, ...), custom_call_target="tpu_custom_call", output_to_operand_aliasing={{0}: (6, {})} | custom-call | tf_op jit(solution)/shard_map/finish/pallas_call | solution.py:453
  (3 shorter events, 0.1 us)
Async XLA Ops:
  3.2 12.1 %collective-permute-start.1 = (f32[36,16,128]{2,1,0:T(8,128)S(1)}, f32[36,16,128]{2,1,0:T(8,128)S(1)}, u32[]{:S(2)}, u32[]{:S(2)}) collective-permute-start(f32[36,16,128]{2,1,0:T(8,128)S(1)} %get-tuple-element.80), channel_id=1, source_target_pairs={{1,2},{2,1},{5,6},{6,5},{9,10},{10,9},{13,14},{14,13},{17,18},{18,... | collective-permute-start | bytes 884744 | tf_op jit(solution)/shard_map/ppermute | solution.py:576
  3.9 13.8 %collective-permute-start = (f32[36,16,128]{2,1,0:T(8,128)S(1)}, f32[36,16,128]{2,1,0:T(8,128)S(1)}, u32[]{:S(2)}, u32[]{:S(2)}) collective-permute-start(f32[36,16,128]{2,1,0:T(8,128)S(1)} %get-tuple-element.81), channel_id=1, source_target_pairs={{0,1},{1,0},{2,3},{3,2},{4,5},{5,4},{6,7},{7,6},{8,9},{9,8},{10,11... | collective-permute-start | bytes 884744 | tf_op jit(solution)/shard_map/ppermute | solution.py:576
  9.8 11.4 %collective-permute-start.7 = (f32[36,16,128]{2,1,0:T(8,128)S(1)}, f32[36,16,128]{2,1,0:T(8,128)S(1)}, u32[]{:S(2)}, u32[]{:S(2)}) collective-permute-start(f32[36,16,128]{2,1,0:T(8,128)S(1)} %get-tuple-element.78), channel_id=1, source_target_pairs={{1,2},{2,1},{5,6},{6,5},{9,10},{10,9},{13,14},{14,13},{17,18},{18,... | collective-permute-start | bytes 884744 | tf_op jit(solution)/shard_map/ppermute | solution.py:576
  10.5 12.3 %collective-permute-start.6 = (f32[36,16,128]{2,1,0:T(8,128)S(1)}, f32[36,16,128]{2,1,0:T(8,128)S(1)}, u32[]{:S(2)}, u32[]{:S(2)}) collective-permute-start(f32[36,16,128]{2,1,0:T(8,128)S(1)} %get-tuple-element.79), channel_id=1, source_target_pairs={{0,1},{1,0},{2,3},{3,2},{4,5},{5,4},{6,7},{7,6},{8,9},{9,8},{10,11... | collective-permute-start | bytes 884744 | tf_op jit(solution)/shard_map/ppermute | solution.py:576
  12.9 0.7 %copy-start.1 = (f32[512]{0:T(512)S(1)}, f32[512]{0:T(512)}, u32[]{:S(2)}) copy-start(f32[512]{0:T(512)} %param.14) | copy-start | bytes 6148
  13.6 0.7 %copy-start = (s32[512]{0:T(512)S(1)}, s32[512]{0:T(512)}, u32[]{:S(2)}) copy-start(s32[512]{0:T(512)} %param.13) | copy-start | bytes 6148
  13.6 0.7 %copy-start.2 = (s32[8]{0:T(128)S(1)}, s32[8]{0:T(128)}, u32[]{:S(2)}) copy-start(s32[8]{0:T(128)} %slopes_ref.1) | copy-start | bytes 100
  18.2 6.8 %collective-permute-start.2 = (f32[40,512]{1,0:T(8,128)S(1)}, f32[40,512]{1,0:T(8,128)S(1)}, u32[]{:S(2)}, u32[]{:S(2)}) collective-permute-start(f32[40,512]{1,0:T(8,128)S(1)} %get-tuple-element.46), channel_id=1, source_target_pairs={{0,24},{4,28},{8,16},{12,20},{16,8},{20,12},{24,0},{28,4},{1,25},{... | collective-permute-start | bytes 245768 | tf_op jit(solution)/shard_map/ppermute | solution.py:541
  20.7 5.5 %collective-permute-start.3 = (f32[40,512]{1,0:T(8,128)S(1)}, f32[40,512]{1,0:T(8,128)S(1)}, u32[]{:S(2)}, u32[]{:S(2)}) collective-permute-start(f32[40,512]{1,0:T(8,128)S(1)} %get-tuple-element.47), channel_id=1, source_target_pairs={{0,28},{4,24},{8,20},{12,16},{16,12},{20,8},{24,4},{28,0},{1,29},{... | collective-permute-start | bytes 245768 | tf_op jit(solution)/shard_map/ppermute | solution.py:541
  20.7 6.5 %collective-permute-start.4 = (f32[40,512]{1,0:T(8,128)S(1)}, f32[40,512]{1,0:T(8,128)S(1)}, u32[]{:S(2)}, u32[]{:S(2)}) collective-permute-start(f32[40,512]{1,0:T(8,128)S(1)} %get-tuple-element.48), channel_id=1, source_target_pairs={{0,8},{4,12},{8,0},{12,4},{16,24},{20,28},{24,16},{28,20},{1,9},{5... | collective-permute-start | bytes 245768 | tf_op jit(solution)/shard_map/ppermute | solution.py:541
  21.2 7.6 %collective-permute-start.5 = (f32[40,512]{1,0:T(8,128)S(1)}, f32[40,512]{1,0:T(8,128)S(1)}, u32[]{:S(2)}, u32[]{:S(2)}) collective-permute-start(f32[40,512]{1,0:T(8,128)S(1)} %get-tuple-element.49), channel_id=1, source_target_pairs={{0,12},{4,8},{8,4},{12,0},{16,28},{20,24},{24,20},{28,16},{1,13},{... | collective-permute-start | bytes 245768 | tf_op jit(solution)/shard_map/ppermute | solution.py:541
  23.4 5.5 %collective-permute-start.8 = (f32[40,512]{1,0:T(8,128)S(1)}, f32[40,512]{1,0:T(8,128)S(1)}, u32[]{:S(2)}, u32[]{:S(2)}) collective-permute-start(f32[40,512]{1,0:T(8,128)S(1)} %get-tuple-element.56), channel_id=1, source_target_pairs={{0,16},{4,20},{8,24},{12,28},{16,0},{20,4},{24,8},{28,12},{1,17},{... | collective-permute-start | bytes 245768 | tf_op jit(solution)/shard_map/ppermute | solution.py:541
  24.9 4.7 %collective-permute-start.9 = (f32[40,512]{1,0:T(8,128)S(1)}, f32[40,512]{1,0:T(8,128)S(1)}, u32[]{:S(2)}, u32[]{:S(2)}) collective-permute-start(f32[40,512]{1,0:T(8,128)S(1)} %get-tuple-element.57), channel_id=1, source_target_pairs={{0,20},{4,16},{8,28},{12,24},{16,4},{20,0},{24,12},{28,8},{1,21},{... | collective-permute-start | bytes 245768 | tf_op jit(solution)/shard_map/ppermute | solution.py:541
  26.2 3.4 %collective-permute-start.10 = (f32[40,512]{1,0:T(8,128)S(1)}, f32[40,512]{1,0:T(8,128)S(1)}, u32[]{:S(2)}, u32[]{:S(2)}) collective-permute-start(f32[40,512]{1,0:T(8,128)S(1)} %get-tuple-element.59), channel_id=1, source_target_pairs={{0,4},{4,0},{8,12},{12,8},{16,20},{20,16},{24,28},{28,24},{1,5},{5... | collective-permute-start | bytes 245768 | tf_op jit(solution)/shard_map/ppermute | solution.py:541
  30.1 9.8 %collective-permute-start.15 = (f32[2,160,128]{2,1,0:T(8,128)S(1)}, f32[2,160,128]{2,1,0:T(8,128)S(1)}, u32[]{:S(2)}, u32[]{:S(2)}) collective-permute-start(f32[2,160,128]{2,1,0:T(8,128)S(1)} %get-tuple-element.65.refs_4_), channel_id=1, source_target_pairs={{0,16},{4,20},{8,24},{12,28},{16,0},{20,4},{24,8},{28,12},{1,17},{... | collective-permute-start | bytes 491528 | tf_op jit(solution)/shard_map/ppermute | solution.py:541
  30.7 9.2 %collective-permute-start.14 = (f32[2,160,128]{2,1,0:T(8,128)S(1)}, f32[2,160,128]{2,1,0:T(8,128)S(1)}, u32[]{:S(2)}, u32[]{:S(2)}) collective-permute-start(f32[2,160,128]{2,1,0:T(8,128)S(1)} %get-tuple-element.66.refs_5_), channel_id=1, source_target_pairs={{0,24},{4,28},{8,16},{12,20},{16,8},{20,12},{24,0},{28,4},{1,25},{... | collective-permute-start | bytes 491528 | tf_op jit(solution)/shard_map/ppermute | solution.py:541
  34.0 9.4 %all-to-all-start = ((f32[4,2,8,512]{3,2,1,0:T(8,128)}), f32[4,2,8,512]{3,2,1,0:T(8,128)S(1)}, u32[]{:S(2)}, u32[]{:S(2)}) async-start(f32[4,2,8,512]{3,2,1,0:T(8,128)} %project.1), calls=%async_computation | async-start | bytes 262144 | tf_op jit(solution)/shard_map/all_to_all | solution.py:590
  37.4 5.3 %collective-permute-start.12 = (f32[160,128]{1,0:T(8,128)S(1)}, f32[160,128]{1,0:T(8,128)S(1)}, u32[]{:S(2)}, u32[]{:S(2)}) collective-permute-start(f32[160,128]{1,0:T(8,128)S(1)} %get-tuple-element.63.refs_2_), channel_id=1, source_target_pairs={{0,8},{4,12},{8,0},{12,4},{16,24},{20,28},{24,16},{28,20},{1,9},{5... | collective-permute-start | bytes 245768 | tf_op jit(solution)/shard_map/ppermute | solution.py:541
  38.1 4.7 %collective-permute-start.13 = (f32[160,128]{1,0:T(8,128)S(1)}, f32[160,128]{1,0:T(8,128)S(1)}, u32[]{:S(2)}, u32[]{:S(2)}) collective-permute-start(f32[160,128]{1,0:T(8,128)S(1)} %get-tuple-element.64.refs_3_), channel_id=1, source_target_pairs={{0,12},{4,8},{8,4},{12,0},{16,28},{20,24},{24,20},{28,16},{1,13},{... | collective-permute-start | bytes 245768 | tf_op jit(solution)/shard_map/ppermute | solution.py:541
  39.9 3.5 %collective-permute-start.16 = (f32[160,128]{1,0:T(8,128)S(1)}, f32[160,128]{1,0:T(8,128)S(1)}, u32[]{:S(2)}, u32[]{:S(2)}) collective-permute-start(f32[160,128]{1,0:T(8,128)S(1)} %get-tuple-element.67), channel_id=1, source_target_pairs={{0,4},{4,0},{8,12},{12,8},{16,20},{20,16},{24,28},{28,24},{1,5},{5... | collective-permute-start | bytes 245768 | tf_op jit(solution)/shard_map/ppermute | solution.py:541
  40.0 3.4 %collective-permute-start.17 = (f32[160,128]{1,0:T(8,128)S(1)}, f32[160,128]{1,0:T(8,128)S(1)}, u32[]{:S(2)}, u32[]{:S(2)}) collective-permute-start(f32[160,128]{1,0:T(8,128)S(1)} %get-tuple-element.68), channel_id=1, source_target_pairs={{0,4},{4,0},{8,12},{12,8},{16,20},{20,16},{24,28},{28,24},{1,5},{5... | collective-permute-start | bytes 245768 | tf_op jit(solution)/shard_map/ppermute | solution.py:541
  40.5 2.9 %collective-permute-start.11 = (f32[160,128]{1,0:T(8,128)S(1)}, f32[160,128]{1,0:T(8,128)S(1)}, u32[]{:S(2)}, u32[]{:S(2)}) collective-permute-start(f32[160,128]{1,0:T(8,128)S(1)} %get-tuple-element.60.refs_1_), channel_id=1, source_target_pairs={{0,4},{4,0},{8,12},{12,8},{16,20},{20,16},{24,28},{28,24},{1,5},{5... | collective-permute-start | bytes 245768 | tf_op jit(solution)/shard_map/ppermute | solution.py:541
